TPU v7x, 32 devices: a whole 2x2x4 slice. The times are simulated.
32 devices in a mesh: head: 4 (over y, x), ctx: 8 (over z, core).
Axes of the slice: x: 2, y: 2, z: 4, core: 2. Of those that a mesh axis runs over, the one named last changes fastest.
Arguments:
- query: bfloat16 [8, 512, 4096], P('ctx', 'head'), may hold values from -6 to 6
- keys: bfloat16 [8, 512, 4096], P('ctx', 'head'), may hold values from -6 to 6
- values: bfloat16 [8, 512, 4096], P('ctx', 'head'), may hold values from -6 to 6
- grad_out: bfloat16 [8, 512, 4096], P('ctx', 'head'), may hold values from -6 to 6
Outputs:
- grad_q: bfloat16 [8, 512, 4096], P('ctx', None, 'head')
- grad_k: bfloat16 [8, 512, 4096], P('ctx', None, 'head')
- grad_v: bfloat16 [8, 512, 4096], P('ctx', None, 'head')
All inputs are finite; a program needn't handle non-finite values.
Results may differ from a plain program's by a relative error of at most 0.0049.
Values may be sent and summed in bfloat16 or wider, within the bound.
No kernel may reach another device: no remote copies, remote signals or barrier semaphores. Data moves between devices by JAX's collectives and lax.ppermute only.
A program may use at most 192 MiB of HBM per device.

v0:
```python
import jax
import jax.numpy as jnp
from jax import lax
from jax.sharding import PartitionSpec as P

HD = 128
BLOCK = 512


def shifted(value, axis, steps):
    count = lax.axis_size(axis)
    leading, last = (max(0, -steps), min(count, count - steps))
    return lax.ppermute(value, axis, [(source, source + steps) for source in range(leading, last)])


def earlier_total(state):
    total = state
    distance = 1
    while distance < lax.axis_size("ctx"):
        total = total + shifted(total, "ctx", distance)
        distance = distance * 2
    return total


def later_total(state):
    total = state
    distance = 1
    while distance < lax.axis_size("ctx"):
        total = total + shifted(total, "ctx", -distance)
        distance = distance * 2
    return total


def shards(query, keys, values, grad_out):
    query_part, keys_part, values_part, grads_part = (
        lax.all_to_all(query, "head", split_axis=2, concat_axis=1, tiled=True),
        lax.all_to_all(keys, "head", split_axis=2, concat_axis=1, tiled=True),
        lax.all_to_all(values, "head", split_axis=2, concat_axis=1, tiled=True),
        lax.all_to_all(grad_out, "head", split_axis=2, concat_axis=1, tiled=True),
    )
    row_count = keys_part.shape[1]
    full_width = keys_part.shape[2]
    head_count = full_width // HD
    count = row_count // BLOCK
    length = row_count * lax.axis_size("ctx")
    factor = (HD * length) ** (-0.5)

    def split_heads(x):
        return x.reshape(count, BLOCK, head_count, HD).transpose(0, 2, 1, 3)

    query_blocks = split_heads(query_part)
    keys_blocks = split_heads(keys_part)
    values_blocks = split_heads(values_part)
    grads_blocks = split_heads(grads_part)
    key_own = jnp.einsum(
        "nhca,nhcb->nhab", keys_blocks, values_blocks, preferred_element_type=jnp.float32
    )
    query_own = jnp.einsum(
        "nhca,nhcb->nhab", query_blocks, grads_blocks, preferred_element_type=jnp.float32
    )
    key_device = jnp.sum(key_own, 0)
    query_device = jnp.sum(query_own, 0)
    key_prior = earlier_total(key_device) - key_device
    query_later = later_total(query_device) - query_device
    key_states = key_prior[None] + (jnp.cumsum(key_own, 0) - key_own)
    query_states = query_later[None] + (query_device[None] - jnp.cumsum(query_own, 0))
    key_rounded = key_states.astype(jnp.bfloat16)
    query_rounded = query_states.astype(jnp.bfloat16)
    causal = jnp.tril(jnp.ones((BLOCK, BLOCK), jnp.bool_))
    out_scores = (
        jnp.einsum(
            "nhpd,nhtd->nhpt", grads_blocks, values_blocks, preferred_element_type=jnp.float32
        )
        * factor
    )
    out_scores = jnp.where(causal[None, None], out_scores, 0.0).astype(jnp.bfloat16)
    key_scores = (
        jnp.einsum("nhpd,nhtd->nhpt", query_blocks, keys_blocks, preferred_element_type=jnp.float32)
        * factor
    )
    key_scores = jnp.where(causal[None, None], key_scores, 0.0).astype(jnp.bfloat16)
    grad_query = jnp.einsum(
        "nhpt,nhtd->nhpd", out_scores, keys_blocks, preferred_element_type=jnp.float32
    )
    grad_query = grad_query + factor * jnp.einsum(
        "nhpe,nhde->nhpd", grads_blocks, key_rounded, preferred_element_type=jnp.float32
    )
    grad_key = jnp.einsum(
        "nhpt,nhpd->nhtd", out_scores, query_blocks, preferred_element_type=jnp.float32
    )
    grad_key = grad_key + factor * jnp.einsum(
        "nhte,nhde->nhtd", values_blocks, query_rounded, preferred_element_type=jnp.float32
    )
    grad_value = jnp.einsum(
        "nhpt,nhpe->nhte", key_scores, grads_blocks, preferred_element_type=jnp.float32
    )
    grad_value = grad_value + factor * jnp.einsum(
        "nhtd,nhde->nhte", keys_blocks, query_rounded, preferred_element_type=jnp.float32
    )
    shape = (1, row_count, full_width)

    def merge_heads(x):
        return x.astype(jnp.bfloat16).transpose(0, 2, 1, 3).reshape(shape)

    return (merge_heads(grad_query), merge_heads(grad_key), merge_heads(grad_value))


def solution(mesh):
    in_specs = (
        P("ctx", "head", None),
        P("ctx", "head", None),
        P("ctx", "head", None),
        P("ctx", "head", None),
    )
    out_specs = (P("ctx", None, "head"), P("ctx", None, "head"), P("ctx", None, "head"))
    return jax.shard_map(shards, mesh=mesh, in_specs=in_specs, out_specs=out_specs, check_vma=False)
```

profile of v0, /device:TPU:0, one launch (start us, length us, event | category | flops | bytes accessed | tf_op | source)
XLA Modules:
  0.0 240.3 jit_solution(14525378874674280255)
XLA Ops:
  0.6 5.0 %copy.45 = bf16[1,128,4096]{1,0,2:T(2,128)(2,1)S(1)} copy(bf16[1,128,4096]{2,1,0:T(8,128)(2,1)} %param.7) | data formatting | bytes 2097152 | tf_op args[3]
  6.2 22.4 %reduce.1 = bf16[4096,128]{1,0:T(8,128)(2,1)S(1)} reduce(bf16[4096,1,128]{2,1,0:T(2,128)(2,1)S(1)} %bitcast.120, bf16[]{:T(256)} %broadcast.34), dimensions={1}, to_apply=%bitcast.98.reduce_sub_computation | reduce | bytes 2097154
  30.3 5.2 %all-to-all-start = ((bf16[4,2,65536]{2,1,0:T(2,128)(2,1)}), bf16[4,2,65536]{2,1,0:T(2,128)(2,1)S(1)}, u32[]{:S(2)}, u32[]{:S(2)}) async-start(bf16[4,2,65536]{2,1,0:T(2,128)(2,1)} %reshape.124), calls=%async_computation | async-start | bytes 2097152 | tf_op jit(solution)/shard_map/all_to_all | solution.py:39
  35.5 5.0 %copy.53 = bf16[1,128,4096]{1,0,2:T(2,128)(2,1)S(1)} copy(bf16[1,128,4096]{2,1,0:T(8,128)(2,1)} %param.4) | data formatting | bytes 2097152 | tf_op args[0]
  40.5 23.4 %reduce.3 = bf16[4096,128]{1,0:T(8,128)(2,1)} reduce(bf16[4096,1,128]{2,1,0:T(2,128)(2,1)S(1)} %bitcast.122, bf16[]{:T(256)} %broadcast.34), dimensions={1}, to_apply=%bitcast.102.reduce_sub_computation | reduce | bytes 2097154
  63.9 3.5 %reshape.128 = bf16[4,2,65536]{2,1,0:T(2,128)(2,1)} reshape(bf16[4096,128]{1,0:T(8,128)(2,1)} %reduce.3) | data formatting | bytes 2097152
  67.4 4.4 %all-to-all-start.3 = ((bf16[4,2,65536]{2,1,0:T(2,128)(2,1)}), bf16[4,2,65536]{2,1,0:T(2,128)(2,1)}, u32[]{:S(2)}, u32[]{:S(2)}) async-start(bf16[4,2,65536]{2,1,0:T(2,128)(2,1)} %reshape.128), calls=%async_computation.3 | async-start | bytes 2097152 | tf_op jit(solution)/shard_map/all_to_all | solution.py:36
  71.8 5.0 %copy.51 = bf16[1,128,4096]{1,0,2:T(2,128)(2,1)S(1)} copy(bf16[1,128,4096]{2,1,0:T(8,128)(2,1)} %param.5) | data formatting | bytes 2097152 | tf_op args[1]
  76.9 23.4 %reduce.2 = bf16[4096,128]{1,0:T(8,128)(2,1)} reduce(bf16[4096,1,128]{2,1,0:T(2,128)(2,1)S(1)} %bitcast.123, bf16[]{:T(256)} %broadcast.34), dimensions={1}, to_apply=%bitcast.100.reduce_sub_computation | reduce | bytes 2097154
  100.3 3.5 %reshape.126 = bf16[4,2,65536]{2,1,0:T(2,128)(2,1)} reshape(bf16[4096,128]{1,0:T(8,128)(2,1)} %reduce.2) | data formatting | bytes 2097152
  103.7 4.2 %all-to-all-start.2 = ((bf16[4,2,65536]{2,1,0:T(2,128)(2,1)}), bf16[4,2,65536]{2,1,0:T(2,128)(2,1)}, u32[]{:S(2)}, u32[]{:S(2)}) async-start(bf16[4,2,65536]{2,1,0:T(2,128)(2,1)} %reshape.126), calls=%async_computation.2 | async-start | bytes 2097152 | tf_op jit(solution)/shard_map/all_to_all | solution.py:37
  108.0 5.0 %copy.48 = bf16[1,128,4096]{1,0,2:T(2,128)(2,1)S(1)} copy(bf16[1,128,4096]{2,1,0:T(8,128)(2,1)} %param.6) | data formatting | bytes 2097152 | tf_op args[2]
  113.0 23.4 %reduce = bf16[4096,128]{1,0:T(8,128)(2,1)} reduce(bf16[4096,1,128]{2,1,0:T(2,128)(2,1)S(1)} %bitcast.121, bf16[]{:T(256)} %broadcast.34), dimensions={1}, to_apply=%bitcast.96.reduce_sub_computation | reduce | bytes 2097154
  136.4 3.5 %reshape.122 = bf16[4,2,65536]{2,1,0:T(2,128)(2,1)} reshape(bf16[4096,128]{1,0:T(8,128)(2,1)} %reduce) | data formatting | bytes 2097152
  139.9 4.5 %all-to-all-start.1 = ((bf16[4,2,65536]{2,1,0:T(2,128)(2,1)}), bf16[4,2,65536]{2,1,0:T(2,128)(2,1)}, u32[]{:S(2)}, u32[]{:S(2)}) async-start(bf16[4,2,65536]{2,1,0:T(2,128)(2,1)} %reshape.122), calls=%async_computation.1 | async-start | bytes 2097152 | tf_op jit(solution)/shard_map/all_to_all | solution.py:38
  146.4 2.6 %reshape.129 = bf16[4096,1,128]{2,1,0:T(2,128)(2,1)S(1)} reshape(bf16[4,2,65536]{2,1,0:T(2,128)(2,1)} %all-to-all-done.3) | data formatting | bytes 2097152
  153.0 4.0 %reshape.127 = bf16[4096,1,128]{2,1,0:T(2,128)(2,1)} reshape(bf16[4,2,65536]{2,1,0:T(2,128)(2,1)} %all-to-all-done.2) | data formatting | bytes 2097152
  162.0 4.0 %reshape.123 = bf16[4096,1,128]{2,1,0:T(2,128)(2,1)} reshape(bf16[4,2,65536]{2,1,0:T(2,128)(2,1)} %all-to-all-done.1) | data formatting | bytes 2097152
  165.9 2.7 %copy.71 = bf16[1,128,4096]{1,2,0:T(8,128)(2,1)} copy(bf16[1,128,4096]{1,0,2:T(2,128)(2,1)} %bitcast.119) | data formatting | bytes 2097152
  168.6 2.3 copy.49
  172.9 3.1 %collective-permute-start = (f32[8,128,128]{2,1,0:T(8,128)S(1)}, f32[8,128,128]{2,1,0:T(8,128)S(1)}, u32[]{:S(2)}, u32[]{:S(2)}) collective-permute-start(f32[8,128,128]{2,1,0:T(8,128)S(1)} %fusion.20), channel_id=1, source_target_pairs={{0,1},{1,2},{2,3},{3,4},{4,5},{5,6},{6,7},{8,9},{9,10},{10,11},{11... | collective-permute-start | bytes 1572872 | tf_op jit(solution)/shard_map/ppermute | solution.py:13
  182.0 2.8 %fusion.27 = f32[8,512,128]{1,2,0:T(8,128)} fusion(bf16[8,512,512]{2,1,0:T(8,128)(2,1)S(1)} %select_convert_fusion.1, bf16[1,512,8,128]{1,3,2,0:T(8,128)(2,1)S(1)} %reshape.115), kind=kOutput, calls=%fused_computation.29 | convolution fusion | flops 536870912 | bytes 7340032 | tf_op jit(solution)/shard_map/nhpt,nhtd->nhpd/dot_general | solution.py:82
  185.7 5.4 %collective-permute-start.1 = (f32[8,128,128]{2,1,0:T(8,128)}, f32[8,128,128]{2,1,0:T(8,128)}, u32[]{:S(2)}, u32[]{:S(2)}) collective-permute-start(f32[8,128,128]{2,1,0:T(8,128)} %add.42), channel_id=1, source_target_pairs={{0,2},{1,3},{2,4},{3,5},{4,6},{5,7},{8,10},{9,11},{10,12},{11,13},... | collective-permute-start | bytes 1572872 | tf_op jit(solution)/shard_map/ppermute | solution.py:13
  191.1 4.1 %collective-permute-done.4 = f32[8,128,128]{2,1,0:T(8,128)S(1)} collective-permute-done((f32[8,128,128]{2,1,0:T(8,128)S(1)}, f32[8,128,128]{2,1,0:T(8,128)S(1)}, u32[]{:S(2)}, u32[]{:S(2)}) %collective-permute-start.4) | collective-permute-done | bytes 524320 | tf_op jit(solution)/shard_map/ppermute | solution.py:13
  198.4 4.6 %fusion = f32[8,512,128]{1,2,0:T(8,128)} fusion(pred[512,512]{1,0:T(8,128)(4,1)S(1)} %iota_compare_fusion, bf16[8,512,128]{2,0,1:T(8,128)(2,1)} %bitcast_bitcast_fusion, bf16[1,512,8,128]{1,3,2,0:T(8,128)(2,1)S(1)} %reshape.118, bf16[1,512,8,128]{1,3,2,0:T(8,128)(2,1)S(1)} %reshape.115), kind=kOutput, calls=%fused_computation.2 | convolution fusion | flops 1080033280 | bytes 5505024 | tf_op jit(solution)/shard_map/nhpt,nhpe->nhte/dot_general | solution.py:94
  205.2 7.1 %collective-permute-start.2 = (f32[8,128,128]{2,1,0:T(8,128)}, f32[8,128,128]{2,1,0:T(8,128)}, u32[]{:S(2)}, u32[]{:S(2)}) collective-permute-start(f32[8,128,128]{2,1,0:T(8,128)} %add.43), channel_id=1, source_target_pairs={{0,4},{1,5},{2,6},{3,7},{8,12},{9,13},{10,14},{11,15},{16,20},{17,... | collective-permute-start | bytes 1572872 | tf_op jit(solution)/shard_map/ppermute | solution.py:13
  212.3 12.1 %collective-permute-done.5 = f32[8,128,128]{2,1,0:T(8,128)} collective-permute-done((f32[8,128,128]{2,1,0:T(8,128)}, f32[8,128,128]{2,1,0:T(8,128)}, u32[]{:S(2)}, u32[]{:S(2)}) %collective-permute-start.5) | collective-permute-done | bytes 524320 | tf_op jit(solution)/shard_map/ppermute | solution.py:13
  227.3 2.4 copy.62
  229.7 3.0 %fusion.7 = bf16[8,512,128]{1,2,0:T(8,128)(2,1)} fusion(f32[8,512,128]{1,2,0:T(8,128)} %fusion.14, bf16[8,128,128]{2,1,0:T(8,128)(2,1)S(1)} %add_convert_fusion, bf16[1,512,8,128]{3,2,1,0:T(8,128)(2,1)S(1)} %bitcast.115), kind=kOutput, calls=%fused_computation.10 | convolution fusion | flops 135790592 | bytes 4456448 | tf_op jit(solution)/shard_map/nhte,nhde->nhtd/dot_general | solution.py:91
  232.7 2.4 %copy.61 = bf16[1,512,1024]{2,1,0:T(8,128)(2,1)} copy(bf16[1,512,1024]{1,2,0:T(8,128)(2,1)} %bitcast.124) | data formatting | bytes 2097152
  235.2 2.9 %fusion.8 = bf16[8,512,128]{1,2,0:T(8,128)(2,1)} fusion(f32[8,512,128]{1,2,0:T(8,128)S(1)} %copy-done.2, bf16[1,512,8,128]{3,2,1,0:T(8,128)(2,1)S(1)} %bitcast.112, f32[8,128,128]{2,1,0:T(8,128)} %copy-done.3, f32[8,128,128]{2,1,0:T(8,128)} %add.43, f32[8,128,128]{2,1,0:T(8,128)} %collective-permute-done.2), kind=kOutput, calls=%fused_computation.12 | convolution fusion | flops 136445952 | bytes 5767168 | tf_op jit(solution)/shard_map/nhpe,nhde->nhpd/dot_general | solution.py:85
  238.0 2.3 copy.60
  (46 shorter events, 30.4 us)
Async XLA Ops:
  30.3 37.1 %all-to-all-start = ((bf16[4,2,65536]{2,1,0:T(2,128)(2,1)}), bf16[4,2,65536]{2,1,0:T(2,128)(2,1)S(1)}, u32[]{:S(2)}, u32[]{:S(2)}) async-start(bf16[4,2,65536]{2,1,0:T(2,128)(2,1)} %reshape.124), calls=%async_computation | async-start | bytes 2097152 | tf_op jit(solution)/shard_map/all_to_all | solution.py:39
  67.4 36.3 %all-to-all-start.3 = ((bf16[4,2,65536]{2,1,0:T(2,128)(2,1)}), bf16[4,2,65536]{2,1,0:T(2,128)(2,1)}, u32[]{:S(2)}, u32[]{:S(2)}) async-start(bf16[4,2,65536]{2,1,0:T(2,128)(2,1)} %reshape.128), calls=%async_computation.3 | async-start | bytes 2097152 | tf_op jit(solution)/shard_map/all_to_all | solution.py:36
  103.7 36.2 %all-to-all-start.2 = ((bf16[4,2,65536]{2,1,0:T(2,128)(2,1)}), bf16[4,2,65536]{2,1,0:T(2,128)(2,1)}, u32[]{:S(2)}, u32[]{:S(2)}) async-start(bf16[4,2,65536]{2,1,0:T(2,128)(2,1)} %reshape.126), calls=%async_computation.2 | async-start | bytes 2097152 | tf_op jit(solution)/shard_map/all_to_all | solution.py:37
  139.9 22.1 %all-to-all-start.1 = ((bf16[4,2,65536]{2,1,0:T(2,128)(2,1)}), bf16[4,2,65536]{2,1,0:T(2,128)(2,1)}, u32[]{:S(2)}, u32[]{:S(2)}) async-start(bf16[4,2,65536]{2,1,0:T(2,128)(2,1)} %reshape.122), calls=%async_computation.1 | async-start | bytes 2097152 | tf_op jit(solution)/shard_map/all_to_all | solution.py:38
  151.7 25.7 %collective-permute-start.3 = (f32[8,128,128]{2,1,0:T(8,128)}, f32[8,128,128]{2,1,0:T(8,128)}, u32[]{:S(2)}, u32[]{:S(2)}) collective-permute-start(f32[8,128,128]{2,1,0:T(8,128)} %fusion.12), channel_id=1, source_target_pairs={{1,0},{2,1},{3,2},{4,3},{5,4},{6,5},{7,6},{9,8},{10,9},{11,10},{12... | collective-permute-start | bytes 1572872 | tf_op jit(solution)/shard_map/ppermute | solution.py:13
  172.4 5.1 %copy-start = (bf16[64,8,8,128]{3,2,1,0:T(8,128)(2,1)}, bf16[64,8,8,128]{3,2,1,0:T(8,128)(2,1)S(1)}, u32[]{:S(2)}) copy-start(bf16[64,8,8,128]{3,2,1,0:T(8,128)(2,1)S(1)} %copy.75) | copy-start | bytes 3145732
  172.9 12.0 %copy-start.3 = (f32[8,128,128]{2,1,0:T(8,128)}, f32[8,128,128]{2,1,0:T(8,128)S(1)}, u32[]{:S(2)}) copy-start(f32[8,128,128]{2,1,0:T(8,128)S(1)} %fusion.20) | copy-start | bytes 1572868
  172.9 12.0 %collective-permute-start = (f32[8,128,128]{2,1,0:T(8,128)S(1)}, f32[8,128,128]{2,1,0:T(8,128)S(1)}, u32[]{:S(2)}, u32[]{:S(2)}) collective-permute-start(f32[8,128,128]{2,1,0:T(8,128)S(1)} %fusion.20), channel_id=1, source_target_pairs={{0,1},{1,2},{2,3},{3,4},{4,5},{5,6},{6,7},{8,9},{9,10},{10,11},{11... | collective-permute-start | bytes 1572872 | tf_op jit(solution)/shard_map/ppermute | solution.py:13
  178.7 16.5 %collective-permute-start.4 = (f32[8,128,128]{2,1,0:T(8,128)S(1)}, f32[8,128,128]{2,1,0:T(8,128)S(1)}, u32[]{:S(2)}, u32[]{:S(2)}) collective-permute-start(f32[8,128,128]{2,1,0:T(8,128)S(1)} %add.47), channel_id=1, source_target_pairs={{2,0},{3,1},{4,2},{5,3},{6,4},{7,5},{10,8},{11,9},{12,10},{13,11},... | collective-permute-start | bytes 1572872 | tf_op jit(solution)/shard_map/ppermute | solution.py:13
  185.7 17.3 %collective-permute-start.1 = (f32[8,128,128]{2,1,0:T(8,128)}, f32[8,128,128]{2,1,0:T(8,128)}, u32[]{:S(2)}, u32[]{:S(2)}) collective-permute-start(f32[8,128,128]{2,1,0:T(8,128)} %add.42), channel_id=1, source_target_pairs={{0,2},{1,3},{2,4},{3,5},{4,6},{5,7},{8,10},{9,11},{10,12},{11,13},... | collective-permute-start | bytes 1572872 | tf_op jit(solution)/shard_map/ppermute | solution.py:13
  196.1 28.3 %collective-permute-start.5 = (f32[8,128,128]{2,1,0:T(8,128)}, f32[8,128,128]{2,1,0:T(8,128)}, u32[]{:S(2)}, u32[]{:S(2)}) collective-permute-start(f32[8,128,128]{2,1,0:T(8,128)} %add.48), channel_id=1, source_target_pairs={{4,0},{5,1},{6,2},{7,3},{12,8},{13,9},{14,10},{15,11},{20,16},{21,... | collective-permute-start | bytes 1572872 | tf_op jit(solution)/shard_map/ppermute | solution.py:13
  203.0 22.8 %copy-start.4 = (f32[8,512,128]{1,2,0:T(8,128)S(1)}, f32[8,512,128]{1,2,0:T(8,128)}, u32[]{:S(2)}) copy-start(f32[8,512,128]{1,2,0:T(8,128)} %fusion) | copy-start | bytes 6291460
  205.2 29.9 %collective-permute-start.2 = (f32[8,128,128]{2,1,0:T(8,128)}, f32[8,128,128]{2,1,0:T(8,128)}, u32[]{:S(2)}, u32[]{:S(2)}) collective-permute-start(f32[8,128,128]{2,1,0:T(8,128)} %add.43), channel_id=1, source_target_pairs={{0,4},{1,5},{2,6},{3,7},{8,12},{9,13},{10,14},{11,15},{16,20},{17,... | collective-permute-start | bytes 1572872 | tf_op jit(solution)/shard_map/ppermute | solution.py:13
  227.3 2.4 copy-start.1
  232.7 2.4 %copy-start.2 = (f32[8,512,128]{1,2,0:T(8,128)S(1)}, f32[8,512,128]{1,2,0:T(8,128)}, u32[]{:S(2)}) copy-start(f32[8,512,128]{1,2,0:T(8,128)} %fusion.27) | copy-start | bytes 6291460
where the time goes:
time: 242 us; the launch traced here: 240 us
  other arithmetic  99.3 us (41%)
  local copies, waits for them, and re-layouts  66.1 us (27%)
  starting transfers between devices  37.7 us (16%)
  matrix products  20.1 us (8%)
  waiting for transfers between devices  16.2 us (7%)
    unnamed x4, other arithmetic  92.6 us
    unnamed x32, local copies, waits for them, and re-layouts  57.8 us
    ppermute x6, starting transfers between devices, shifted(): lax.ppermute(value, axis, [(source, source + steps) for source in range(l...  19.4 us
    ppermute x6, waiting for transfers between devices, shifted(): lax.ppermute(value, axis, [(source, source + steps) for source in range(l...  16.2 us
    all_to_all x1, starting transfers between devices, shards(): lax.all_to_all(grad_out, 'head', split_axis=2, concat_axis=1, tiled=True)  5.16 us
  transfers between devices with their start and end apart: 10, of which 2 were waited for; matrix products, arithmetic and copies ran while one was open for 63% of the time, Pallas kernels for 0%

commit v1 on v0

v1 whole, which is shorter than its diff:
```python
import functools

import jax
import jax.numpy as jnp
from jax import lax
from jax.experimental import pallas as pl
from jax.experimental.pallas import tpu as pltpu
from jax.sharding import PartitionSpec as P

HD = 128
TILE = 256
F32 = jnp.float32
BF16 = jnp.bfloat16
PARAMS = pltpu.CompilerParams(vmem_limit_bytes=40 * 1024 * 1024)


def dot(a, b, contract):
    return lax.dot_general(a, b, ((contract[:1], contract[1:]), ((), ())), preferred_element_type=F32)


def cost(flops, count):
    return pl.CostEstimate(flops=10**10, bytes_accessed=2 * count, transcendentals=0)


def target_of(me, step, parts):
    if parts & (parts - 1) == 0:
        return me ^ step
    return (me + step) % parts


def source_of(me, step, parts):
    if parts & (parts - 1) == 0:
        return me ^ step
    return (me + parts - step) % parts


def send(value, axis, target):
    count = lax.axis_size(axis)
    return lax.ppermute(value, axis, [(index, target(index)) for index in range(count)])


def pack_kernel(parts, heads, chunks, *refs):
    inputs, outputs, (loaded, staged, load_sem, store_sem) = refs[:4], refs[4:-4], refs[-4:]
    me = lax.axis_index("head")
    group = heads * HD

    def load(step, tensor):
        start = pl.multiple_of(target_of(me, step, parts) * group, group)
        return pltpu.make_async_copy(
            inputs[tensor].at[0, :, pl.ds(start, group)],
            loaded.at[step, tensor],
            load_sem.at[step, tensor],
        )

    order = list(range(1, parts)) + [0]
    for step in order:
        for tensor in range(4):
            load(step, tensor).start()
    last = len(chunks) - 1
    stores = []
    for step in order:
        for tensor in range(4):
            load(step, tensor).wait()
        at = 0
        head = 0
        for chunk, count in enumerate(chunks):
            first = at
            for _ in range(count):
                for tensor in range(4):
                    staged[step, at] = loaded[step, tensor, :, head * HD : (head + 1) * HD]
                    at += 1
                head += 1
            if chunk == 0:
                for late in range(heads - chunks[last], heads):
                    query, keys, values, grads = (
                        loaded[step, tensor, :, late * HD : (late + 1) * HD] for tensor in range(4)
                    )
                    staged[step, at] = dot(values, keys, (0, 0)).astype(BF16)
                    staged[step, at + 1] = dot(query, grads, (0, 0)).astype(BF16)
                    at += 2
            store = pltpu.make_async_copy(
                staged.at[step, first:at],
                outputs[chunk * parts + step],
                store_sem.at[step, chunk],
            )
            store.start()
            stores.append(store)
    for store in stores:
        store.wait()


@jax.named_scope("pack")
def pack(arrays, parts, heads, chunks):
    _, rows, full = arrays[0].shape
    units = [4 * count for count in chunks]
    units[0] += 2 * chunks[-1]
    out = [jax.ShapeDtypeStruct((unit, rows, HD), BF16) for unit in units for _ in range(parts)]
    flat = pl.pallas_call(
        functools.partial(pack_kernel, parts, heads, chunks),
        in_specs=[pl.BlockSpec(memory_space=pltpu.HBM)] * 4,
        out_specs=[pl.BlockSpec(memory_space=pl.ANY)] * len(out),
        out_shape=out,
        scratch_shapes=[
            pltpu.VMEM((parts, 4, rows, heads * HD), BF16),
            pltpu.VMEM((parts, sum(units), rows, HD), BF16),
            pltpu.SemaphoreType.DMA((parts, 4)),
            pltpu.SemaphoreType.DMA((parts, len(chunks))),
        ],
        compiler_params=PARAMS,
        cost_estimate=cost(0, 8 * rows * full),
    )(*[pltpu.with_memory_space_constraint(value, pltpu.HBM) for value in arrays])
    return [flat[chunk * parts : (chunk + 1) * parts] for chunk in range(len(chunks))]


def state_kernel(parts, heads, extra, *refs):
    inputs, out = refs[:parts], refs[-1]
    for head in range(heads):
        query, keys, values, grads = (
            jnp.concatenate([ref[4 * head + tensor] for ref in inputs], 0) for tensor in range(4)
        )
        out[0, head] = dot(values, keys, (0, 0))
        out[1, head] = dot(query, grads, (0, 0))
    for late in range(extra):
        for state in range(2):
            at = 4 * heads + 2 * late + state
            out[state, heads + late] = sum(ref[at].astype(F32) for ref in inputs)


@jax.named_scope("own_states")
def own_states(received, heads, extra, before):
    parts = len(received)
    rows = received[0].shape[1]
    return pl.pallas_call(
        functools.partial(state_kernel, parts, heads, extra),
        in_specs=[pl.BlockSpec(memory_space=pltpu.VMEM)] * parts
        + [pl.BlockSpec(memory_space=pl.ANY)] * len(before),
        out_shape=jax.ShapeDtypeStruct((2, heads + extra, HD, HD), F32),
        compiler_params=PARAMS,
        cost_estimate=cost(4 * heads * parts * rows * HD * HD, parts * received[0].size),
    )(*received, *before)


def chip_kernel(chips, own, partner, *outputs):
    chip = lax.axis_index("ctx") // 2
    keys = (own[0] + partner[0]).astype(BF16)
    query = (own[1] + partner[1]).astype(BF16)
    for step in range(1, chips):
        outputs[step - 1][...] = jnp.where(chip + step < chips, keys, query)


@jax.named_scope("chip_states")
def chip_states(own, partner, chips):
    shape = own.shape[1:]
    return pl.pallas_call(
        functools.partial(chip_kernel, chips),
        out_shape=[jax.ShapeDtypeStruct(shape, BF16)] * (chips - 1),
        compiler_params=PARAMS,
        cost_estimate=cost(0, 4 * own.size),
    )(own, partner)


def other_states(own):
    spans = lax.axis_size("ctx")
    chips = spans // 2
    if spans % 2 or chips > 4:
        return [lax.all_gather(own.astype(BF16), "ctx")]
    partner = send(own, "ctx", lambda index: index ^ 1)
    sums = chip_states(own, partner, chips)
    return [partner] + [
        send(value, "ctx", lambda index: (index + 2 * step) % spans)
        for step, value in enumerate(sums, 1)
    ]


def read_states(refs, spans, head):
    me = lax.axis_index("ctx")
    zero = jnp.zeros((HD, HD), F32)
    if len(refs) == 1:

        def add(span, totals):
            keys, query = totals
            keys = keys + jnp.where(span < me, refs[0][span, 0, head].astype(F32), 0.0)
            query = query + jnp.where(span > me, refs[0][span, 1, head].astype(F32), 0.0)
            return keys, query

        return lax.fori_loop(0, spans, add, (zero, zero))
    partner, others = refs[0], refs[1:]
    chip, core = me // 2, me % 2
    keys = jnp.where(core == 1, partner[0, head], 0.0)
    query = jnp.where(core == 0, partner[1, head], 0.0)
    for step, ref in enumerate(others, 1):
        part = ref[head].astype(F32)
        keys = keys + jnp.where(chip >= step, part, 0.0)
        query = query + jnp.where(chip < step, part, 0.0)
    return keys, query


def grads_kernel(parts, spans, factor, offset, counts, *refs):
    received, states = refs[: counts[0]], refs[counts[0] : counts[0] + counts[1]]
    grad_query, grad_key, grad_value, ordered = refs[-4:]
    me = lax.axis_index("head")
    rows = received[0].shape[1]
    head = pl.program_id(0)
    for step, ref in enumerate(received):
        place = source_of(me, step, parts)
        for tensor in range(4):
            ordered[tensor, place] = ref[tensor]
    key_state, query_state = read_states(states, spans, head + offset)
    key_state = key_state.astype(BF16)
    query_turned = query_state.T.astype(BF16)
    query_state = query_state.astype(BF16)
    length = parts * rows
    tiles = length // TILE
    query, keys, values, grads = (
        ordered[tensor].reshape(tiles, TILE, HD) for tensor in range(4)
    )
    row = lax.broadcasted_iota(jnp.int32, (TILE, TILE), 0)
    column = lax.broadcasted_iota(jnp.int32, (TILE, TILE), 1)

    def scores(a, b, keep):
        value = dot(a, b, (1, 1))
        if keep is not None:
            value = jnp.where(keep, value, 0.0)
        return value.astype(BF16)

    def total(lefts, rights):
        value = dot(jnp.concatenate(lefts, 1), jnp.concatenate(rights, 0), (1, 0))
        return (value * factor).astype(BF16)

    for i in range(tiles):
        at = slice(i * TILE, (i + 1) * TILE)
        low = [scores(grads[i], values[j], column <= row if i == j else None) for j in range(i + 1)]
        grad_query[0, at] = total(
            low + [grads[i]], [keys[j] for j in range(i + 1)] + [key_state]
        )
        high = [scores(values[i], grads[j], row <= column if i == j else None) for j in range(i, tiles)]
        grad_key[0, at] = total(
            high + [values[i]], [query[j] for j in range(i, tiles)] + [query_turned]
        )
        high = [scores(keys[i], query[j], row <= column if i == j else None) for j in range(i, tiles)]
        grad_value[0, at] = total(
            high + [keys[i]], [grads[j] for j in range(i, tiles)] + [query_state]
        )


@jax.named_scope("gradients")
def gradients(received, states, offset, held, first, heads, group, factor):
    parts = len(received)
    rows = received[0].shape[1]
    spans = lax.axis_size("ctx")
    length = parts * rows
    kept = len(held)
    counts = (parts, len(states))
    return pl.pallas_call(
        functools.partial(grads_kernel, parts, spans, factor, offset, counts),
        grid=(heads,),
        in_specs=[pl.BlockSpec((4, rows, HD), lambda h: (h, 0, 0))] * parts
        + [pl.BlockSpec(value.shape, lambda h, rank=value.ndim: (0,) * rank) for value in states]
        + [pl.BlockSpec(memory_space=pl.ANY)] * kept,
        out_specs=[pl.BlockSpec((1, length, HD), lambda h: (0, 0, first + h))] * 3,
        out_shape=[jax.ShapeDtypeStruct((1, length, group), BF16)] * 3,
        scratch_shapes=[pltpu.VMEM((4, parts, rows, HD), BF16)],
        input_output_aliases={sum(counts) + index: index for index in range(kept)},
        compiler_params=PARAMS,
        cost_estimate=cost(
            heads * (8 * length * length * HD + 6 * length * HD * HD), 7 * heads * length * HD
        ),
    )(*received, *states, *held)


def shards(query, keys, values, grad_out):
    parts = lax.axis_size("head")
    spans = lax.axis_size("ctx")
    _, rows, full = query.shape
    group = full // parts
    heads = group // HD
    factor = (HD * rows * parts * spans) ** -0.5
    late = max(1, heads // 4)
    middle = (heads - late) // 2
    chunks = [heads - late - middle, middle, late]
    packed = pack((query, keys, values, grad_out), parts, heads, chunks)
    received = [
        [values[0]]
        + [
            send(values[step], "head", lambda index: target_of(index, step, parts))
            for step in range(1, parts)
        ]
        for values in packed
    ]
    early = other_states(own_states(received[0], chunks[0], late, []))
    second = other_states(own_states(received[1], middle, 0, early[1:]))
    held = gradients(received[0], early, 0, (), 0, chunks[0], group, factor)
    held = gradients(received[1], second, 0, held, chunks[0], middle, group, factor)
    held = gradients(received[2], early, chunks[0], held, heads - late, late, group, factor)
    return tuple(held)


def solution(mesh):
    spec = P("ctx", "head", None)
    out = P("ctx", None, "head")
    return jax.shard_map(
        shards, mesh=mesh, in_specs=(spec,) * 4, out_specs=(out,) * 3, check_vma=False
    )
```

time: 242 us -> 79.1 us (0.33)
  other arithmetic: 99.3 us -> 0 us
  local copies, waits for them, and re-layouts: 66.1 us -> 0 us
  matrix products: 20.1 us -> 0 us
  Pallas kernels: 0 us -> 18.5 us
  waiting for transfers between devices: 16.2 us -> 34.6 us
  starting transfers between devices: 37.7 us -> 25.2 us
    unnamed x4 -> x0, other arithmetic: 92.6 us -> none
    unnamed x32 -> x0, local copies, waits for them, and re-layouts: 57.8 us -> none
    dot_general x9 -> x0, matrix products: 20.1 us -> none  [the longest x1 4.59 us: shards(): jnp.einsum('nhpt,nhpe->nhte', key_scores, grads_blocks, preferred_element...]
    pallas_call x0 -> x8, Pallas kernels: none -> 18.5 us  [the longest x3 13.3 us: gradients(): pl.pallas_call(functools.partial(grads_kernel, parts, spans, factor, offs...]
    ppermute x6 -> x17, waiting for transfers between devices: 16.2 us -> 34.6 us  [send(): lax.ppermute(value, axis, [(index, target(index)) for index in range(coun...]
    all_to_all x4 -> x0, starting transfers between devices: 18.3 us -> none  [the longest x1 5.16 us: shards(): lax.all_to_all(grad_out, 'head', split_axis=2, concat_axis=1, tiled=True)]
    ppermute x6 -> x17, starting transfers between devices: 19.4 us -> 25.2 us  [send(): lax.ppermute(value, axis, [(index, target(index)) for index in range(coun...]
    all_to_all x4 -> x0, local copies, waits for them, and re-layouts: 5.39 us -> none  [the longest x1 2.26 us: shards(): lax.all_to_all(values, 'head', split_axis=2, concat_axis=1, tiled=True)]
  transfers between devices with their start and end apart: 10 -> 17, of which waited for: 2 -> 6; matrix products, arithmetic and copies ran while one was open for 63% -> 0% of each run, Pallas kernels for 0% -> 13%
where the time goes in v1:
time: 79.1 us; the launch traced here: 78.9 us
  waiting for transfers between devices  34.6 us (44%)
  starting transfers between devices  25.2 us (32%)
  Pallas kernels  18.5 us (23%)
    ppermute x17, waiting for transfers between devices, send(): lax.ppermute(value, axis, [(index, target(index)) for index in range(coun...  34.6 us
    ppermute x17, starting transfers between devices, send(): lax.ppermute(value, axis, [(index, target(index)) for index in range(coun...  25.2 us
    pallas_call x3, Pallas kernels, gradients(): pl.pallas_call(functools.partial(grads_kernel, parts, spans, factor, offs...  13.3 us
    pallas_call x1, Pallas kernels, pack(): pl.pallas_call(functools.partial(pack_kernel, parts, heads, chunks), in_s...  4.16 us
  transfers between devices with their start and end apart: 17, of which 6 were waited for; matrix products, arithmetic and copies ran while one was open for 0% of the time, Pallas kernels for 13%

profile of v1, /device:TPU:0, one launch (start us, length us, event | category | flops | bytes accessed | tf_op | source)
XLA Modules:
  0.0 78.9 jit_solution(4205186019680740605)
XLA Ops:
  0.6 4.2 %pack.1 = (bf16[16,128,128]{2,1,0:T(8,128)(2,1)S(1)}, bf16[16,128,128]{2,1,0:T(8,128)(2,1)S(1)}, bf16[16,128,128]{2,1,0:T(8,128)(2,1)S(1)}, bf16[16,128,128]{2,1...) custom-call(bf16[1,128,4096]{2,1,0:T(8,128)(2,1)} %refs_0_.1, ...), custom_call_target="tpu_custom_call" | custom-call | flops 10000000000 | bytes 8388608 | tf_op jit(solution)/shard_map/pack/pallas_call | solution.py:98
  4.8 3.0 %collective-permute-start.3 = (bf16[16,128,128]{2,1,0:T(8,128)(2,1)S(1)}, bf16[16,128,128]{2,1,0:T(8,128)(2,1)S(1)}, u32[]{:S(2)}, u32[]{:S(2)}) collective-permute-start(bf16[16,128,128]{2,1,0:T(8,128)(2,1)S(1)} %get-tuple-element.32), channel_id=1, source_target_pairs={{0,8},{8,0},{16,24},{24,16},{1,9},{9,1},{17,25},{25,17},{2,10},{10... | collective-permute-start | bytes 1572872 | tf_op jit(solution)/shard_map/ppermute | solution.py:39
  7.8 1.5 %collective-permute-start.4 = (bf16[16,128,128]{2,1,0:T(8,128)(2,1)S(1)}, bf16[16,128,128]{2,1,0:T(8,128)(2,1)S(1)}, u32[]{:S(2)}, u32[]{:S(2)}) collective-permute-start(bf16[16,128,128]{2,1,0:T(8,128)(2,1)S(1)} %get-tuple-element.33), channel_id=1, source_target_pairs={{0,16},{8,24},{16,0},{24,8},{1,17},{9,25},{17,1},{25,9},{2,18},{10... | collective-permute-start | bytes 1572872 | tf_op jit(solution)/shard_map/ppermute | solution.py:39
  9.3 0.0 collective-permute-start.5
  9.3 11.2 %collective-permute-done.3.refs_1_ = bf16[16,128,128]{2,1,0:T(8,128)(2,1)S(1)} collective-permute-done((bf16[16,128,128]{2,1,0:T(8,128)(2,1)S(1)}, bf16[16,128,128]{2,1,0:T(8,128)(2,1)S(1)}, u32[]{:S(2)}, u32[]{:S(2)}) %collective-permute-start.3) | collective-permute-done | bytes 524320 | tf_op jit(solution)/shard_map/ppermute | solution.py:39
  20.6 11.9 %collective-permute-done.4.refs_2_ = bf16[16,128,128]{2,1,0:T(8,128)(2,1)S(1)} collective-permute-done((bf16[16,128,128]{2,1,0:T(8,128)(2,1)S(1)}, bf16[16,128,128]{2,1,0:T(8,128)(2,1)S(1)}, u32[]{:S(2)}, u32[]{:S(2)}) %collective-permute-start.4) | collective-permute-done | bytes 524320 | tf_op jit(solution)/shard_map/ppermute | solution.py:39
  32.4 0.0 collective-permute-done.5.refs_3_
  32.4 0.4 own_states.2.own
  32.8 0.1 collective-permute-start.6
  32.9 1.3 %collective-permute-start.10 = (bf16[12,128,128]{2,1,0:T(8,128)(2,1)S(1)}, bf16[12,128,128]{2,1,0:T(8,128)(2,1)S(1)}, u32[]{:S(2)}, u32[]{:S(2)}) collective-permute-start(bf16[12,128,128]{2,1,0:T(8,128)(2,1)S(1)} %get-tuple-element.39), channel_id=1, source_target_pairs={{0,8},{8,0},{16,24},{24,16},{1,9},{9,1},{17,25},{25,17},{2,10},{10... | collective-permute-start | bytes 1179656 | tf_op jit(solution)/shard_map/ppermute | solution.py:39
  34.2 0.8 %collective-permute-start.11 = (bf16[12,128,128]{2,1,0:T(8,128)(2,1)S(1)}, bf16[12,128,128]{2,1,0:T(8,128)(2,1)S(1)}, u32[]{:S(2)}, u32[]{:S(2)}) collective-permute-start(bf16[12,128,128]{2,1,0:T(8,128)(2,1)S(1)} %get-tuple-element.40), channel_id=1, source_target_pairs={{0,16},{8,24},{16,0},{24,8},{1,17},{9,25},{17,1},{25,9},{2,18},{10... | collective-permute-start | bytes 1179656 | tf_op jit(solution)/shard_map/ppermute | solution.py:39
  35.0 1.4 %collective-permute-start.12 = (bf16[12,128,128]{2,1,0:T(8,128)(2,1)S(1)}, bf16[12,128,128]{2,1,0:T(8,128)(2,1)S(1)}, u32[]{:S(2)}, u32[]{:S(2)}) collective-permute-start(bf16[12,128,128]{2,1,0:T(8,128)(2,1)S(1)} %get-tuple-element.41), channel_id=1, source_target_pairs={{0,24},{8,16},{16,8},{24,0},{1,25},{9,17},{17,9},{25,1},{2,26},{10... | collective-permute-start | bytes 1179656 | tf_op jit(solution)/shard_map/ppermute | solution.py:39
  36.5 0.1 chip_states.2
  36.6 1.6 %collective-permute-start.7 = (bf16[5,128,128]{2,1,0:T(8,128)(2,1)S(1)}, bf16[5,128,128]{2,1,0:T(8,128)(2,1)S(1)}, u32[]{:S(2)}, u32[]{:S(2)}) collective-permute-start(bf16[5,128,128]{2,1,0:T(8,128)(2,1)S(1)} %get-tuple-element.35), channel_id=1, source_target_pairs={{0,2},{1,3},{2,4},{3,5},{4,6},{5,7},{6,0},{7,1},{8,10},{9,11},{10,... | collective-permute-start | bytes 491528 | tf_op jit(solution)/shard_map/ppermute | solution.py:39
  38.2 2.6 %collective-permute-start.8 = (bf16[5,128,128]{2,1,0:T(8,128)(2,1)S(1)}, bf16[5,128,128]{2,1,0:T(8,128)(2,1)S(1)}, u32[]{:S(2)}, u32[]{:S(2)}) collective-permute-start(bf16[5,128,128]{2,1,0:T(8,128)(2,1)S(1)} %get-tuple-element.36), channel_id=1, source_target_pairs={{0,4},{1,5},{2,6},{3,7},{4,0},{5,1},{6,2},{7,3},{8,12},{9,13},{10,... | collective-permute-start | bytes 491528 | tf_op jit(solution)/shard_map/ppermute | solution.py:39
  40.8 4.1 %collective-permute-done.10.refs_1_ = bf16[12,128,128]{2,1,0:T(8,128)(2,1)S(1)} collective-permute-done((bf16[12,128,128]{2,1,0:T(8,128)(2,1)S(1)}, bf16[12,128,128]{2,1,0:T(8,128)(2,1)S(1)}, u32[]{:S(2)}, u32[]{:S(2)}) %collective-permute-start.10) | collective-permute-done | bytes 393248 | tf_op jit(solution)/shard_map/ppermute | solution.py:39
  44.9 3.6 %collective-permute-start.9 = (bf16[5,128,128]{2,1,0:T(8,128)(2,1)S(1)}, bf16[5,128,128]{2,1,0:T(8,128)(2,1)S(1)}, u32[]{:S(2)}, u32[]{:S(2)}) collective-permute-start(bf16[5,128,128]{2,1,0:T(8,128)(2,1)S(1)} %get-tuple-element.37), channel_id=1, source_target_pairs={{0,6},{1,7},{2,0},{3,1},{4,2},{5,3},{6,4},{7,5},{8,14},{9,15},{10,... | collective-permute-start | bytes 491528 | tf_op jit(solution)/shard_map/ppermute | solution.py:39
  48.5 3.7 %collective-permute-done.11.refs_2_ = bf16[12,128,128]{2,1,0:T(8,128)(2,1)S(1)} collective-permute-done((bf16[12,128,128]{2,1,0:T(8,128)(2,1)S(1)}, bf16[12,128,128]{2,1,0:T(8,128)(2,1)S(1)}, u32[]{:S(2)}, u32[]{:S(2)}) %collective-permute-start.11) | collective-permute-done | bytes 393248 | tf_op jit(solution)/shard_map/ppermute | solution.py:39
  52.2 1.6 %collective-permute-done.12.refs_3_ = bf16[12,128,128]{2,1,0:T(8,128)(2,1)S(1)} collective-permute-done((bf16[12,128,128]{2,1,0:T(8,128)(2,1)S(1)}, bf16[12,128,128]{2,1,0:T(8,128)(2,1)S(1)}, u32[]{:S(2)}, u32[]{:S(2)}) %collective-permute-start.12) | collective-permute-done | bytes 393248 | tf_op jit(solution)/shard_map/ppermute | solution.py:39
  53.9 0.4 own_states.3.own
  54.3 0.1 collective-permute-start.13
  54.4 1.1 %collective-permute-start = (bf16[8,128,128]{2,1,0:T(8,128)(2,1)S(1)}, bf16[8,128,128]{2,1,0:T(8,128)(2,1)S(1)}, u32[]{:S(2)}, u32[]{:S(2)}) collective-permute-start(bf16[8,128,128]{2,1,0:T(8,128)(2,1)S(1)} %get-tuple-element.28), channel_id=1, source_target_pairs={{0,8},{8,0},{16,24},{24,16},{1,9},{9,1},{17,25},{25,17},{2,10},{10... | collective-permute-start | bytes 786440 | tf_op jit(solution)/shard_map/ppermute | solution.py:39
  55.4 1.3 %collective-permute-start.1 = (bf16[8,128,128]{2,1,0:T(8,128)(2,1)S(1)}, bf16[8,128,128]{2,1,0:T(8,128)(2,1)S(1)}, u32[]{:S(2)}, u32[]{:S(2)}) collective-permute-start(bf16[8,128,128]{2,1,0:T(8,128)(2,1)S(1)} %get-tuple-element.29), channel_id=1, source_target_pairs={{0,16},{8,24},{16,0},{24,8},{1,17},{9,25},{17,1},{25,9},{2,18},{10... | collective-permute-start | bytes 786440 | tf_op jit(solution)/shard_map/ppermute | solution.py:39
  56.7 0.1 chip_states.3
  56.8 1.6 %collective-permute-start.14 = (bf16[3,128,128]{2,1,0:T(8,128)(2,1)S(1)}, bf16[3,128,128]{2,1,0:T(8,128)(2,1)S(1)}, u32[]{:S(2)}, u32[]{:S(2)}) collective-permute-start(bf16[3,128,128]{2,1,0:T(8,128)(2,1)S(1)} %get-tuple-element.42), channel_id=1, source_target_pairs={{0,2},{1,3},{2,4},{3,5},{4,6},{5,7},{6,0},{7,1},{8,10},{9,11},{10,... | collective-permute-start | bytes 294920 | tf_op jit(solution)/shard_map/ppermute | solution.py:39
  58.4 2.6 %collective-permute-start.15 = (bf16[3,128,128]{2,1,0:T(8,128)(2,1)S(1)}, bf16[3,128,128]{2,1,0:T(8,128)(2,1)S(1)}, u32[]{:S(2)}, u32[]{:S(2)}) collective-permute-start(bf16[3,128,128]{2,1,0:T(8,128)(2,1)S(1)} %get-tuple-element.43), channel_id=1, source_target_pairs={{0,4},{1,5},{2,6},{3,7},{4,0},{5,1},{6,2},{7,3},{8,12},{9,13},{10,... | collective-permute-start | bytes 294920 | tf_op jit(solution)/shard_map/ppermute | solution.py:39
  61.0 1.3 %collective-permute-start.16 = (bf16[3,128,128]{2,1,0:T(8,128)(2,1)S(1)}, bf16[3,128,128]{2,1,0:T(8,128)(2,1)S(1)}, u32[]{:S(2)}, u32[]{:S(2)}) collective-permute-start(bf16[3,128,128]{2,1,0:T(8,128)(2,1)S(1)} %get-tuple-element.44), channel_id=1, source_target_pairs={{0,6},{1,7},{2,0},{3,1},{4,2},{5,3},{6,4},{7,5},{8,14},{9,15},{10,... | collective-permute-start | bytes 294920 | tf_op jit(solution)/shard_map/ppermute | solution.py:39
  62.4 4.9 %gradients.3 = (bf16[1,512,1024]{2,1,0:T(8,128)(2,1)}, bf16[1,512,1024]{2,1,0:T(8,128)(2,1)}, bf16[1,512,1024]{2,1,0:T(8,128)(2,1)}) custom-call(bf16[16,128,128]{2,1,0:T(8,128)(2,1)S(1)} %get-tuple-element.31.refs_0_, bf16[16,128,128]{2,1,0:T(8,128)(2,1)S(1)} %collective-permute-done.3.refs_1_, bf16[16,128,128]{2,1,0:T(8,128)(2,1)S(1)} %collective-permute-done.4.refs_2_, ...), custom_call_target="tpu_custom_call" | custom-call | flops 10000000000 | bytes 2752512 | tf_op jit(solution)/shard_map/gradients/pallas_call | solution.py:254
  67.3 1.2 %collective-permute-start.2 = (bf16[8,128,128]{2,1,0:T(8,128)(2,1)S(1)}, bf16[8,128,128]{2,1,0:T(8,128)(2,1)S(1)}, u32[]{:S(2)}, u32[]{:S(2)}) collective-permute-start(bf16[8,128,128]{2,1,0:T(8,128)(2,1)S(1)} %get-tuple-element.30), channel_id=1, source_target_pairs={{0,24},{8,16},{16,8},{24,0},{1,25},{9,17},{17,9},{25,1},{2,26},{10... | collective-permute-start | bytes 786440 | tf_op jit(solution)/shard_map/ppermute | solution.py:39
  68.5 4.9 %gradients.4 = (bf16[1,512,1024]{2,1,0:T(8,128)(2,1)}, bf16[1,512,1024]{2,1,0:T(8,128)(2,1)}, bf16[1,512,1024]{2,1,0:T(8,128)(2,1)}) custom-call(bf16[12,128,128]{2,1,0:T(8,128)(2,1)S(1)} %get-tuple-element.38.refs_0_, bf16[12,128,128]{2,1,0:T(8,128)(2,1)S(1)} %collective-permute-done.10.refs_1_, ...), custom_call_target="tpu_custom_call", output_to_operand_aliasing={{0}: (8, {}), {1}: (9, {}), {2}: (10, {})} | custom-call | flops 10000000000 | bytes 2752512 | tf_op jit(solution)/shard_map/gradients/pallas_call | solution.py:254
  73.4 2.1 %collective-permute-done.2.refs_3_ = bf16[8,128,128]{2,1,0:T(8,128)(2,1)S(1)} collective-permute-done((bf16[8,128,128]{2,1,0:T(8,128)(2,1)S(1)}, bf16[8,128,128]{2,1,0:T(8,128)(2,1)S(1)}, u32[]{:S(2)}, u32[]{:S(2)}) %collective-permute-start.2) | collective-permute-done | bytes 262176 | tf_op jit(solution)/shard_map/ppermute | solution.py:39
  75.4 3.5 %gradients.5 = (bf16[1,512,1024]{2,1,0:T(8,128)(2,1)}, bf16[1,512,1024]{2,1,0:T(8,128)(2,1)}, bf16[1,512,1024]{2,1,0:T(8,128)(2,1)}) custom-call(bf16[8,128,128]{2,1,0:T(8,128)(2,1)S(1)} %get-tuple-element.27.refs_0_, bf16[8,128,128]{2,1,0:T(8,128)(2,1)S(1)} %collective-permute-done.refs_1_, ...), custom_call_target="tpu_custom_call", output_to_operand_aliasing={{0}: (8, {}), {1}: (9, {}), {2}: (10, {})} | custom-call | flops 10000000000 | bytes 1835008 | tf_op jit(solution)/shard_map/gradients/pallas_call | solution.py:254
  (10 shorter events, 0.0 us)
Async XLA Ops:
  4.8 15.8 %collective-permute-start.3 = (bf16[16,128,128]{2,1,0:T(8,128)(2,1)S(1)}, bf16[16,128,128]{2,1,0:T(8,128)(2,1)S(1)}, u32[]{:S(2)}, u32[]{:S(2)}) collective-permute-start(bf16[16,128,128]{2,1,0:T(8,128)(2,1)S(1)} %get-tuple-element.32), channel_id=1, source_target_pairs={{0,8},{8,0},{16,24},{24,16},{1,9},{9,1},{17,25},{25,17},{2,10},{10... | collective-permute-start | bytes 1572872 | tf_op jit(solution)/shard_map/ppermute | solution.py:39
  7.8 24.6 %collective-permute-start.4 = (bf16[16,128,128]{2,1,0:T(8,128)(2,1)S(1)}, bf16[16,128,128]{2,1,0:T(8,128)(2,1)S(1)}, u32[]{:S(2)}, u32[]{:S(2)}) collective-permute-start(bf16[16,128,128]{2,1,0:T(8,128)(2,1)S(1)} %get-tuple-element.33), channel_id=1, source_target_pairs={{0,16},{8,24},{16,0},{24,8},{1,17},{9,25},{17,1},{25,9},{2,18},{10... | collective-permute-start | bytes 1572872 | tf_op jit(solution)/shard_map/ppermute | solution.py:39
  9.3 23.1 %collective-permute-start.5 = (bf16[16,128,128]{2,1,0:T(8,128)(2,1)S(1)}, bf16[16,128,128]{2,1,0:T(8,128)(2,1)S(1)}, u32[]{:S(2)}, u32[]{:S(2)}) collective-permute-start(bf16[16,128,128]{2,1,0:T(8,128)(2,1)S(1)} %get-tuple-element.34), channel_id=1, source_target_pairs={{0,24},{8,16},{16,8},{24,0},{1,25},{9,17},{17,9},{25,1},{2,26},{10... | collective-permute-start | bytes 1572872 | tf_op jit(solution)/shard_map/ppermute | solution.py:39
  32.8 3.6 %collective-permute-start.6 = (f32[2,5,128,128]{3,2,1,0:T(8,128)S(1)}, f32[2,5,128,128]{3,2,1,0:T(8,128)S(1)}, u32[]{:S(2)}, u32[]{:S(2)}) collective-permute-start(f32[2,5,128,128]{3,2,1,0:T(8,128)S(1)} %own_states.2.own), channel_id=1, source_target_pairs={{0,1},{1,0},{2,3},{3,2},{4,5},{5,4},{6,7},{7,6},{8,9},{9,8},{10,11... | collective-permute-start | bytes 1966088 | tf_op jit(solution)/shard_map/ppermute | solution.py:39
  32.9 12.0 %collective-permute-start.10 = (bf16[12,128,128]{2,1,0:T(8,128)(2,1)S(1)}, bf16[12,128,128]{2,1,0:T(8,128)(2,1)S(1)}, u32[]{:S(2)}, u32[]{:S(2)}) collective-permute-start(bf16[12,128,128]{2,1,0:T(8,128)(2,1)S(1)} %get-tuple-element.39), channel_id=1, source_target_pairs={{0,8},{8,0},{16,24},{24,16},{1,9},{9,1},{17,25},{25,17},{2,10},{10... | collective-permute-start | bytes 1179656 | tf_op jit(solution)/shard_map/ppermute | solution.py:39
  34.2 18.0 %collective-permute-start.11 = (bf16[12,128,128]{2,1,0:T(8,128)(2,1)S(1)}, bf16[12,128,128]{2,1,0:T(8,128)(2,1)S(1)}, u32[]{:S(2)}, u32[]{:S(2)}) collective-permute-start(bf16[12,128,128]{2,1,0:T(8,128)(2,1)S(1)} %get-tuple-element.40), channel_id=1, source_target_pairs={{0,16},{8,24},{16,0},{24,8},{1,17},{9,25},{17,1},{25,9},{2,18},{10... | collective-permute-start | bytes 1179656 | tf_op jit(solution)/shard_map/ppermute | solution.py:39
  35.0 18.8 %collective-permute-start.12 = (bf16[12,128,128]{2,1,0:T(8,128)(2,1)S(1)}, bf16[12,128,128]{2,1,0:T(8,128)(2,1)S(1)}, u32[]{:S(2)}, u32[]{:S(2)}) collective-permute-start(bf16[12,128,128]{2,1,0:T(8,128)(2,1)S(1)} %get-tuple-element.41), channel_id=1, source_target_pairs={{0,24},{8,16},{16,8},{24,0},{1,25},{9,17},{17,9},{25,1},{2,26},{10... | collective-permute-start | bytes 1179656 | tf_op jit(solution)/shard_map/ppermute | solution.py:39
  36.6 17.2 %collective-permute-start.7 = (bf16[5,128,128]{2,1,0:T(8,128)(2,1)S(1)}, bf16[5,128,128]{2,1,0:T(8,128)(2,1)S(1)}, u32[]{:S(2)}, u32[]{:S(2)}) collective-permute-start(bf16[5,128,128]{2,1,0:T(8,128)(2,1)S(1)} %get-tuple-element.35), channel_id=1, source_target_pairs={{0,2},{1,3},{2,4},{3,5},{4,6},{5,7},{6,0},{7,1},{8,10},{9,11},{10,... | collective-permute-start | bytes 491528 | tf_op jit(solution)/shard_map/ppermute | solution.py:39
  38.2 15.6 %collective-permute-start.8 = (bf16[5,128,128]{2,1,0:T(8,128)(2,1)S(1)}, bf16[5,128,128]{2,1,0:T(8,128)(2,1)S(1)}, u32[]{:S(2)}, u32[]{:S(2)}) collective-permute-start(bf16[5,128,128]{2,1,0:T(8,128)(2,1)S(1)} %get-tuple-element.36), channel_id=1, source_target_pairs={{0,4},{1,5},{2,6},{3,7},{4,0},{5,1},{6,2},{7,3},{8,12},{9,13},{10,... | collective-permute-start | bytes 491528 | tf_op jit(solution)/shard_map/ppermute | solution.py:39
  44.9 8.9 %collective-permute-start.9 = (bf16[5,128,128]{2,1,0:T(8,128)(2,1)S(1)}, bf16[5,128,128]{2,1,0:T(8,128)(2,1)S(1)}, u32[]{:S(2)}, u32[]{:S(2)}) collective-permute-start(bf16[5,128,128]{2,1,0:T(8,128)(2,1)S(1)} %get-tuple-element.37), channel_id=1, source_target_pairs={{0,6},{1,7},{2,0},{3,1},{4,2},{5,3},{6,4},{7,5},{8,14},{9,15},{10,... | collective-permute-start | bytes 491528 | tf_op jit(solution)/shard_map/ppermute | solution.py:39
  54.3 2.5 %collective-permute-start.13 = (f32[2,3,128,128]{3,2,1,0:T(8,128)S(1)}, f32[2,3,128,128]{3,2,1,0:T(8,128)S(1)}, u32[]{:S(2)}, u32[]{:S(2)}) collective-permute-start(f32[2,3,128,128]{3,2,1,0:T(8,128)S(1)} %own_states.3.own), channel_id=1, source_target_pairs={{0,1},{1,0},{2,3},{3,2},{4,5},{5,4},{6,7},{7,6},{8,9},{9,8},{10,11... | collective-permute-start | bytes 1179656 | tf_op jit(solution)/shard_map/ppermute | solution.py:39
  54.4 19.0 %collective-permute-start = (bf16[8,128,128]{2,1,0:T(8,128)(2,1)S(1)}, bf16[8,128,128]{2,1,0:T(8,128)(2,1)S(1)}, u32[]{:S(2)}, u32[]{:S(2)}) collective-permute-start(bf16[8,128,128]{2,1,0:T(8,128)(2,1)S(1)} %get-tuple-element.28), channel_id=1, source_target_pairs={{0,8},{8,0},{16,24},{24,16},{1,9},{9,1},{17,25},{25,17},{2,10},{10... | collective-permute-start | bytes 786440 | tf_op jit(solution)/shard_map/ppermute | solution.py:39
  55.4 17.9 %collective-permute-start.1 = (bf16[8,128,128]{2,1,0:T(8,128)(2,1)S(1)}, bf16[8,128,128]{2,1,0:T(8,128)(2,1)S(1)}, u32[]{:S(2)}, u32[]{:S(2)}) collective-permute-start(bf16[8,128,128]{2,1,0:T(8,128)(2,1)S(1)} %get-tuple-element.29), channel_id=1, source_target_pairs={{0,16},{8,24},{16,0},{24,8},{1,17},{9,25},{17,1},{25,9},{2,18},{10... | collective-permute-start | bytes 786440 | tf_op jit(solution)/shard_map/ppermute | solution.py:39
  56.8 10.5 %collective-permute-start.14 = (bf16[3,128,128]{2,1,0:T(8,128)(2,1)S(1)}, bf16[3,128,128]{2,1,0:T(8,128)(2,1)S(1)}, u32[]{:S(2)}, u32[]{:S(2)}) collective-permute-start(bf16[3,128,128]{2,1,0:T(8,128)(2,1)S(1)} %get-tuple-element.42), channel_id=1, source_target_pairs={{0,2},{1,3},{2,4},{3,5},{4,6},{5,7},{6,0},{7,1},{8,10},{9,11},{10,... | collective-permute-start | bytes 294920 | tf_op jit(solution)/shard_map/ppermute | solution.py:39
  58.4 10.0 %collective-permute-start.15 = (bf16[3,128,128]{2,1,0:T(8,128)(2,1)S(1)}, bf16[3,128,128]{2,1,0:T(8,128)(2,1)S(1)}, u32[]{:S(2)}, u32[]{:S(2)}) collective-permute-start(bf16[3,128,128]{2,1,0:T(8,128)(2,1)S(1)} %get-tuple-element.43), channel_id=1, source_target_pairs={{0,4},{1,5},{2,6},{3,7},{4,0},{5,1},{6,2},{7,3},{8,12},{9,13},{10,... | collective-permute-start | bytes 294920 | tf_op jit(solution)/shard_map/ppermute | solution.py:39
  61.0 7.4 %collective-permute-start.16 = (bf16[3,128,128]{2,1,0:T(8,128)(2,1)S(1)}, bf16[3,128,128]{2,1,0:T(8,128)(2,1)S(1)}, u32[]{:S(2)}, u32[]{:S(2)}) collective-permute-start(bf16[3,128,128]{2,1,0:T(8,128)(2,1)S(1)} %get-tuple-element.44), channel_id=1, source_target_pairs={{0,6},{1,7},{2,0},{3,1},{4,2},{5,3},{6,4},{7,5},{8,14},{9,15},{10,... | collective-permute-start | bytes 294920 | tf_op jit(solution)/shard_map/ppermute | solution.py:39
  67.3 8.2 %collective-permute-start.2 = (bf16[8,128,128]{2,1,0:T(8,128)(2,1)S(1)}, bf16[8,128,128]{2,1,0:T(8,128)(2,1)S(1)}, u32[]{:S(2)}, u32[]{:S(2)}) collective-permute-start(bf16[8,128,128]{2,1,0:T(8,128)(2,1)S(1)} %get-tuple-element.30), channel_id=1, source_target_pairs={{0,24},{8,16},{16,8},{24,0},{1,25},{9,17},{17,9},{25,1},{2,26},{10... | collective-permute-start | bytes 786440 | tf_op jit(solution)/shard_map/ppermute | solution.py:39

commit v2 on v1

v2 whole, which is shorter than its diff:
```python
import functools

import jax
import jax.numpy as jnp
from jax import lax
from jax.experimental import pallas as pl
from jax.experimental.pallas import tpu as pltpu
from jax.sharding import PartitionSpec as P

HD = 128
TILE = 256
F32 = jnp.float32
BF16 = jnp.bfloat16
PARAMS = pltpu.CompilerParams(vmem_limit_bytes=40 * 1024 * 1024)


def dot(a, b, contract):
    return lax.dot_general(a, b, ((contract[:1], contract[1:]), ((), ())), preferred_element_type=F32)


def in_hbm(arrays):
    return [pltpu.with_memory_space_constraint(value, pltpu.HBM) for value in arrays]


def cost(flops, count):
    return pl.CostEstimate(flops=flops, bytes_accessed=2 * count, transcendentals=0)


def target_of(me, step, parts):
    if parts & (parts - 1) == 0:
        return me ^ step
    return (me + step) % parts


def source_of(me, step, parts):
    if parts & (parts - 1) == 0:
        return me ^ step
    return (me + parts - step) % parts


def send(value, axis, target):
    count = lax.axis_size(axis)
    return lax.ppermute(value, axis, [(index, target(index)) for index in range(count)])


def copy_heads(inputs, parts, heads, step, head, count, target, at, sem):
    column = (target_of(lax.axis_index("head"), step, parts) * heads + head) * HD
    return [
        pltpu.make_async_copy(
            inputs[tensor].at[0, :, pl.ds(pl.multiple_of(column + index * HD, HD), HD)],
            target.at[at + 4 * index + tensor],
            sem,
        )
        for index in range(count)
        for tensor in range(4)
    ]


def first_kernel(parts, heads, count, late, *refs):
    inputs, outputs, (loaded, load_sem, copy_sem) = refs[:4], refs[4 : 3 + parts], refs[-3:]
    steps = range(1, parts)
    loads = [
        copy_heads(inputs, parts, heads, step, heads - late, late, loaded.at[step - 1], 0, load_sem.at[step - 1])
        for step in steps
    ]
    copies = [
        copy_heads(inputs, parts, heads, step, 0, count, outputs[step - 1], 0, copy_sem.at[step - 1])
        for step in steps
    ]
    for copy in sum(loads, []) + sum(copies, []):
        copy.start()
    for step in steps:
        for copy in loads[step - 1]:
            copy.wait()
        for index in range(late):
            query, keys, values, grads = (loaded[step - 1, 4 * index + tensor] for tensor in range(4))
            at = 4 * count + 2 * index
            outputs[step - 1][at] = dot(values, keys, (0, 0)).astype(BF16)
            outputs[step - 1][at + 1] = dot(query, grads, (0, 0)).astype(BF16)
    for copy in sum(copies, []):
        copy.wait()


@jax.named_scope("pack")
def pack_first(arrays, parts, heads, count, late):
    _, rows, full = arrays[0].shape
    units = 4 * count + 2 * late
    return pl.pallas_call(
        functools.partial(first_kernel, parts, heads, count, late),
        in_specs=[pl.BlockSpec(memory_space=pltpu.HBM)] * 4,
        out_specs=[pl.BlockSpec(memory_space=pltpu.VMEM)] * (parts - 1),
        out_shape=[jax.ShapeDtypeStruct((units, rows, HD), BF16)] * (parts - 1),
        scratch_shapes=[
            pltpu.VMEM((parts - 1, 4 * late, rows, HD), BF16),
            pltpu.SemaphoreType.DMA((parts - 1,)),
            pltpu.SemaphoreType.DMA((parts - 1,)),
        ],
        compiler_params=PARAMS,
        cost_estimate=cost(1000, 1024),
    )(*in_hbm(arrays))


def rest_kernel(parts, heads, chunks, *refs):
    inputs, outputs, (loaded, load_sem, copy_sem) = refs[:4], refs[4:-3], refs[-3:]
    late = chunks[-1]
    loads = copy_heads(inputs, parts, heads, 0, heads - late, late, loaded, 0, load_sem)
    copies, head = [], 0
    for chunk, count in enumerate(chunks):
        for step in range(parts):
            if chunk or not step:
                target = outputs[0] if not chunk else outputs[1 + (chunk - 1) * parts + step]
                copies += copy_heads(inputs, parts, heads, step, head, count, target, 0, copy_sem)
        head += count
    for copy in loads + copies:
        copy.start()
    for copy in loads:
        copy.wait()
    for index in range(late):
        query, keys, values, grads = (loaded[4 * index + tensor] for tensor in range(4))
        at = 4 * chunks[0] + 2 * index
        outputs[0][at] = dot(values, keys, (0, 0)).astype(BF16)
        outputs[0][at + 1] = dot(query, grads, (0, 0)).astype(BF16)
    for copy in copies:
        copy.wait()


@jax.named_scope("pack")
def pack_rest(arrays, parts, heads, chunks):
    _, rows, full = arrays[0].shape
    units = [4 * chunks[0] + 2 * chunks[-1]] + [4 * count for count in chunks[1:] for _ in range(parts)]
    flat = pl.pallas_call(
        functools.partial(rest_kernel, parts, heads, chunks),
        in_specs=[pl.BlockSpec(memory_space=pltpu.HBM)] * 4,
        out_specs=[pl.BlockSpec(memory_space=pltpu.VMEM)] * len(units),
        out_shape=[jax.ShapeDtypeStruct((unit, rows, HD), BF16) for unit in units],
        scratch_shapes=[
            pltpu.VMEM((4 * chunks[-1], rows, HD), BF16),
            pltpu.SemaphoreType.DMA,
            pltpu.SemaphoreType.DMA,
        ],
        compiler_params=PARAMS,
        cost_estimate=cost(1000, 1024),
    )(*in_hbm(arrays))
    return flat[0], [flat[1 + chunk * parts : 1 + (chunk + 1) * parts] for chunk in range(len(chunks) - 1)]


def state_kernel(parts, heads, extra, *refs):
    inputs, out = refs[:parts], refs[-1]
    for head in range(heads):
        query, keys, values, grads = (
            jnp.concatenate([ref[4 * head + tensor] for ref in inputs], 0) for tensor in range(4)
        )
        out[0, head] = dot(values, keys, (0, 0))
        out[1, head] = dot(query, grads, (0, 0))
    for late in range(extra):
        for state in range(2):
            at = 4 * heads + 2 * late + state
            out[state, heads + late] = sum(ref[at].astype(F32) for ref in inputs)


@jax.named_scope("own_states")
def own_states(received, heads, extra, before):
    parts = len(received)
    rows = received[0].shape[1]
    return pl.pallas_call(
        functools.partial(state_kernel, parts, heads, extra),
        in_specs=[pl.BlockSpec(memory_space=pltpu.VMEM)] * parts
        + [pl.BlockSpec(memory_space=pl.ANY)] * len(before),
        out_shape=jax.ShapeDtypeStruct((2, heads + extra, HD, HD), F32),
        compiler_params=PARAMS,
        cost_estimate=cost(1000, 1024),
    )(*received, *before)


def chip_kernel(chips, own, partner, *outputs):
    chip = lax.axis_index("ctx") // 2
    keys = (own[0] + partner[0]).astype(BF16)
    query = (own[1] + partner[1]).astype(BF16)
    for step in range(1, chips):
        outputs[step - 1][...] = jnp.where(chip + step < chips, keys, query)


@jax.named_scope("chip_states")
def chip_states(own, partner, chips):
    shape = own.shape[1:]
    return pl.pallas_call(
        functools.partial(chip_kernel, chips),
        out_shape=[jax.ShapeDtypeStruct(shape, BF16)] * (chips - 1),
        compiler_params=PARAMS,
        cost_estimate=cost(10**10, 1024),
    )(own, partner)


def other_states(own):
    spans = lax.axis_size("ctx")
    chips = spans // 2
    if spans % 2 or chips > 4:
        return [lax.all_gather(own.astype(BF16), "ctx")]
    partner = send(own, "ctx", lambda index: index ^ 1)
    sums = chip_states(own, partner, chips)
    return [partner] + [
        send(value, "ctx", lambda index: (index + 2 * step) % spans)
        for step, value in enumerate(sums, 1)
    ]


def read_states(refs, spans, head):
    me = lax.axis_index("ctx")
    zero = jnp.zeros((HD, HD), F32)
    if len(refs) == 1:

        def add(span, totals):
            keys, query = totals
            keys = keys + jnp.where(span < me, refs[0][span, 0, head].astype(F32), 0.0)
            query = query + jnp.where(span > me, refs[0][span, 1, head].astype(F32), 0.0)
            return keys, query

        return lax.fori_loop(0, spans, add, (zero, zero))
    partner, others = refs[0], refs[1:]
    chip, core = me // 2, me % 2
    keys = jnp.where(core == 1, partner[0, head], 0.0)
    query = jnp.where(core == 0, partner[1, head], 0.0)
    for step, ref in enumerate(others, 1):
        part = ref[head].astype(F32)
        keys = keys + jnp.where(chip >= step, part, 0.0)
        query = query + jnp.where(chip < step, part, 0.0)
    return keys, query


def grads_kernel(parts, spans, factor, offset, first, counts, *refs):
    received, states = refs[: counts[0]], refs[counts[0] : counts[0] + counts[1]]
    outputs, (ordered, staged, sem) = refs[-6:-3], refs[-3:]
    heads = ordered.shape[0]
    me = lax.axis_index("head")
    rows = received[0].shape[1]
    length = parts * rows
    tiles = length // TILE
    row = lax.broadcasted_iota(jnp.int32, (TILE, TILE), 0)
    column = lax.broadcasted_iota(jnp.int32, (TILE, TILE), 1)
    low, high = column <= row, row <= column

    def scores(a, b, keep):
        value = dot(a, b, (1, 1))
        if keep is not None:
            value = jnp.where(keep, value, 0.0)
        return value.astype(BF16)

    def total(lefts, rights):
        value = dot(jnp.concatenate(lefts, 1), jnp.concatenate(rights, 0), (1, 0))
        return (value * factor).astype(BF16)

    copies = []
    for head in range(heads):
        for step, ref in enumerate(received):
            place = source_of(me, step, parts)
            for tensor in range(4):
                ordered[head, tensor, place] = ref[4 * head + tensor]
        key_state, query_state = read_states(states, spans, head + offset)
        key_state = key_state.astype(BF16)
        query_turned = query_state.T.astype(BF16)
        query_state = query_state.astype(BF16)
        query, keys, values, grads = (
            ordered[head, tensor].reshape(tiles, TILE, HD) for tensor in range(4)
        )
        for i in range(tiles):
            at = slice(i * TILE, (i + 1) * TILE)
            before, after = range(i + 1), range(i, tiles)
            staged[head, 0, at] = total(
                [scores(grads[i], values[j], low if i == j else None) for j in before] + [grads[i]],
                [keys[j] for j in before] + [key_state],
            )
            staged[head, 1, at] = total(
                [scores(values[i], grads[j], high if i == j else None) for j in after] + [values[i]],
                [query[j] for j in after] + [query_turned],
            )
            staged[head, 2, at] = total(
                [scores(keys[i], query[j], high if i == j else None) for j in after] + [keys[i]],
                [grads[j] for j in after] + [query_state],
            )
        for index, out in enumerate(outputs):
            copies.append(
                pltpu.make_async_copy(
                    staged.at[head, index],
                    out.at[0, :, pl.ds((first + head) * HD, HD)],
                    sem.at[head, index],
                )
            )
            copies[-1].start()
    for copy in copies:
        copy.wait()


@jax.named_scope("gradients")
def gradients(received, states, offset, held, first, heads, group, factor):
    parts = len(received)
    rows = received[0].shape[1]
    spans = lax.axis_size("ctx")
    length = parts * rows
    kept = len(held)
    counts = (parts, len(states))
    return pl.pallas_call(
        functools.partial(grads_kernel, parts, spans, factor, offset, first, counts),
        in_specs=[pl.BlockSpec(memory_space=pltpu.VMEM)] * sum(counts)
        + [pl.BlockSpec(memory_space=pltpu.HBM)] * kept,
        out_specs=[pl.BlockSpec(memory_space=pltpu.HBM)] * 3,
        out_shape=[jax.ShapeDtypeStruct((1, length, group), BF16)] * 3,
        scratch_shapes=[
            pltpu.VMEM((heads, 4, parts, rows, HD), BF16),
            pltpu.VMEM((heads, 3, length, HD), BF16),
            pltpu.SemaphoreType.DMA((heads, 3)),
        ],
        input_output_aliases={sum(counts) + index: index for index in range(kept)},
        compiler_params=PARAMS,
        cost_estimate=cost(1000, 1024),
    )(*received, *states, *held)


def shards(query, keys, values, grad_out):
    parts = lax.axis_size("head")
    spans = lax.axis_size("ctx")
    _, rows, full = query.shape
    group = full // parts
    heads = group // HD
    factor = (HD * rows * parts * spans) ** -0.5
    late = max(1, heads // 4)
    middle = (heads - late) // 2
    chunks = [heads - late - middle, middle, late]
    arrays = (query, keys, values, grad_out)
    first = pack_first(arrays, parts, heads, chunks[0], late)
    own, packed = pack_rest(arrays, parts, heads, chunks)

    def exchange(own, values):
        moved = {
            step: send(value, "head", lambda index: target_of(index, step, parts))
            for step, value in list(enumerate(values, 1))[1:] + [(1, values[0])]
        }
        return [own] + [moved[step] for step in range(1, parts)]

    received = [exchange(own, first)] + [exchange(values[0], values[1:]) for values in packed]
    early = other_states(own_states(received[0], chunks[0], late, []))
    second = other_states(own_states(received[1], middle, 0, early[1:]))
    held = gradients(received[0], early, 0, (), 0, chunks[0], group, factor)
    held = gradients(received[1], second, 0, held, chunks[0], middle, group, factor)
    held = gradients(received[2], early, chunks[0], held, heads - late, late, group, factor)
    return tuple(held)


def solution(mesh):
    spec = P("ctx", "head", None)
    out = P("ctx", None, "head")
    return jax.shard_map(
        shards, mesh=mesh, in_specs=(spec,) * 4, out_specs=(out,) * 3, check_vma=False
    )
```

time: 79.1 us -> 77 us (0.973)
  Pallas kernels: 18.5 us -> 17.1 us
  waiting for transfers between devices: 34.6 us -> 33.6 us
    pallas_call x3, Pallas kernels: 13.3 us -> 12.1 us  [gradients(): pl.pallas_call(functools.partial(grads_kernel, parts, spans, factor, offs...]
    ppermute x17, waiting for transfers between devices: 34.6 us -> 33.6 us  [send(): lax.ppermute(value, axis, [(index, target(index)) for index in range(coun...]
    pallas_call x1 -> x2, Pallas kernels: 4.16 us -> 4 us  [the longest x1 2.15 us: pack_rest(): pl.pallas_call(functools.partial(rest_kernel, parts, heads, chunks), in_s...]
  transfers between devices with their start and end apart: 17 -> 17, of which waited for: 6 -> 6; matrix products, arithmetic and copies ran while one was open for 0% -> 0% of each run, Pallas kernels for 13% -> 14%
where the time goes in v2:
time: 77 us; the launch traced here: 76.7 us
  waiting for transfers between devices  33.6 us (44%)
  starting transfers between devices  25.1 us (33%)
  Pallas kernels  17.1 us (22%)
  between operations  0.91 us (1%)
    ppermute x17, waiting for transfers between devices, send(): lax.ppermute(value, axis, [(index, target(index)) for index in range(coun...  33.6 us
    ppermute x17, starting transfers between devices, send(): lax.ppermute(value, axis, [(index, target(index)) for index in range(coun...  25.1 us
    pallas_call x3, Pallas kernels, gradients(): pl.pallas_call(functools.partial(grads_kernel, parts, spans, factor, offs...  12.1 us
    pallas_call x1, Pallas kernels, pack_rest(): pl.pallas_call(functools.partial(rest_kernel, parts, heads, chunks), in_s...  2.15 us
    pallas_call x1, Pallas kernels, pack_first(): pl.pallas_call(functools.partial(first_kernel, parts, heads, count, late)...  1.85 us
  transfers between devices with their start and end apart: 17, of which 6 were waited for; matrix products, arithmetic and copies ran while one was open for 0% of the time, Pallas kernels for 14%

profile of v2, /device:TPU:0, one launch (start us, length us, event | category | flops | bytes accessed | tf_op | source)
XLA Modules:
  0.0 76.7 jit_solution(11659211854510449999)
XLA Ops:
  0.6 1.9 %pack.3 = (bf16[16,128,128]{2,1,0:T(8,128)(2,1)S(1)}, bf16[16,128,128]{2,1,0:T(8,128)(2,1)S(1)}, bf16[16,128,128]{2,1,0:T(8,128)(2,1)S(1)}) custom-call(bf16[1,128,4096]{2,1,0:T(8,128)(2,1)} %refs_0_.3, bf16[1,128,4096]{2,1,0:T(8,128)(2,1)} %refs_1_.3, bf16[1,128,4096]{2,1,0:T(8,128)(2,1)} %refs_2_.3, bf16[1,128,4096]{2,1,0:T(8,128)(2,1)} %refs_3_.3), custom_call_target="tpu_custom_call" | custom-call | flops 1000 | bytes 2048 | tf_op jit(solution)/shard_map/pack/pallas_call | solution.py:88
  2.5 3.0 %collective-permute-start.3 = (bf16[16,128,128]{2,1,0:T(8,128)(2,1)S(1)}, bf16[16,128,128]{2,1,0:T(8,128)(2,1)S(1)}, u32[]{:S(2)}, u32[]{:S(2)}) collective-permute-start(bf16[16,128,128]{2,1,0:T(8,128)(2,1)S(1)} %get-tuple-element.32), channel_id=1, source_target_pairs={{0,8},{8,0},{16,24},{24,16},{1,9},{9,1},{17,25},{25,17},{2,10},{10... | collective-permute-start | bytes 1572872 | tf_op jit(solution)/shard_map/ppermute | solution.py:43
  5.5 1.5 %collective-permute-start.4 = (bf16[16,128,128]{2,1,0:T(8,128)(2,1)S(1)}, bf16[16,128,128]{2,1,0:T(8,128)(2,1)S(1)}, u32[]{:S(2)}, u32[]{:S(2)}) collective-permute-start(bf16[16,128,128]{2,1,0:T(8,128)(2,1)S(1)} %get-tuple-element.33), channel_id=1, source_target_pairs={{0,16},{8,24},{16,0},{24,8},{1,17},{9,25},{17,1},{25,9},{2,18},{10... | collective-permute-start | bytes 1572872 | tf_op jit(solution)/shard_map/ppermute | solution.py:43
  7.0 0.0 collective-permute-start.5
  7.0 2.1 %pack.2 = (bf16[16,128,128]{2,1,0:T(8,128)(2,1)S(1)}, bf16[12,128,128]{2,1,0:T(8,128)(2,1)S(1)}, bf16[12,128,128]{2,1,0:T(8,128)(2,1)S(1)}, bf16[12,128,128]{2,1...) custom-call(bf16[1,128,4096]{2,1,0:T(8,128)(2,1)} %refs_0_.3, ...), custom_call_target="tpu_custom_call" | custom-call | flops 1000 | bytes 2048 | tf_op jit(solution)/shard_map/pack/pallas_call | solution.py:131
  9.2 9.1 %collective-permute-done.3.refs_1_ = bf16[16,128,128]{2,1,0:T(8,128)(2,1)S(1)} collective-permute-done((bf16[16,128,128]{2,1,0:T(8,128)(2,1)S(1)}, bf16[16,128,128]{2,1,0:T(8,128)(2,1)S(1)}, u32[]{:S(2)}, u32[]{:S(2)}) %collective-permute-start.3) | collective-permute-done | bytes 524320 | tf_op jit(solution)/shard_map/ppermute | solution.py:43
  18.2 11.9 %collective-permute-done.4.refs_2_ = bf16[16,128,128]{2,1,0:T(8,128)(2,1)S(1)} collective-permute-done((bf16[16,128,128]{2,1,0:T(8,128)(2,1)S(1)}, bf16[16,128,128]{2,1,0:T(8,128)(2,1)S(1)}, u32[]{:S(2)}, u32[]{:S(2)}) %collective-permute-start.4) | collective-permute-done | bytes 524320 | tf_op jit(solution)/shard_map/ppermute | solution.py:43
  30.1 0.4 own_states.2.own
  30.5 0.1 collective-permute-start.6
  30.6 1.3 %collective-permute-start.10 = (bf16[12,128,128]{2,1,0:T(8,128)(2,1)S(1)}, bf16[12,128,128]{2,1,0:T(8,128)(2,1)S(1)}, u32[]{:S(2)}, u32[]{:S(2)}) collective-permute-start(bf16[12,128,128]{2,1,0:T(8,128)(2,1)S(1)} %get-tuple-element.39), channel_id=1, source_target_pairs={{0,8},{8,0},{16,24},{24,16},{1,9},{9,1},{17,25},{25,17},{2,10},{10... | collective-permute-start | bytes 1179656 | tf_op jit(solution)/shard_map/ppermute | solution.py:43
  31.9 0.8 %collective-permute-start.11 = (bf16[12,128,128]{2,1,0:T(8,128)(2,1)S(1)}, bf16[12,128,128]{2,1,0:T(8,128)(2,1)S(1)}, u32[]{:S(2)}, u32[]{:S(2)}) collective-permute-start(bf16[12,128,128]{2,1,0:T(8,128)(2,1)S(1)} %get-tuple-element.40), channel_id=1, source_target_pairs={{0,16},{8,24},{16,0},{24,8},{1,17},{9,25},{17,1},{25,9},{2,18},{10... | collective-permute-start | bytes 1179656 | tf_op jit(solution)/shard_map/ppermute | solution.py:43
  32.7 1.4 %collective-permute-start.12 = (bf16[12,128,128]{2,1,0:T(8,128)(2,1)S(1)}, bf16[12,128,128]{2,1,0:T(8,128)(2,1)S(1)}, u32[]{:S(2)}, u32[]{:S(2)}) collective-permute-start(bf16[12,128,128]{2,1,0:T(8,128)(2,1)S(1)} %get-tuple-element.41), channel_id=1, source_target_pairs={{0,24},{8,16},{16,8},{24,0},{1,25},{9,17},{17,9},{25,1},{2,26},{10... | collective-permute-start | bytes 1179656 | tf_op jit(solution)/shard_map/ppermute | solution.py:43
  34.2 0.1 chip_states.2
  34.3 1.6 %collective-permute-start.7 = (bf16[5,128,128]{2,1,0:T(8,128)(2,1)S(1)}, bf16[5,128,128]{2,1,0:T(8,128)(2,1)S(1)}, u32[]{:S(2)}, u32[]{:S(2)}) collective-permute-start(bf16[5,128,128]{2,1,0:T(8,128)(2,1)S(1)} %get-tuple-element.35), channel_id=1, source_target_pairs={{0,2},{1,3},{2,4},{3,5},{4,6},{5,7},{6,0},{7,1},{8,10},{9,11},{10,... | collective-permute-start | bytes 491528 | tf_op jit(solution)/shard_map/ppermute | solution.py:43
  35.9 2.6 %collective-permute-start.8 = (bf16[5,128,128]{2,1,0:T(8,128)(2,1)S(1)}, bf16[5,128,128]{2,1,0:T(8,128)(2,1)S(1)}, u32[]{:S(2)}, u32[]{:S(2)}) collective-permute-start(bf16[5,128,128]{2,1,0:T(8,128)(2,1)S(1)} %get-tuple-element.36), channel_id=1, source_target_pairs={{0,4},{1,5},{2,6},{3,7},{4,0},{5,1},{6,2},{7,3},{8,12},{9,13},{10,... | collective-permute-start | bytes 491528 | tf_op jit(solution)/shard_map/ppermute | solution.py:43
  38.5 4.1 %collective-permute-done.10.refs_1_ = bf16[12,128,128]{2,1,0:T(8,128)(2,1)S(1)} collective-permute-done((bf16[12,128,128]{2,1,0:T(8,128)(2,1)S(1)}, bf16[12,128,128]{2,1,0:T(8,128)(2,1)S(1)}, u32[]{:S(2)}, u32[]{:S(2)}) %collective-permute-start.10) | collective-permute-done | bytes 393248 | tf_op jit(solution)/shard_map/ppermute | solution.py:43
  42.6 3.6 %collective-permute-start.9 = (bf16[5,128,128]{2,1,0:T(8,128)(2,1)S(1)}, bf16[5,128,128]{2,1,0:T(8,128)(2,1)S(1)}, u32[]{:S(2)}, u32[]{:S(2)}) collective-permute-start(bf16[5,128,128]{2,1,0:T(8,128)(2,1)S(1)} %get-tuple-element.37), channel_id=1, source_target_pairs={{0,6},{1,7},{2,0},{3,1},{4,2},{5,3},{6,4},{7,5},{8,14},{9,15},{10,... | collective-permute-start | bytes 491528 | tf_op jit(solution)/shard_map/ppermute | solution.py:43
  46.2 3.7 %collective-permute-done.11.refs_2_ = bf16[12,128,128]{2,1,0:T(8,128)(2,1)S(1)} collective-permute-done((bf16[12,128,128]{2,1,0:T(8,128)(2,1)S(1)}, bf16[12,128,128]{2,1,0:T(8,128)(2,1)S(1)}, u32[]{:S(2)}, u32[]{:S(2)}) %collective-permute-start.11) | collective-permute-done | bytes 393248 | tf_op jit(solution)/shard_map/ppermute | solution.py:43
  49.9 1.6 %collective-permute-done.12.refs_3_ = bf16[12,128,128]{2,1,0:T(8,128)(2,1)S(1)} collective-permute-done((bf16[12,128,128]{2,1,0:T(8,128)(2,1)S(1)}, bf16[12,128,128]{2,1,0:T(8,128)(2,1)S(1)}, u32[]{:S(2)}, u32[]{:S(2)}) %collective-permute-start.12) | collective-permute-done | bytes 393248 | tf_op jit(solution)/shard_map/ppermute | solution.py:43
  51.5 0.4 own_states.3.own
  52.0 0.1 collective-permute-start.13
  52.0 1.1 %collective-permute-start = (bf16[8,128,128]{2,1,0:T(8,128)(2,1)S(1)}, bf16[8,128,128]{2,1,0:T(8,128)(2,1)S(1)}, u32[]{:S(2)}, u32[]{:S(2)}) collective-permute-start(bf16[8,128,128]{2,1,0:T(8,128)(2,1)S(1)} %get-tuple-element.28), channel_id=1, source_target_pairs={{0,8},{8,0},{16,24},{24,16},{1,9},{9,1},{17,25},{25,17},{2,10},{10... | collective-permute-start | bytes 786440 | tf_op jit(solution)/shard_map/ppermute | solution.py:43
  53.1 1.3 %collective-permute-start.1 = (bf16[8,128,128]{2,1,0:T(8,128)(2,1)S(1)}, bf16[8,128,128]{2,1,0:T(8,128)(2,1)S(1)}, u32[]{:S(2)}, u32[]{:S(2)}) collective-permute-start(bf16[8,128,128]{2,1,0:T(8,128)(2,1)S(1)} %get-tuple-element.29), channel_id=1, source_target_pairs={{0,16},{8,24},{16,0},{24,8},{1,17},{9,25},{17,1},{25,9},{2,18},{10... | collective-permute-start | bytes 786440 | tf_op jit(solution)/shard_map/ppermute | solution.py:43
  54.4 1.2 %collective-permute-start.2 = (bf16[8,128,128]{2,1,0:T(8,128)(2,1)S(1)}, bf16[8,128,128]{2,1,0:T(8,128)(2,1)S(1)}, u32[]{:S(2)}, u32[]{:S(2)}) collective-permute-start(bf16[8,128,128]{2,1,0:T(8,128)(2,1)S(1)} %get-tuple-element.30), channel_id=1, source_target_pairs={{0,24},{8,16},{16,8},{24,0},{1,25},{9,17},{17,9},{25,1},{2,26},{10... | collective-permute-start | bytes 786440 | tf_op jit(solution)/shard_map/ppermute | solution.py:43
  55.6 0.1 chip_states.3
  55.7 1.6 %collective-permute-start.14 = (bf16[3,128,128]{2,1,0:T(8,128)(2,1)S(1)}, bf16[3,128,128]{2,1,0:T(8,128)(2,1)S(1)}, u32[]{:S(2)}, u32[]{:S(2)}) collective-permute-start(bf16[3,128,128]{2,1,0:T(8,128)(2,1)S(1)} %get-tuple-element.42), channel_id=1, source_target_pairs={{0,2},{1,3},{2,4},{3,5},{4,6},{5,7},{6,0},{7,1},{8,10},{9,11},{10,... | collective-permute-start | bytes 294920 | tf_op jit(solution)/shard_map/ppermute | solution.py:43
  57.3 2.6 %collective-permute-start.15 = (bf16[3,128,128]{2,1,0:T(8,128)(2,1)S(1)}, bf16[3,128,128]{2,1,0:T(8,128)(2,1)S(1)}, u32[]{:S(2)}, u32[]{:S(2)}) collective-permute-start(bf16[3,128,128]{2,1,0:T(8,128)(2,1)S(1)} %get-tuple-element.43), channel_id=1, source_target_pairs={{0,4},{1,5},{2,6},{3,7},{4,0},{5,1},{6,2},{7,3},{8,12},{9,13},{10,... | collective-permute-start | bytes 294920 | tf_op jit(solution)/shard_map/ppermute | solution.py:43
  59.9 3.3 %collective-permute-done.14.refs_5_ = bf16[3,128,128]{2,1,0:T(8,128)(2,1)S(1)} collective-permute-done((bf16[3,128,128]{2,1,0:T(8,128)(2,1)S(1)}, bf16[3,128,128]{2,1,0:T(8,128)(2,1)S(1)}, u32[]{:S(2)}, u32[]{:S(2)}) %collective-permute-start.14) | collective-permute-done | bytes 98336 | tf_op jit(solution)/shard_map/ppermute | solution.py:43
  63.1 1.2 %collective-permute-start.16 = (bf16[3,128,128]{2,1,0:T(8,128)(2,1)S(1)}, bf16[3,128,128]{2,1,0:T(8,128)(2,1)S(1)}, u32[]{:S(2)}, u32[]{:S(2)}) collective-permute-start(bf16[3,128,128]{2,1,0:T(8,128)(2,1)S(1)} %get-tuple-element.44), channel_id=1, source_target_pairs={{0,6},{1,7},{2,0},{3,1},{4,2},{5,3},{6,4},{7,5},{8,14},{9,15},{10,... | collective-permute-start | bytes 294920 | tf_op jit(solution)/shard_map/ppermute | solution.py:43
  64.4 4.4 %gradients.3 = (bf16[1,512,1024]{2,1,0:T(8,128)(2,1)}, bf16[1,512,1024]{2,1,0:T(8,128)(2,1)}, bf16[1,512,1024]{2,1,0:T(8,128)(2,1)}) custom-call(bf16[16,128,128]{2,1,0:T(8,128)(2,1)S(1)} %get-tuple-element.31.refs_0_, bf16[16,128,128]{2,1,0:T(8,128)(2,1)S(1)} %collective-permute-done.3.refs_1_, bf16[16,128,128]{2,1,0:T(8,128)(2,1)S(1)} %collective-permute-done.4.refs_2_, ...), custom_call_target="tpu_custom_call" | custom-call | flops 1000 | bytes 2048 | tf_op jit(solution)/shard_map/gradients/pallas_call | solution.py:301
  68.8 4.4 %gradients.4 = (bf16[1,512,1024]{2,1,0:T(8,128)(2,1)}, bf16[1,512,1024]{2,1,0:T(8,128)(2,1)}, bf16[1,512,1024]{2,1,0:T(8,128)(2,1)}) custom-call(bf16[12,128,128]{2,1,0:T(8,128)(2,1)S(1)} %get-tuple-element.38.refs_0_, bf16[12,128,128]{2,1,0:T(8,128)(2,1)S(1)} %collective-permute-done.10.refs_1_, ...), custom_call_target="tpu_custom_call", output_to_operand_aliasing={{0}: (8, {}), {1}: (9, {}), {2}: (10, {})} | custom-call | flops 1000 | bytes 2048 | tf_op jit(solution)/shard_map/gradients/pallas_call | solution.py:301
  73.2 3.3 %gradients.5 = (bf16[1,512,1024]{2,1,0:T(8,128)(2,1)}, bf16[1,512,1024]{2,1,0:T(8,128)(2,1)}, bf16[1,512,1024]{2,1,0:T(8,128)(2,1)}) custom-call(bf16[8,128,128]{2,1,0:T(8,128)(2,1)S(1)} %get-tuple-element.27.refs_0_, bf16[8,128,128]{2,1,0:T(8,128)(2,1)S(1)} %collective-permute-done.refs_1_, ...), custom_call_target="tpu_custom_call", output_to_operand_aliasing={{0}: (8, {}), {1}: (9, {}), {2}: (10, {})} | custom-call | flops 1000 | bytes 2048 | tf_op jit(solution)/shard_map/gradients/pallas_call | solution.py:301
  (11 shorter events, 0.0 us)
Async XLA Ops:
  2.5 15.8 %collective-permute-start.3 = (bf16[16,128,128]{2,1,0:T(8,128)(2,1)S(1)}, bf16[16,128,128]{2,1,0:T(8,128)(2,1)S(1)}, u32[]{:S(2)}, u32[]{:S(2)}) collective-permute-start(bf16[16,128,128]{2,1,0:T(8,128)(2,1)S(1)} %get-tuple-element.32), channel_id=1, source_target_pairs={{0,8},{8,0},{16,24},{24,16},{1,9},{9,1},{17,25},{25,17},{2,10},{10... | collective-permute-start | bytes 1572872 | tf_op jit(solution)/shard_map/ppermute | solution.py:43
  5.5 24.6 %collective-permute-start.4 = (bf16[16,128,128]{2,1,0:T(8,128)(2,1)S(1)}, bf16[16,128,128]{2,1,0:T(8,128)(2,1)S(1)}, u32[]{:S(2)}, u32[]{:S(2)}) collective-permute-start(bf16[16,128,128]{2,1,0:T(8,128)(2,1)S(1)} %get-tuple-element.33), channel_id=1, source_target_pairs={{0,16},{8,24},{16,0},{24,8},{1,17},{9,25},{17,1},{25,9},{2,18},{10... | collective-permute-start | bytes 1572872 | tf_op jit(solution)/shard_map/ppermute | solution.py:43
  7.0 23.1 %collective-permute-start.5 = (bf16[16,128,128]{2,1,0:T(8,128)(2,1)S(1)}, bf16[16,128,128]{2,1,0:T(8,128)(2,1)S(1)}, u32[]{:S(2)}, u32[]{:S(2)}) collective-permute-start(bf16[16,128,128]{2,1,0:T(8,128)(2,1)S(1)} %get-tuple-element.34), channel_id=1, source_target_pairs={{0,24},{8,16},{16,8},{24,0},{1,25},{9,17},{17,9},{25,1},{2,26},{10... | collective-permute-start | bytes 1572872 | tf_op jit(solution)/shard_map/ppermute | solution.py:43
  30.5 3.6 %collective-permute-start.6 = (f32[2,5,128,128]{3,2,1,0:T(8,128)S(1)}, f32[2,5,128,128]{3,2,1,0:T(8,128)S(1)}, u32[]{:S(2)}, u32[]{:S(2)}) collective-permute-start(f32[2,5,128,128]{3,2,1,0:T(8,128)S(1)} %own_states.2.own), channel_id=1, source_target_pairs={{0,1},{1,0},{2,3},{3,2},{4,5},{5,4},{6,7},{7,6},{8,9},{9,8},{10,11... | collective-permute-start | bytes 1966088 | tf_op jit(solution)/shard_map/ppermute | solution.py:43
  30.6 12.0 %collective-permute-start.10 = (bf16[12,128,128]{2,1,0:T(8,128)(2,1)S(1)}, bf16[12,128,128]{2,1,0:T(8,128)(2,1)S(1)}, u32[]{:S(2)}, u32[]{:S(2)}) collective-permute-start(bf16[12,128,128]{2,1,0:T(8,128)(2,1)S(1)} %get-tuple-element.39), channel_id=1, source_target_pairs={{0,8},{8,0},{16,24},{24,16},{1,9},{9,1},{17,25},{25,17},{2,10},{10... | collective-permute-start | bytes 1179656 | tf_op jit(solution)/shard_map/ppermute | solution.py:43
  31.9 18.0 %collective-permute-start.11 = (bf16[12,128,128]{2,1,0:T(8,128)(2,1)S(1)}, bf16[12,128,128]{2,1,0:T(8,128)(2,1)S(1)}, u32[]{:S(2)}, u32[]{:S(2)}) collective-permute-start(bf16[12,128,128]{2,1,0:T(8,128)(2,1)S(1)} %get-tuple-element.40), channel_id=1, source_target_pairs={{0,16},{8,24},{16,0},{24,8},{1,17},{9,25},{17,1},{25,9},{2,18},{10... | collective-permute-start | bytes 1179656 | tf_op jit(solution)/shard_map/ppermute | solution.py:43
  32.7 18.8 %collective-permute-start.12 = (bf16[12,128,128]{2,1,0:T(8,128)(2,1)S(1)}, bf16[12,128,128]{2,1,0:T(8,128)(2,1)S(1)}, u32[]{:S(2)}, u32[]{:S(2)}) collective-permute-start(bf16[12,128,128]{2,1,0:T(8,128)(2,1)S(1)} %get-tuple-element.41), channel_id=1, source_target_pairs={{0,24},{8,16},{16,8},{24,0},{1,25},{9,17},{17,9},{25,1},{2,26},{10... | collective-permute-start | bytes 1179656 | tf_op jit(solution)/shard_map/ppermute | solution.py:43
  34.3 17.2 %collective-permute-start.7 = (bf16[5,128,128]{2,1,0:T(8,128)(2,1)S(1)}, bf16[5,128,128]{2,1,0:T(8,128)(2,1)S(1)}, u32[]{:S(2)}, u32[]{:S(2)}) collective-permute-start(bf16[5,128,128]{2,1,0:T(8,128)(2,1)S(1)} %get-tuple-element.35), channel_id=1, source_target_pairs={{0,2},{1,3},{2,4},{3,5},{4,6},{5,7},{6,0},{7,1},{8,10},{9,11},{10,... | collective-permute-start | bytes 491528 | tf_op jit(solution)/shard_map/ppermute | solution.py:43
  35.9 15.6 %collective-permute-start.8 = (bf16[5,128,128]{2,1,0:T(8,128)(2,1)S(1)}, bf16[5,128,128]{2,1,0:T(8,128)(2,1)S(1)}, u32[]{:S(2)}, u32[]{:S(2)}) collective-permute-start(bf16[5,128,128]{2,1,0:T(8,128)(2,1)S(1)} %get-tuple-element.36), channel_id=1, source_target_pairs={{0,4},{1,5},{2,6},{3,7},{4,0},{5,1},{6,2},{7,3},{8,12},{9,13},{10,... | collective-permute-start | bytes 491528 | tf_op jit(solution)/shard_map/ppermute | solution.py:43
  42.6 8.9 %collective-permute-start.9 = (bf16[5,128,128]{2,1,0:T(8,128)(2,1)S(1)}, bf16[5,128,128]{2,1,0:T(8,128)(2,1)S(1)}, u32[]{:S(2)}, u32[]{:S(2)}) collective-permute-start(bf16[5,128,128]{2,1,0:T(8,128)(2,1)S(1)} %get-tuple-element.37), channel_id=1, source_target_pairs={{0,6},{1,7},{2,0},{3,1},{4,2},{5,3},{6,4},{7,5},{8,14},{9,15},{10,... | collective-permute-start | bytes 491528 | tf_op jit(solution)/shard_map/ppermute | solution.py:43
  52.0 3.6 %collective-permute-start.13 = (f32[2,3,128,128]{3,2,1,0:T(8,128)S(1)}, f32[2,3,128,128]{3,2,1,0:T(8,128)S(1)}, u32[]{:S(2)}, u32[]{:S(2)}) collective-permute-start(f32[2,3,128,128]{3,2,1,0:T(8,128)S(1)} %own_states.3.own), channel_id=1, source_target_pairs={{0,1},{1,0},{2,3},{3,2},{4,5},{5,4},{6,7},{7,6},{8,9},{9,8},{10,11... | collective-permute-start | bytes 1179656 | tf_op jit(solution)/shard_map/ppermute | solution.py:43
  52.0 21.1 %collective-permute-start = (bf16[8,128,128]{2,1,0:T(8,128)(2,1)S(1)}, bf16[8,128,128]{2,1,0:T(8,128)(2,1)S(1)}, u32[]{:S(2)}, u32[]{:S(2)}) collective-permute-start(bf16[8,128,128]{2,1,0:T(8,128)(2,1)S(1)} %get-tuple-element.28), channel_id=1, source_target_pairs={{0,8},{8,0},{16,24},{24,16},{1,9},{9,1},{17,25},{25,17},{2,10},{10... | collective-permute-start | bytes 786440 | tf_op jit(solution)/shard_map/ppermute | solution.py:43
  53.1 20.1 %collective-permute-start.1 = (bf16[8,128,128]{2,1,0:T(8,128)(2,1)S(1)}, bf16[8,128,128]{2,1,0:T(8,128)(2,1)S(1)}, u32[]{:S(2)}, u32[]{:S(2)}) collective-permute-start(bf16[8,128,128]{2,1,0:T(8,128)(2,1)S(1)} %get-tuple-element.29), channel_id=1, source_target_pairs={{0,16},{8,24},{16,0},{24,8},{1,17},{9,25},{17,1},{25,9},{2,18},{10... | collective-permute-start | bytes 786440 | tf_op jit(solution)/shard_map/ppermute | solution.py:43
  54.4 18.8 %collective-permute-start.2 = (bf16[8,128,128]{2,1,0:T(8,128)(2,1)S(1)}, bf16[8,128,128]{2,1,0:T(8,128)(2,1)S(1)}, u32[]{:S(2)}, u32[]{:S(2)}) collective-permute-start(bf16[8,128,128]{2,1,0:T(8,128)(2,1)S(1)} %get-tuple-element.30), channel_id=1, source_target_pairs={{0,24},{8,16},{16,8},{24,0},{1,25},{9,17},{17,9},{25,1},{2,26},{10... | collective-permute-start | bytes 786440 | tf_op jit(solution)/shard_map/ppermute | solution.py:43
  55.7 7.5 %collective-permute-start.14 = (bf16[3,128,128]{2,1,0:T(8,128)(2,1)S(1)}, bf16[3,128,128]{2,1,0:T(8,128)(2,1)S(1)}, u32[]{:S(2)}, u32[]{:S(2)}) collective-permute-start(bf16[3,128,128]{2,1,0:T(8,128)(2,1)S(1)} %get-tuple-element.42), channel_id=1, source_target_pairs={{0,2},{1,3},{2,4},{3,5},{4,6},{5,7},{6,0},{7,1},{8,10},{9,11},{10,... | collective-permute-start | bytes 294920 | tf_op jit(solution)/shard_map/ppermute | solution.py:43
  57.3 11.5 %collective-permute-start.15 = (bf16[3,128,128]{2,1,0:T(8,128)(2,1)S(1)}, bf16[3,128,128]{2,1,0:T(8,128)(2,1)S(1)}, u32[]{:S(2)}, u32[]{:S(2)}) collective-permute-start(bf16[3,128,128]{2,1,0:T(8,128)(2,1)S(1)} %get-tuple-element.43), channel_id=1, source_target_pairs={{0,4},{1,5},{2,6},{3,7},{4,0},{5,1},{6,2},{7,3},{8,12},{9,13},{10,... | collective-permute-start | bytes 294920 | tf_op jit(solution)/shard_map/ppermute | solution.py:43
  63.1 5.6 %collective-permute-start.16 = (bf16[3,128,128]{2,1,0:T(8,128)(2,1)S(1)}, bf16[3,128,128]{2,1,0:T(8,128)(2,1)S(1)}, u32[]{:S(2)}, u32[]{:S(2)}) collective-permute-start(bf16[3,128,128]{2,1,0:T(8,128)(2,1)S(1)} %get-tuple-element.44), channel_id=1, source_target_pairs={{0,6},{1,7},{2,0},{3,1},{4,2},{5,3},{6,4},{7,5},{8,14},{9,15},{10,... | collective-permute-start | bytes 294920 | tf_op jit(solution)/shard_map/ppermute | solution.py:43

commit v3 on v2

--- a/solution.py
+++ b/solution.py
@@ -36,6 +36,10 @@
     if parts & (parts - 1) == 0:
         return me ^ step
     return (me + parts - step) % parts
+
+
+def steps_of(parts):
+    return [0] + list(range(2, parts)) + [1]
 
 
 def send(value, axis, target):
@@ -145,17 +149,19 @@
 
 
 def state_kernel(parts, heads, extra, *refs):
-    inputs, out = refs[:parts], refs[-1]
+    inputs, (out, give) = refs[:parts], refs[-2:]
     for head in range(heads):
         query, keys, values, grads = (
             jnp.concatenate([ref[4 * head + tensor] for ref in inputs], 0) for tensor in range(4)
         )
         out[0, head] = dot(values, keys, (0, 0))
         out[1, head] = dot(query, grads, (0, 0))
+        give[:, head] = out[:, head].astype(BF16)
     for late in range(extra):
         for state in range(2):
             at = 4 * heads + 2 * late + state
             out[state, heads + late] = sum(ref[at].astype(F32) for ref in inputs)
+        give[:, heads + late] = out[:, heads + late].astype(BF16)
 
 
 @jax.named_scope("own_states")
@@ -166,7 +172,7 @@
         functools.partial(state_kernel, parts, heads, extra),
         in_specs=[pl.BlockSpec(memory_space=pltpu.VMEM)] * parts
         + [pl.BlockSpec(memory_space=pl.ANY)] * len(before),
-        out_shape=jax.ShapeDtypeStruct((2, heads + extra, HD, HD), F32),
+        out_shape=[jax.ShapeDtypeStruct((2, heads + extra, HD, HD), kind) for kind in (F32, BF16)],
         compiler_params=PARAMS,
         cost_estimate=cost(1000, 1024),
     )(*received, *before)
@@ -187,16 +193,16 @@
         functools.partial(chip_kernel, chips),
         out_shape=[jax.ShapeDtypeStruct(shape, BF16)] * (chips - 1),
         compiler_params=PARAMS,
-        cost_estimate=cost(10**10, 1024),
+        cost_estimate=cost(1000, 1024),
     )(own, partner)
 
 
-def other_states(own):
+def other_states(own, give):
     spans = lax.axis_size("ctx")
     chips = spans // 2
     if spans % 2 or chips > 4:
-        return [lax.all_gather(own.astype(BF16), "ctx")]
-    partner = send(own, "ctx", lambda index: index ^ 1)
+        return [lax.all_gather(give, "ctx")]
+    partner = send(give, "ctx", lambda index: index ^ 1)
     sums = chip_states(own, partner, chips)
     return [partner] + [
         send(value, "ctx", lambda index: (index + 2 * step) % spans)
@@ -218,8 +224,8 @@
         return lax.fori_loop(0, spans, add, (zero, zero))
     partner, others = refs[0], refs[1:]
     chip, core = me // 2, me % 2
-    keys = jnp.where(core == 1, partner[0, head], 0.0)
-    query = jnp.where(core == 0, partner[1, head], 0.0)
+    keys = jnp.where(core == 1, partner[0, head].astype(F32), 0.0)
+    query = jnp.where(core == 0, partner[1, head].astype(F32), 0.0)
     for step, ref in enumerate(others, 1):
         part = ref[head].astype(F32)
         keys = keys + jnp.where(chip >= step, part, 0.0)
@@ -229,7 +235,7 @@
 
 def grads_kernel(parts, spans, factor, offset, first, counts, *refs):
     received, states = refs[: counts[0]], refs[counts[0] : counts[0] + counts[1]]
-    outputs, (ordered, staged, sem) = refs[-6:-3], refs[-3:]
+    outputs, token, (ordered, staged, sem) = refs[-7:-4], refs[-4], refs[-3:]
     heads = ordered.shape[0]
     me = lax.axis_index("head")
     rows = received[0].shape[1]
@@ -251,7 +257,7 @@
 
     copies = []
     for head in range(heads):
-        for step, ref in enumerate(received):
+        for step, ref in zip(steps_of(parts), received):
             place = source_of(me, step, parts)
             for tensor in range(4):
                 ordered[head, tensor, place] = ref[4 * head + tensor]
@@ -288,22 +294,23 @@
             copies[-1].start()
     for copy in copies:
         copy.wait()
+    token[...] = jnp.zeros_like(token)
 
 
 @jax.named_scope("gradients")
 def gradients(received, states, offset, held, first, heads, group, factor):
     parts = len(received)
     rows = received[0].shape[1]
-    spans = lax.axis_size("ctx")
     length = parts * rows
     kept = len(held)
     counts = (parts, len(states))
     return pl.pallas_call(
-        functools.partial(grads_kernel, parts, spans, factor, offset, first, counts),
+        functools.partial(grads_kernel, parts, lax.axis_size("ctx"), factor, offset, first, counts),
         in_specs=[pl.BlockSpec(memory_space=pltpu.VMEM)] * sum(counts)
         + [pl.BlockSpec(memory_space=pltpu.HBM)] * kept,
-        out_specs=[pl.BlockSpec(memory_space=pltpu.HBM)] * 3,
-        out_shape=[jax.ShapeDtypeStruct((1, length, group), BF16)] * 3,
+        out_specs=[pl.BlockSpec(memory_space=pltpu.HBM)] * 3 + [pl.BlockSpec(memory_space=pltpu.VMEM)],
+        out_shape=[jax.ShapeDtypeStruct((1, length, group), BF16)] * 3
+        + [jax.ShapeDtypeStruct((8, HD), F32)],
         scratch_shapes=[
             pltpu.VMEM((heads, 4, parts, rows, HD), BF16),
             pltpu.VMEM((heads, 3, length, HD), BF16),
@@ -330,18 +337,17 @@
     own, packed = pack_rest(arrays, parts, heads, chunks)
 
     def exchange(own, values):
-        moved = {
-            step: send(value, "head", lambda index: target_of(index, step, parts))
-            for step, value in list(enumerate(values, 1))[1:] + [(1, values[0])]
-        }
-        return [own] + [moved[step] for step in range(1, parts)]
+        return [own] + [
+            send(values[step - 1], "head", lambda index: target_of(index, step, parts))
+            for step in steps_of(parts)[1:]
+        ]
 
     received = [exchange(own, first)] + [exchange(values[0], values[1:]) for values in packed]
-    early = other_states(own_states(received[0], chunks[0], late, []))
-    second = other_states(own_states(received[1], middle, 0, early[1:]))
-    held = gradients(received[0], early, 0, (), 0, chunks[0], group, factor)
-    held = gradients(received[1], second, 0, held, chunks[0], middle, group, factor)
-    held = gradients(received[2], early, chunks[0], held, heads - late, late, group, factor)
+    early = other_states(*own_states(received[0], chunks[0], late, []))
+    *held, token = gradients(received[0], early, 0, (), 0, chunks[0], group, factor)
+    second = other_states(*own_states(received[1], middle, 0, [token]))
+    *held, _ = gradients(received[1], second, 0, held, chunks[0], middle, group, factor)
+    *held, _ = gradients(received[2], early, chunks[0], held, heads - late, late, group, factor)
     return tuple(held)
 
 

time: 77 us -> 83.6 us (1.086)
  waiting for transfers between devices: 33.6 us -> 41.1 us
  starting transfers between devices: 25.1 us -> 23 us
  Pallas kernels: 17.1 us -> 18.3 us
    ppermute x17, waiting for transfers between devices: 33.6 us -> 41.1 us  [send(): lax.ppermute(value, axis, [(index, target(index)) for index in range(coun...]
    ppermute x17, starting transfers between devices: 25.1 us -> 23 us  [send(): lax.ppermute(value, axis, [(index, target(index)) for index in range(coun...]
    pallas_call x3, Pallas kernels: 12.1 us -> 13.3 us  [gradients(): pl.pallas_call(functools.partial(grads_kernel, parts, lax.axis_size('ctx'...]
  transfers between devices with their start and end apart: 17 -> 17, of which waited for: 6 -> 8; matrix products, arithmetic and copies ran while one was open for 0% -> 0% of each run, Pallas kernels for 14% -> 14%
where the time goes in v3:
time: 83.6 us; the launch traced here: 83.3 us
  waiting for transfers between devices  41.1 us (49%)
  starting transfers between devices  23 us (28%)
  Pallas kernels  18.3 us (22%)
  between operations  0.92 us (1%)
    ppermute x17, waiting for transfers between devices, send(): lax.ppermute(value, axis, [(index, target(index)) for index in range(coun...  41.1 us
    ppermute x17, starting transfers between devices, send(): lax.ppermute(value, axis, [(index, target(index)) for index in range(coun...  23 us
    pallas_call x3, Pallas kernels, gradients(): pl.pallas_call(functools.partial(grads_kernel, parts, lax.axis_size('ctx'...  13.3 us
    pallas_call x1, Pallas kernels, pack_rest(): pl.pallas_call(functools.partial(rest_kernel, parts, heads, chunks), in_s...  2.15 us
    pallas_call x1, Pallas kernels, pack_first(): pl.pallas_call(functools.partial(first_kernel, parts, heads, count, late)...  1.85 us
  transfers between devices with their start and end apart: 17, of which 8 were waited for; matrix products, arithmetic and copies ran while one was open for 0% of the time, Pallas kernels for 14%

profile of v3, /device:TPU:0, one launch (start us, length us, event | category | flops | bytes accessed | tf_op | source)
XLA Modules:
  0.0 83.3 jit_solution(3073066577507825291)
XLA Ops:
  0.6 1.9 %pack.3 = (bf16[16,128,128]{2,1,0:T(8,128)(2,1)S(1)}, bf16[16,128,128]{2,1,0:T(8,128)(2,1)S(1)}, bf16[16,128,128]{2,1,0:T(8,128)(2,1)S(1)}) custom-call(bf16[1,128,4096]{2,1,0:T(8,128)(2,1)} %refs_0_.3, bf16[1,128,4096]{2,1,0:T(8,128)(2,1)} %refs_1_.3, bf16[1,128,4096]{2,1,0:T(8,128)(2,1)} %refs_2_.3, bf16[1,128,4096]{2,1,0:T(8,128)(2,1)} %refs_3_.3), custom_call_target="tpu_custom_call" | custom-call | flops 1000 | bytes 2048 | tf_op jit(solution)/shard_map/pack/pallas_call | solution.py:92
  2.5 3.0 %collective-permute-start.3 = (bf16[16,128,128]{2,1,0:T(8,128)(2,1)S(1)}, bf16[16,128,128]{2,1,0:T(8,128)(2,1)S(1)}, u32[]{:S(2)}, u32[]{:S(2)}) collective-permute-start(bf16[16,128,128]{2,1,0:T(8,128)(2,1)S(1)} %get-tuple-element.40), channel_id=1, source_target_pairs={{0,16},{8,24},{16,0},{24,8},{1,17},{9,25},{17,1},{25,9},{2,18},{10... | collective-permute-start | bytes 1572872 | tf_op jit(solution)/shard_map/ppermute | solution.py:47
  5.5 1.4 %collective-permute-start.4 = (bf16[16,128,128]{2,1,0:T(8,128)(2,1)S(1)}, bf16[16,128,128]{2,1,0:T(8,128)(2,1)S(1)}, u32[]{:S(2)}, u32[]{:S(2)}) collective-permute-start(bf16[16,128,128]{2,1,0:T(8,128)(2,1)S(1)} %get-tuple-element.41), channel_id=1, source_target_pairs={{0,24},{8,16},{16,8},{24,0},{1,25},{9,17},{17,9},{25,1},{2,26},{10... | collective-permute-start | bytes 1572872 | tf_op jit(solution)/shard_map/ppermute | solution.py:47
  7.0 0.1 collective-permute-start.5
  7.1 2.1 %pack.2 = (bf16[16,128,128]{2,1,0:T(8,128)(2,1)S(1)}, bf16[12,128,128]{2,1,0:T(8,128)(2,1)S(1)}, bf16[12,128,128]{2,1,0:T(8,128)(2,1)S(1)}, bf16[12,128,128]{2,1...) custom-call(bf16[1,128,4096]{2,1,0:T(8,128)(2,1)} %refs_0_.3, ...), custom_call_target="tpu_custom_call" | custom-call | flops 1000 | bytes 2048 | tf_op jit(solution)/shard_map/pack/pallas_call | solution.py:135
  9.2 19.5 %collective-permute-done.3.refs_1_ = bf16[16,128,128]{2,1,0:T(8,128)(2,1)S(1)} collective-permute-done((bf16[16,128,128]{2,1,0:T(8,128)(2,1)S(1)}, bf16[16,128,128]{2,1,0:T(8,128)(2,1)S(1)}, u32[]{:S(2)}, u32[]{:S(2)}) %collective-permute-start.3) | collective-permute-done | bytes 524320 | tf_op jit(solution)/shard_map/ppermute | solution.py:47
  28.7 1.3 %collective-permute-done.5.refs_3_ = bf16[16,128,128]{2,1,0:T(8,128)(2,1)S(1)} collective-permute-done((bf16[16,128,128]{2,1,0:T(8,128)(2,1)S(1)}, bf16[16,128,128]{2,1,0:T(8,128)(2,1)S(1)}, u32[]{:S(2)}, u32[]{:S(2)}) %collective-permute-start.5) | collective-permute-done | bytes 524320 | tf_op jit(solution)/shard_map/ppermute | solution.py:47
  30.0 0.4 own_states.2
  30.5 1.7 %collective-permute-start.10 = (bf16[12,128,128]{2,1,0:T(8,128)(2,1)S(1)}, bf16[12,128,128]{2,1,0:T(8,128)(2,1)S(1)}, u32[]{:S(2)}, u32[]{:S(2)}) collective-permute-start(bf16[12,128,128]{2,1,0:T(8,128)(2,1)S(1)} %get-tuple-element.49), channel_id=1, source_target_pairs={{0,16},{8,24},{16,0},{24,8},{1,17},{9,25},{17,1},{25,9},{2,18},{10... | collective-permute-start | bytes 1179656 | tf_op jit(solution)/shard_map/ppermute | solution.py:47
  32.2 1.4 %collective-permute-start.11 = (bf16[12,128,128]{2,1,0:T(8,128)(2,1)S(1)}, bf16[12,128,128]{2,1,0:T(8,128)(2,1)S(1)}, u32[]{:S(2)}, u32[]{:S(2)}) collective-permute-start(bf16[12,128,128]{2,1,0:T(8,128)(2,1)S(1)} %get-tuple-element.50), channel_id=1, source_target_pairs={{0,24},{8,16},{16,8},{24,0},{1,25},{9,17},{17,9},{25,1},{2,26},{10... | collective-permute-start | bytes 1179656 | tf_op jit(solution)/shard_map/ppermute | solution.py:47
  33.7 0.4 collective-permute-start.12
  34.1 0.1 chip_states.2
  34.2 1.8 %collective-permute-start.7 = (bf16[5,128,128]{2,1,0:T(8,128)(2,1)S(1)}, bf16[5,128,128]{2,1,0:T(8,128)(2,1)S(1)}, u32[]{:S(2)}, u32[]{:S(2)}) collective-permute-start(bf16[5,128,128]{2,1,0:T(8,128)(2,1)S(1)} %get-tuple-element.45), channel_id=1, source_target_pairs={{0,2},{1,3},{2,4},{3,5},{4,6},{5,7},{6,0},{7,1},{8,10},{9,11},{10,... | collective-permute-start | bytes 491528 | tf_op jit(solution)/shard_map/ppermute | solution.py:47
  36.0 2.6 %collective-permute-start.8 = (bf16[5,128,128]{2,1,0:T(8,128)(2,1)S(1)}, bf16[5,128,128]{2,1,0:T(8,128)(2,1)S(1)}, u32[]{:S(2)}, u32[]{:S(2)}) collective-permute-start(bf16[5,128,128]{2,1,0:T(8,128)(2,1)S(1)} %get-tuple-element.46), channel_id=1, source_target_pairs={{0,4},{1,5},{2,6},{3,7},{4,0},{5,1},{6,2},{7,3},{8,12},{9,13},{10,... | collective-permute-start | bytes 491528 | tf_op jit(solution)/shard_map/ppermute | solution.py:47
  38.6 4.7 %collective-permute-done.7.refs_5_ = bf16[5,128,128]{2,1,0:T(8,128)(2,1)S(1)} collective-permute-done((bf16[5,128,128]{2,1,0:T(8,128)(2,1)S(1)}, bf16[5,128,128]{2,1,0:T(8,128)(2,1)S(1)}, u32[]{:S(2)}, u32[]{:S(2)}) %collective-permute-start.7) | collective-permute-done | bytes 163872 | tf_op jit(solution)/shard_map/ppermute | solution.py:47
  43.2 1.0 %collective-permute-start.9 = (bf16[5,128,128]{2,1,0:T(8,128)(2,1)S(1)}, bf16[5,128,128]{2,1,0:T(8,128)(2,1)S(1)}, u32[]{:S(2)}, u32[]{:S(2)}) collective-permute-start(bf16[5,128,128]{2,1,0:T(8,128)(2,1)S(1)} %get-tuple-element.47), channel_id=1, source_target_pairs={{0,6},{1,7},{2,0},{3,1},{4,2},{5,3},{6,4},{7,5},{8,14},{9,15},{10,... | collective-permute-start | bytes 491528 | tf_op jit(solution)/shard_map/ppermute | solution.py:47
  44.2 4.8 %collective-permute-done.8.refs_6_ = bf16[5,128,128]{2,1,0:T(8,128)(2,1)S(1)} collective-permute-done((bf16[5,128,128]{2,1,0:T(8,128)(2,1)S(1)}, bf16[5,128,128]{2,1,0:T(8,128)(2,1)S(1)}, u32[]{:S(2)}, u32[]{:S(2)}) %collective-permute-start.8) | collective-permute-done | bytes 163872 | tf_op jit(solution)/shard_map/ppermute | solution.py:47
  49.1 3.3 %collective-permute-done.9.refs_7_ = bf16[5,128,128]{2,1,0:T(8,128)(2,1)S(1)} collective-permute-done((bf16[5,128,128]{2,1,0:T(8,128)(2,1)S(1)}, bf16[5,128,128]{2,1,0:T(8,128)(2,1)S(1)}, u32[]{:S(2)}, u32[]{:S(2)}) %collective-permute-start.9) | collective-permute-done | bytes 163872 | tf_op jit(solution)/shard_map/ppermute | solution.py:47
  52.4 4.4 %gradients.3 = (bf16[1,512,1024]{2,1,0:T(8,128)(2,1)}, bf16[1,512,1024]{2,1,0:T(8,128)(2,1)}, bf16[1,512,1024]{2,1,0:T(8,128)(2,1)}, f32[8,128]{1,0:T(8,128)S(1)}) custom-call(bf16[16,128,128]{2,1,0:T(8,128)(2,1)S(1)} %get-tuple-element.39.refs_0_, bf16[16,128,128]{2,1,0:T(8,128)(2,1)S(1)} %collective-permute-done.3.refs_1_, ...), custom_call_target="tpu_custom_call" | custom-call | flops 1000 | bytes 2048 | tf_op jit(solution)/shard_map/gradients/pallas_call | solution.py:307
  56.8 0.4 own_states.3
  57.2 0.1 collective-permute-start.13
  57.3 1.6 %collective-permute-start = (bf16[8,128,128]{2,1,0:T(8,128)(2,1)S(1)}, bf16[8,128,128]{2,1,0:T(8,128)(2,1)S(1)}, u32[]{:S(2)}, u32[]{:S(2)}) collective-permute-start(bf16[8,128,128]{2,1,0:T(8,128)(2,1)S(1)} %get-tuple-element.36), channel_id=1, source_target_pairs={{0,16},{8,24},{16,0},{24,8},{1,17},{9,25},{17,1},{25,9},{2,18},{10... | collective-permute-start | bytes 786440 | tf_op jit(solution)/shard_map/ppermute | solution.py:47
  58.9 1.4 %collective-permute-start.1 = (bf16[8,128,128]{2,1,0:T(8,128)(2,1)S(1)}, bf16[8,128,128]{2,1,0:T(8,128)(2,1)S(1)}, u32[]{:S(2)}, u32[]{:S(2)}) collective-permute-start(bf16[8,128,128]{2,1,0:T(8,128)(2,1)S(1)} %get-tuple-element.37), channel_id=1, source_target_pairs={{0,24},{8,16},{16,8},{24,0},{1,25},{9,17},{17,9},{25,1},{2,26},{10... | collective-permute-start | bytes 786440 | tf_op jit(solution)/shard_map/ppermute | solution.py:47
  60.3 0.5 collective-permute-start.2
  60.9 2.7 %collective-permute-start.14 = (bf16[3,128,128]{2,1,0:T(8,128)(2,1)S(1)}, bf16[3,128,128]{2,1,0:T(8,128)(2,1)S(1)}, u32[]{:S(2)}, u32[]{:S(2)}) collective-permute-start(bf16[3,128,128]{2,1,0:T(8,128)(2,1)S(1)} %get-tuple-element.55), channel_id=1, source_target_pairs={{0,2},{1,3},{2,4},{3,5},{4,6},{5,7},{6,0},{7,1},{8,10},{9,11},{10,... | collective-permute-start | bytes 294920 | tf_op jit(solution)/shard_map/ppermute | solution.py:47
  63.6 1.5 %collective-permute-start.15 = (bf16[3,128,128]{2,1,0:T(8,128)(2,1)S(1)}, bf16[3,128,128]{2,1,0:T(8,128)(2,1)S(1)}, u32[]{:S(2)}, u32[]{:S(2)}) collective-permute-start(bf16[3,128,128]{2,1,0:T(8,128)(2,1)S(1)} %get-tuple-element.56), channel_id=1, source_target_pairs={{0,4},{1,5},{2,6},{3,7},{4,0},{5,1},{6,2},{7,3},{8,12},{9,13},{10,... | collective-permute-start | bytes 294920 | tf_op jit(solution)/shard_map/ppermute | solution.py:47
  65.1 2.4 %collective-permute-done.14.refs_5_ = bf16[3,128,128]{2,1,0:T(8,128)(2,1)S(1)} collective-permute-done((bf16[3,128,128]{2,1,0:T(8,128)(2,1)S(1)}, bf16[3,128,128]{2,1,0:T(8,128)(2,1)S(1)}, u32[]{:S(2)}, u32[]{:S(2)}) %collective-permute-start.14) | collective-permute-done | bytes 98336 | tf_op jit(solution)/shard_map/ppermute | solution.py:47
  67.5 1.6 %collective-permute-start.16 = (bf16[3,128,128]{2,1,0:T(8,128)(2,1)S(1)}, bf16[3,128,128]{2,1,0:T(8,128)(2,1)S(1)}, u32[]{:S(2)}, u32[]{:S(2)}) collective-permute-start(bf16[3,128,128]{2,1,0:T(8,128)(2,1)S(1)} %get-tuple-element.57), channel_id=1, source_target_pairs={{0,6},{1,7},{2,0},{3,1},{4,2},{5,3},{6,4},{7,5},{8,14},{9,15},{10,... | collective-permute-start | bytes 294920 | tf_op jit(solution)/shard_map/ppermute | solution.py:47
  69.1 3.0 %collective-permute-done.15.refs_6_ = bf16[3,128,128]{2,1,0:T(8,128)(2,1)S(1)} collective-permute-done((bf16[3,128,128]{2,1,0:T(8,128)(2,1)S(1)}, bf16[3,128,128]{2,1,0:T(8,128)(2,1)S(1)}, u32[]{:S(2)}, u32[]{:S(2)}) %collective-permute-start.15) | collective-permute-done | bytes 98336 | tf_op jit(solution)/shard_map/ppermute | solution.py:47
  72.1 2.1 %collective-permute-done.16.refs_7_ = bf16[3,128,128]{2,1,0:T(8,128)(2,1)S(1)} collective-permute-done((bf16[3,128,128]{2,1,0:T(8,128)(2,1)S(1)}, bf16[3,128,128]{2,1,0:T(8,128)(2,1)S(1)}, u32[]{:S(2)}, u32[]{:S(2)}) %collective-permute-start.16) | collective-permute-done | bytes 98336 | tf_op jit(solution)/shard_map/ppermute | solution.py:47
  74.2 5.0 %gradients.4 = (bf16[1,512,1024]{2,1,0:T(8,128)(2,1)}, bf16[1,512,1024]{2,1,0:T(8,128)(2,1)}, bf16[1,512,1024]{2,1,0:T(8,128)(2,1)}, f32[8,128]{1,0:T(8,128)}) custom-call(bf16[12,128,128]{2,1,0:T(8,128)(2,1)S(1)} %get-tuple-element.48.refs_0_, ...), custom_call_target="tpu_custom_call", output_to_operand_aliasing={{0}: (8, {}), {1}: (9, {}), {2}: (10, {})} | custom-call | flops 1000 | bytes 2048 | tf_op jit(solution)/shard_map/gradients/pallas_call | solution.py:307
  79.3 3.9 %gradients.5 = (bf16[1,512,1024]{2,1,0:T(8,128)(2,1)}, bf16[1,512,1024]{2,1,0:T(8,128)(2,1)}, bf16[1,512,1024]{2,1,0:T(8,128)(2,1)}, f32[8,128]{1,0:T(8,128)}) custom-call(bf16[8,128,128]{2,1,0:T(8,128)(2,1)S(1)} %get-tuple-element.35.refs_0_, ...), custom_call_target="tpu_custom_call", output_to_operand_aliasing={{0}: (8, {}), {1}: (9, {}), {2}: (10, {})} | custom-call | flops 1000 | bytes 2048 | tf_op jit(solution)/shard_map/gradients/pallas_call | solution.py:307
  (11 shorter events, 0.2 us)
Async XLA Ops:
  2.5 26.2 %collective-permute-start.3 = (bf16[16,128,128]{2,1,0:T(8,128)(2,1)S(1)}, bf16[16,128,128]{2,1,0:T(8,128)(2,1)S(1)}, u32[]{:S(2)}, u32[]{:S(2)}) collective-permute-start(bf16[16,128,128]{2,1,0:T(8,128)(2,1)S(1)} %get-tuple-element.40), channel_id=1, source_target_pairs={{0,16},{8,24},{16,0},{24,8},{1,17},{9,25},{17,1},{25,9},{2,18},{10... | collective-permute-start | bytes 1572872 | tf_op jit(solution)/shard_map/ppermute | solution.py:47
  5.5 23.2 %collective-permute-start.4 = (bf16[16,128,128]{2,1,0:T(8,128)(2,1)S(1)}, bf16[16,128,128]{2,1,0:T(8,128)(2,1)S(1)}, u32[]{:S(2)}, u32[]{:S(2)}) collective-permute-start(bf16[16,128,128]{2,1,0:T(8,128)(2,1)S(1)} %get-tuple-element.41), channel_id=1, source_target_pairs={{0,24},{8,16},{16,8},{24,0},{1,25},{9,17},{17,9},{25,1},{2,26},{10... | collective-permute-start | bytes 1572872 | tf_op jit(solution)/shard_map/ppermute | solution.py:47
  7.0 23.0 %collective-permute-start.5 = (bf16[16,128,128]{2,1,0:T(8,128)(2,1)S(1)}, bf16[16,128,128]{2,1,0:T(8,128)(2,1)S(1)}, u32[]{:S(2)}, u32[]{:S(2)}) collective-permute-start(bf16[16,128,128]{2,1,0:T(8,128)(2,1)S(1)} %get-tuple-element.42), channel_id=1, source_target_pairs={{0,8},{8,0},{16,24},{24,16},{1,9},{9,1},{17,25},{25,17},{2,10},{10... | collective-permute-start | bytes 1572872 | tf_op jit(solution)/shard_map/ppermute | solution.py:47
  30.4 3.6 %collective-permute-start.6 = (bf16[2,5,128,128]{3,2,1,0:T(8,128)(2,1)S(1)}, bf16[2,5,128,128]{3,2,1,0:T(8,128)(2,1)S(1)}, u32[]{:S(2)}, u32[]{:S(2)}) collective-permute-start(bf16[2,5,128,128]{3,2,1,0:T(8,128)(2,1)S(1)} %get-tuple-element.43), channel_id=1, source_target_pairs={{0,1},{1,0},{2,3},{3,2},{4,5},{5,4},{6,7},{7,6},{8,9},{9,8},{10,11... | collective-permute-start | bytes 983048 | tf_op jit(solution)/shard_map/ppermute | solution.py:47
  30.5 26.3 %collective-permute-start.10 = (bf16[12,128,128]{2,1,0:T(8,128)(2,1)S(1)}, bf16[12,128,128]{2,1,0:T(8,128)(2,1)S(1)}, u32[]{:S(2)}, u32[]{:S(2)}) collective-permute-start(bf16[12,128,128]{2,1,0:T(8,128)(2,1)S(1)} %get-tuple-element.49), channel_id=1, source_target_pairs={{0,16},{8,24},{16,0},{24,8},{1,17},{9,25},{17,1},{25,9},{2,18},{10... | collective-permute-start | bytes 1179656 | tf_op jit(solution)/shard_map/ppermute | solution.py:47
  32.2 24.5 %collective-permute-start.11 = (bf16[12,128,128]{2,1,0:T(8,128)(2,1)S(1)}, bf16[12,128,128]{2,1,0:T(8,128)(2,1)S(1)}, u32[]{:S(2)}, u32[]{:S(2)}) collective-permute-start(bf16[12,128,128]{2,1,0:T(8,128)(2,1)S(1)} %get-tuple-element.50), channel_id=1, source_target_pairs={{0,24},{8,16},{16,8},{24,0},{1,25},{9,17},{17,9},{25,1},{2,26},{10... | collective-permute-start | bytes 1179656 | tf_op jit(solution)/shard_map/ppermute | solution.py:47
  33.7 23.1 %collective-permute-start.12 = (bf16[12,128,128]{2,1,0:T(8,128)(2,1)S(1)}, bf16[12,128,128]{2,1,0:T(8,128)(2,1)S(1)}, u32[]{:S(2)}, u32[]{:S(2)}) collective-permute-start(bf16[12,128,128]{2,1,0:T(8,128)(2,1)S(1)} %get-tuple-element.51), channel_id=1, source_target_pairs={{0,8},{8,0},{16,24},{24,16},{1,9},{9,1},{17,25},{25,17},{2,10},{10... | collective-permute-start | bytes 1179656 | tf_op jit(solution)/shard_map/ppermute | solution.py:47
  34.2 9.0 %collective-permute-start.7 = (bf16[5,128,128]{2,1,0:T(8,128)(2,1)S(1)}, bf16[5,128,128]{2,1,0:T(8,128)(2,1)S(1)}, u32[]{:S(2)}, u32[]{:S(2)}) collective-permute-start(bf16[5,128,128]{2,1,0:T(8,128)(2,1)S(1)} %get-tuple-element.45), channel_id=1, source_target_pairs={{0,2},{1,3},{2,4},{3,5},{4,6},{5,7},{6,0},{7,1},{8,10},{9,11},{10,... | collective-permute-start | bytes 491528 | tf_op jit(solution)/shard_map/ppermute | solution.py:47
  36.0 13.1 %collective-permute-start.8 = (bf16[5,128,128]{2,1,0:T(8,128)(2,1)S(1)}, bf16[5,128,128]{2,1,0:T(8,128)(2,1)S(1)}, u32[]{:S(2)}, u32[]{:S(2)}) collective-permute-start(bf16[5,128,128]{2,1,0:T(8,128)(2,1)S(1)} %get-tuple-element.46), channel_id=1, source_target_pairs={{0,4},{1,5},{2,6},{3,7},{4,0},{5,1},{6,2},{7,3},{8,12},{9,13},{10,... | collective-permute-start | bytes 491528 | tf_op jit(solution)/shard_map/ppermute | solution.py:47
  43.2 9.1 %collective-permute-start.9 = (bf16[5,128,128]{2,1,0:T(8,128)(2,1)S(1)}, bf16[5,128,128]{2,1,0:T(8,128)(2,1)S(1)}, u32[]{:S(2)}, u32[]{:S(2)}) collective-permute-start(bf16[5,128,128]{2,1,0:T(8,128)(2,1)S(1)} %get-tuple-element.47), channel_id=1, source_target_pairs={{0,6},{1,7},{2,0},{3,1},{4,2},{5,3},{6,4},{7,5},{8,14},{9,15},{10,... | collective-permute-start | bytes 491528 | tf_op jit(solution)/shard_map/ppermute | solution.py:47
  57.2 3.6 %collective-permute-start.13 = (bf16[2,3,128,128]{3,2,1,0:T(8,128)(2,1)S(1)}, bf16[2,3,128,128]{3,2,1,0:T(8,128)(2,1)S(1)}, u32[]{:S(2)}, u32[]{:S(2)}) collective-permute-start(bf16[2,3,128,128]{3,2,1,0:T(8,128)(2,1)S(1)} %get-tuple-element.53), channel_id=1, source_target_pairs={{0,1},{1,0},{2,3},{3,2},{4,5},{5,4},{6,7},{7,6},{8,9},{9,8},{10,11... | collective-permute-start | bytes 589832 | tf_op jit(solution)/shard_map/ppermute | solution.py:47
  57.3 22.0 %collective-permute-start = (bf16[8,128,128]{2,1,0:T(8,128)(2,1)S(1)}, bf16[8,128,128]{2,1,0:T(8,128)(2,1)S(1)}, u32[]{:S(2)}, u32[]{:S(2)}) collective-permute-start(bf16[8,128,128]{2,1,0:T(8,128)(2,1)S(1)} %get-tuple-element.36), channel_id=1, source_target_pairs={{0,16},{8,24},{16,0},{24,8},{1,17},{9,25},{17,1},{25,9},{2,18},{10... | collective-permute-start | bytes 786440 | tf_op jit(solution)/shard_map/ppermute | solution.py:47
  58.9 20.4 %collective-permute-start.1 = (bf16[8,128,128]{2,1,0:T(8,128)(2,1)S(1)}, bf16[8,128,128]{2,1,0:T(8,128)(2,1)S(1)}, u32[]{:S(2)}, u32[]{:S(2)}) collective-permute-start(bf16[8,128,128]{2,1,0:T(8,128)(2,1)S(1)} %get-tuple-element.37), channel_id=1, source_target_pairs={{0,24},{8,16},{16,8},{24,0},{1,25},{9,17},{17,9},{25,1},{2,26},{10... | collective-permute-start | bytes 786440 | tf_op jit(solution)/shard_map/ppermute | solution.py:47
  60.3 19.0 %collective-permute-start.2 = (bf16[8,128,128]{2,1,0:T(8,128)(2,1)S(1)}, bf16[8,128,128]{2,1,0:T(8,128)(2,1)S(1)}, u32[]{:S(2)}, u32[]{:S(2)}) collective-permute-start(bf16[8,128,128]{2,1,0:T(8,128)(2,1)S(1)} %get-tuple-element.38), channel_id=1, source_target_pairs={{0,8},{8,0},{16,24},{24,16},{1,9},{9,1},{17,25},{25,17},{2,10},{10... | collective-permute-start | bytes 786440 | tf_op jit(solution)/shard_map/ppermute | solution.py:47
  60.9 6.6 %collective-permute-start.14 = (bf16[3,128,128]{2,1,0:T(8,128)(2,1)S(1)}, bf16[3,128,128]{2,1,0:T(8,128)(2,1)S(1)}, u32[]{:S(2)}, u32[]{:S(2)}) collective-permute-start(bf16[3,128,128]{2,1,0:T(8,128)(2,1)S(1)} %get-tuple-element.55), channel_id=1, source_target_pairs={{0,2},{1,3},{2,4},{3,5},{4,6},{5,7},{6,0},{7,1},{8,10},{9,11},{10,... | collective-permute-start | bytes 294920 | tf_op jit(solution)/shard_map/ppermute | solution.py:47
  63.6 8.6 %collective-permute-start.15 = (bf16[3,128,128]{2,1,0:T(8,128)(2,1)S(1)}, bf16[3,128,128]{2,1,0:T(8,128)(2,1)S(1)}, u32[]{:S(2)}, u32[]{:S(2)}) collective-permute-start(bf16[3,128,128]{2,1,0:T(8,128)(2,1)S(1)} %get-tuple-element.56), channel_id=1, source_target_pairs={{0,4},{1,5},{2,6},{3,7},{4,0},{5,1},{6,2},{7,3},{8,12},{9,13},{10,... | collective-permute-start | bytes 294920 | tf_op jit(solution)/shard_map/ppermute | solution.py:47
  67.5 6.8 %collective-permute-start.16 = (bf16[3,128,128]{2,1,0:T(8,128)(2,1)S(1)}, bf16[3,128,128]{2,1,0:T(8,128)(2,1)S(1)}, u32[]{:S(2)}, u32[]{:S(2)}) collective-permute-start(bf16[3,128,128]{2,1,0:T(8,128)(2,1)S(1)} %get-tuple-element.57), channel_id=1, source_target_pairs={{0,6},{1,7},{2,0},{3,1},{4,2},{5,3},{6,4},{7,5},{8,14},{9,15},{10,... | collective-permute-start | bytes 294920 | tf_op jit(solution)/shard_map/ppermute | solution.py:47

commit v4 on v3

--- a/solution.py
+++ b/solution.py
@@ -150,18 +150,26 @@
 
 def state_kernel(parts, heads, extra, *refs):
     inputs, (out, give) = refs[:parts], refs[-2:]
+    first = lax.axis_index("ctx") % 2 == 0
+    half = HD // 2
+
+    def share(head):
+        for state in range(2):
+            value = out[state, head]
+            give[state, head] = jnp.where(first, value[half:], value[:half]).astype(BF16)
+
     for head in range(heads):
         query, keys, values, grads = (
             jnp.concatenate([ref[4 * head + tensor] for ref in inputs], 0) for tensor in range(4)
         )
         out[0, head] = dot(values, keys, (0, 0))
         out[1, head] = dot(query, grads, (0, 0))
-        give[:, head] = out[:, head].astype(BF16)
+        share(head)
     for late in range(extra):
         for state in range(2):
             at = 4 * heads + 2 * late + state
             out[state, heads + late] = sum(ref[at].astype(F32) for ref in inputs)
-        give[:, heads + late] = out[:, heads + late].astype(BF16)
+        share(heads + late)
 
 
 @jax.named_scope("own_states")
@@ -172,73 +180,99 @@
         functools.partial(state_kernel, parts, heads, extra),
         in_specs=[pl.BlockSpec(memory_space=pltpu.VMEM)] * parts
         + [pl.BlockSpec(memory_space=pl.ANY)] * len(before),
-        out_shape=[jax.ShapeDtypeStruct((2, heads + extra, HD, HD), kind) for kind in (F32, BF16)],
+        out_shape=[
+            jax.ShapeDtypeStruct((2, heads + extra, HD, HD), F32),
+            jax.ShapeDtypeStruct((2, heads + extra, HD // 2, HD), BF16),
+        ],
         compiler_params=PARAMS,
         cost_estimate=cost(1000, 1024),
     )(*received, *before)
 
 
-def chip_kernel(chips, own, partner, *outputs):
-    chip = lax.axis_index("ctx") // 2
-    keys = (own[0] + partner[0]).astype(BF16)
-    query = (own[1] + partner[1]).astype(BF16)
-    for step in range(1, chips):
-        outputs[step - 1][...] = jnp.where(chip + step < chips, keys, query)
+def pick_kernel(chips, steps, own, partner, *refs):
+    outputs = refs[-len(steps) :]
+    me = lax.axis_index("ctx")
+    chip, core = me // 2, me % 2
+    half = HD // 2
+    at = pl.ds(pl.multiple_of(core * half, half), half)
+    keys, query = ((own[state, :, at] + partner[state].astype(F32)).astype(BF16) for state in range(2))
+    for step, out in zip(steps, outputs):
+        out[...] = jnp.where(chip + step < chips, keys, query)
 
 
 @jax.named_scope("chip_states")
-def chip_states(own, partner, chips):
-    shape = own.shape[1:]
+def chip_states(own, partner, chips, steps, before=()):
+    _, heads, rows, _ = own.shape
     return pl.pallas_call(
-        functools.partial(chip_kernel, chips),
-        out_shape=[jax.ShapeDtypeStruct(shape, BF16)] * (chips - 1),
-        compiler_params=PARAMS,
-        cost_estimate=cost(1000, 1024),
-    )(own, partner)
-
-
-def other_states(own, give):
+        functools.partial(pick_kernel, chips, steps),
+        in_specs=[pl.BlockSpec(memory_space=pltpu.VMEM)] * 2
+        + [pl.BlockSpec(memory_space=pl.ANY)] * len(before),
+        out_shape=[jax.ShapeDtypeStruct((heads, rows // 2, HD), BF16)] * len(steps),
+        compiler_params=PARAMS,
+        cost_estimate=cost(1000, 1024),
+    )(own, partner, *before)
+
+
+def finish_kernel(chips, own, partner, *refs):
+    others, (mine, give) = refs[:-2], refs[-2:]
+    me = lax.axis_index("ctx")
+    chip, core = me // 2, me % 2
+    half = HD // 2
+    at = pl.ds(pl.multiple_of(core * half, half), half)
+    keys = query = jnp.zeros(others[0].shape, F32)
+    for step, ref in enumerate(others, 1):
+        part = ref[...].astype(F32)
+        keys = keys + jnp.where(chip >= step, part, 0.0)
+        query = query + jnp.where(chip < step, part, 0.0)
+    mine[0] = (keys + jnp.where(core == 1, partner[0].astype(F32), 0.0)).astype(BF16)
+    mine[1] = (query + jnp.where(core == 0, partner[1].astype(F32), 0.0)).astype(BF16)
+    give[0] = (keys + jnp.where(core == 0, own[0, :, at], 0.0)).astype(BF16)
+    give[1] = (query + jnp.where(core == 1, own[1, :, at], 0.0)).astype(BF16)
+
+
+@jax.named_scope("chip_states")
+def finished(own, partner, others):
+    _, heads, rows, _ = own.shape
+    return pl.pallas_call(
+        functools.partial(finish_kernel, len(others) + 1),
+        out_shape=[jax.ShapeDtypeStruct((2, heads, rows // 2, HD), BF16)] * 2,
+        compiler_params=PARAMS,
+        cost_estimate=cost(1000, 1024),
+    )(own, partner, *others)
+
+
+def exchanged(own, give, *before):
     spans = lax.axis_size("ctx")
     chips = spans // 2
-    if spans % 2 or chips > 4:
-        return [lax.all_gather(give, "ctx")]
     partner = send(give, "ctx", lambda index: index ^ 1)
-    sums = chip_states(own, partner, chips)
-    return [partner] + [
-        send(value, "ctx", lambda index: (index + 2 * step) % spans)
-        for step, value in enumerate(sums, 1)
-    ]
-
-
-def read_states(refs, spans, head):
-    me = lax.axis_index("ctx")
-    zero = jnp.zeros((HD, HD), F32)
-    if len(refs) == 1:
-
-        def add(span, totals):
-            keys, query = totals
-            keys = keys + jnp.where(span < me, refs[0][span, 0, head].astype(F32), 0.0)
-            query = query + jnp.where(span > me, refs[0][span, 1, head].astype(F32), 0.0)
-            return keys, query
-
-        return lax.fori_loop(0, spans, add, (zero, zero))
-    partner, others = refs[0], refs[1:]
-    chip, core = me // 2, me % 2
-    keys = jnp.where(core == 1, partner[0, head].astype(F32), 0.0)
-    query = jnp.where(core == 0, partner[1, head].astype(F32), 0.0)
-    for step, ref in enumerate(others, 1):
-        part = ref[head].astype(F32)
-        keys = keys + jnp.where(chip >= step, part, 0.0)
-        query = query + jnp.where(chip < step, part, 0.0)
-    return keys, query
-
-
-def grads_kernel(parts, spans, factor, offset, first, counts, *refs):
-    received, states = refs[: counts[0]], refs[counts[0] : counts[0] + counts[1]]
+    others = []
+    for first in range(1, chips, 2):
+        steps = list(range(first, min(first + 2, chips)))
+        for step, value in zip(steps, chip_states(own, partner, chips, steps, others[-2:][:1] + list(before if others else ()))):
+            others.append(send(value, "ctx", lambda index: (index + 2 * step) % spans))
+    mine, half = finished(own, partner, others)
+    return mine, send(half, "ctx", lambda index: index ^ 1)
+
+
+def read_states(refs, head):
+    first = lax.axis_index("ctx") % 2 == 0
+    mine, theirs = refs
+    return (
+        jnp.concatenate(
+            [
+                jnp.where(first, mine[state, head], theirs[state, head]),
+                jnp.where(first, theirs[state, head], mine[state, head]),
+            ],
+            0,
+        )
+        for state in range(2)
+    )
+
+
+def grads_kernel(parts, factor, groups, *refs):
     outputs, token, (ordered, staged, sem) = refs[-7:-4], refs[-4], refs[-3:]
-    heads = ordered.shape[0]
     me = lax.axis_index("head")
-    rows = received[0].shape[1]
+    rows = refs[0].shape[1]
     length = parts * rows
     tiles = length // TILE
     row = lax.broadcasted_iota(jnp.int32, (TILE, TILE), 0)
@@ -256,70 +290,77 @@
         return (value * factor).astype(BF16)
 
     copies = []
-    for head in range(heads):
-        for step, ref in zip(steps_of(parts), received):
-            place = source_of(me, step, parts)
-            for tensor in range(4):
-                ordered[head, tensor, place] = ref[4 * head + tensor]
-        key_state, query_state = read_states(states, spans, head + offset)
-        key_state = key_state.astype(BF16)
-        query_turned = query_state.T.astype(BF16)
-        query_state = query_state.astype(BF16)
-        query, keys, values, grads = (
-            ordered[head, tensor].reshape(tiles, TILE, HD) for tensor in range(4)
+
+    def store(slot, column, index, tile, value):
+        at = pl.ds(tile * TILE, TILE)
+        staged[slot, index, at] = value
+        copies.append(
+            pltpu.make_async_copy(
+                staged.at[slot, index, at],
+                outputs[index].at[0, at, pl.ds(column * HD, HD)],
+                sem.at[slot, index, tile],
+            )
         )
-        for i in range(tiles):
-            at = slice(i * TILE, (i + 1) * TILE)
-            before, after = range(i + 1), range(i, tiles)
-            staged[head, 0, at] = total(
-                [scores(grads[i], values[j], low if i == j else None) for j in before] + [grads[i]],
-                [keys[j] for j in before] + [key_state],
+        copies[-1].start()
+
+    slot = 0
+    for group, (offset, first, heads) in enumerate(groups):
+        arrays = refs[group * (parts + 2) :][: parts + 2]
+        received, states = arrays[:parts], arrays[parts:]
+        for head in range(heads):
+            for step, ref in zip(steps_of(parts), received):
+                place = source_of(me, step, parts)
+                for tensor in range(4):
+                    ordered[slot, tensor, place] = ref[4 * head + tensor]
+            key_state, query_state = read_states(states, head + offset)
+            query_turned = query_state.astype(F32).T.astype(BF16)
+            query, keys, values, grads = (
+                ordered[slot, tensor].reshape(tiles, TILE, HD) for tensor in range(4)
             )
-            staged[head, 1, at] = total(
-                [scores(values[i], grads[j], high if i == j else None) for j in after] + [values[i]],
-                [query[j] for j in after] + [query_turned],
-            )
-            staged[head, 2, at] = total(
-                [scores(keys[i], query[j], high if i == j else None) for j in after] + [keys[i]],
-                [grads[j] for j in after] + [query_state],
-            )
-        for index, out in enumerate(outputs):
-            copies.append(
-                pltpu.make_async_copy(
-                    staged.at[head, index],
-                    out.at[0, :, pl.ds((first + head) * HD, HD)],
-                    sem.at[head, index],
-                )
-            )
-            copies[-1].start()
+            for i in range(tiles):
+                before, after = range(i + 1), range(i, tiles)
+                column = first + head
+                store(slot, column, 0, i, total(
+                    [scores(grads[i], values[j], low if i == j else None) for j in before] + [grads[i]],
+                    [keys[j] for j in before] + [key_state],
+                ))
+                store(slot, column, 1, i, total(
+                    [scores(values[i], grads[j], high if i == j else None) for j in after] + [values[i]],
+                    [query[j] for j in after] + [query_turned],
+                ))
+                store(slot, column, 2, i, total(
+                    [scores(keys[i], query[j], high if i == j else None) for j in after] + [keys[i]],
+                    [grads[j] for j in after] + [query_state],
+                ))
+            slot += 1
     for copy in copies:
         copy.wait()
     token[...] = jnp.zeros_like(token)
 
 
 @jax.named_scope("gradients")
-def gradients(received, states, offset, held, first, heads, group, factor):
-    parts = len(received)
-    rows = received[0].shape[1]
+def gradients(groups, held, group, factor):
+    parts = len(groups[0][0])
+    rows = groups[0][0][0].shape[1]
     length = parts * rows
-    kept = len(held)
-    counts = (parts, len(states))
+    heads = sum(item[-1] for item in groups)
+    arrays = [value for received, states, *_ in groups for value in (*received, *states)]
     return pl.pallas_call(
-        functools.partial(grads_kernel, parts, lax.axis_size("ctx"), factor, offset, first, counts),
-        in_specs=[pl.BlockSpec(memory_space=pltpu.VMEM)] * sum(counts)
-        + [pl.BlockSpec(memory_space=pltpu.HBM)] * kept,
+        functools.partial(grads_kernel, parts, factor, [item[2:] for item in groups]),
+        in_specs=[pl.BlockSpec(memory_space=pltpu.VMEM)] * len(arrays)
+        + [pl.BlockSpec(memory_space=pltpu.HBM)] * len(held),
         out_specs=[pl.BlockSpec(memory_space=pltpu.HBM)] * 3 + [pl.BlockSpec(memory_space=pltpu.VMEM)],
         out_shape=[jax.ShapeDtypeStruct((1, length, group), BF16)] * 3
         + [jax.ShapeDtypeStruct((8, HD), F32)],
         scratch_shapes=[
             pltpu.VMEM((heads, 4, parts, rows, HD), BF16),
             pltpu.VMEM((heads, 3, length, HD), BF16),
-            pltpu.SemaphoreType.DMA((heads, 3)),
+            pltpu.SemaphoreType.DMA((heads, 3, length // TILE)),
         ],
-        input_output_aliases={sum(counts) + index: index for index in range(kept)},
-        compiler_params=PARAMS,
-        cost_estimate=cost(1000, 1024),
-    )(*received, *states, *held)
+        input_output_aliases={len(arrays) + index: index for index in range(len(held))},
+        compiler_params=PARAMS,
+        cost_estimate=cost(1000, 1024),
+    )(*arrays, *held)
 
 
 def shards(query, keys, values, grad_out):
@@ -343,11 +384,18 @@
         ]
 
     received = [exchange(own, first)] + [exchange(values[0], values[1:]) for values in packed]
-    early = other_states(*own_states(received[0], chunks[0], late, []))
-    *held, token = gradients(received[0], early, 0, (), 0, chunks[0], group, factor)
-    second = other_states(*own_states(received[1], middle, 0, [token]))
-    *held, _ = gradients(received[1], second, 0, held, chunks[0], middle, group, factor)
-    *held, _ = gradients(received[2], early, chunks[0], held, heads - late, late, group, factor)
+    early = exchanged(*own_states(received[0], chunks[0], late, []))
+    *held, token = gradients([(received[0], early, 0, 0, chunks[0])], (), group, factor)
+    second = exchanged(*own_states(received[1], middle, 0, [early[0]]), token)
+    *held, _ = gradients(
+        [
+            (received[2], early, chunks[0], heads - late, late),
+            (received[1], second, 0, chunks[0], middle),
+        ],
+        held,
+        group,
+        factor,
+    )
     return tuple(held)
 
 

time: 83.6 us -> 73.3 us (0.88)
  waiting for transfers between devices: 41.1 us -> 29 us
  starting transfers between devices: 23 us -> 26.1 us
  Pallas kernels: 18.3 us -> 16.8 us
    ppermute x17 -> x19, waiting for transfers between devices: 41.1 us -> 29 us  [send(): lax.ppermute(value, axis, [(index, target(index)) for index in range(coun...]
    ppermute x17 -> x19, starting transfers between devices: 23 us -> 26.1 us  [send(): lax.ppermute(value, axis, [(index, target(index)) for index in range(coun...]
    pallas_call x5 -> x8, Pallas kernels: 13.5 us -> 12 us  [the longest x2 11.6 us: gradients(): pl.pallas_call(functools.partial(grads_kernel, parts, factor, [item[2:] f...]
  transfers between devices with their start and end apart: 17 -> 19, of which waited for: 8 -> 8; matrix products, arithmetic and copies ran while one was open for 0% -> 0% of each run, Pallas kernels for 14% -> 11%
where the time goes in v4:
time: 73.3 us; the launch traced here: 72.9 us
  waiting for transfers between devices  29 us (40%)
  starting transfers between devices  26.1 us (36%)
  Pallas kernels  16.8 us (23%)
  between operations  0.95 us (1%)
    ppermute x19, waiting for transfers between devices, send(): lax.ppermute(value, axis, [(index, target(index)) for index in range(coun...  29 us
    ppermute x19, starting transfers between devices, send(): lax.ppermute(value, axis, [(index, target(index)) for index in range(coun...  26.1 us
    pallas_call x2, Pallas kernels, gradients(): pl.pallas_call(functools.partial(grads_kernel, parts, factor, [item[2:] f...  11.6 us
    pallas_call x1, Pallas kernels, pack_rest(): pl.pallas_call(functools.partial(rest_kernel, parts, heads, chunks), in_s...  2.15 us
    pallas_call x1, Pallas kernels, pack_first(): pl.pallas_call(functools.partial(first_kernel, parts, heads, count, late)...  1.85 us
  transfers between devices with their start and end apart: 19, of which 8 were waited for; matrix products, arithmetic and copies ran while one was open for 0% of the time, Pallas kernels for 11%

profile of v4, /device:TPU:0, one launch (start us, length us, event | category | flops | bytes accessed | tf_op | source)
XLA Modules:
  0.0 72.9 jit_solution(4869774322658961345)
XLA Ops:
  0.6 1.9 %pack.3 = (bf16[16,128,128]{2,1,0:T(8,128)(2,1)S(1)}, bf16[16,128,128]{2,1,0:T(8,128)(2,1)S(1)}, bf16[16,128,128]{2,1,0:T(8,128)(2,1)S(1)}) custom-call(bf16[1,128,4096]{2,1,0:T(8,128)(2,1)} %refs_0_.3, bf16[1,128,4096]{2,1,0:T(8,128)(2,1)} %refs_1_.3, bf16[1,128,4096]{2,1,0:T(8,128)(2,1)} %refs_2_.3, bf16[1,128,4096]{2,1,0:T(8,128)(2,1)} %refs_3_.3), custom_call_target="tpu_custom_call" | custom-call | flops 1000 | bytes 2048 | tf_op jit(solution)/shard_map/pack/pallas_call | solution.py:92
  2.5 3.0 %collective-permute-start.3 = (bf16[16,128,128]{2,1,0:T(8,128)(2,1)S(1)}, bf16[16,128,128]{2,1,0:T(8,128)(2,1)S(1)}, u32[]{:S(2)}, u32[]{:S(2)}) collective-permute-start(bf16[16,128,128]{2,1,0:T(8,128)(2,1)S(1)} %get-tuple-element.39), channel_id=1, source_target_pairs={{0,16},{8,24},{16,0},{24,8},{1,17},{9,25},{17,1},{25,9},{2,18},{10... | collective-permute-start | bytes 1572872 | tf_op jit(solution)/shard_map/ppermute | solution.py:47
  5.5 1.4 %collective-permute-start.4 = (bf16[16,128,128]{2,1,0:T(8,128)(2,1)S(1)}, bf16[16,128,128]{2,1,0:T(8,128)(2,1)S(1)}, u32[]{:S(2)}, u32[]{:S(2)}) collective-permute-start(bf16[16,128,128]{2,1,0:T(8,128)(2,1)S(1)} %get-tuple-element.40), channel_id=1, source_target_pairs={{0,24},{8,16},{16,8},{24,0},{1,25},{9,17},{17,9},{25,1},{2,26},{10... | collective-permute-start | bytes 1572872 | tf_op jit(solution)/shard_map/ppermute | solution.py:47
  7.0 0.1 collective-permute-start.5
  7.1 2.1 %pack.2 = (bf16[16,128,128]{2,1,0:T(8,128)(2,1)S(1)}, bf16[12,128,128]{2,1,0:T(8,128)(2,1)S(1)}, bf16[12,128,128]{2,1,0:T(8,128)(2,1)S(1)}, bf16[12,128,128]{2,1...) custom-call(bf16[1,128,4096]{2,1,0:T(8,128)(2,1)} %refs_0_.3, ...), custom_call_target="tpu_custom_call" | custom-call | flops 1000 | bytes 2048 | tf_op jit(solution)/shard_map/pack/pallas_call | solution.py:135
  9.2 2.0 %collective-permute-start.11 = (bf16[12,128,128]{2,1,0:T(8,128)(2,1)S(1)}, bf16[12,128,128]{2,1,0:T(8,128)(2,1)S(1)}, u32[]{:S(2)}, u32[]{:S(2)}) collective-permute-start(bf16[12,128,128]{2,1,0:T(8,128)(2,1)S(1)} %get-tuple-element.49), channel_id=1, source_target_pairs={{0,16},{8,24},{16,0},{24,8},{1,17},{9,25},{17,1},{25,9},{2,18},{10... | collective-permute-start | bytes 1179656 | tf_op jit(solution)/shard_map/ppermute | solution.py:47
  11.2 1.5 %collective-permute-start.12 = (bf16[12,128,128]{2,1,0:T(8,128)(2,1)S(1)}, bf16[12,128,128]{2,1,0:T(8,128)(2,1)S(1)}, u32[]{:S(2)}, u32[]{:S(2)}) collective-permute-start(bf16[12,128,128]{2,1,0:T(8,128)(2,1)S(1)} %get-tuple-element.50), channel_id=1, source_target_pairs={{0,24},{8,16},{16,8},{24,0},{1,25},{9,17},{17,9},{25,1},{2,26},{10... | collective-permute-start | bytes 1179656 | tf_op jit(solution)/shard_map/ppermute | solution.py:47
  12.7 17.0 %collective-permute-done.3.refs_1_ = bf16[16,128,128]{2,1,0:T(8,128)(2,1)S(1)} collective-permute-done((bf16[16,128,128]{2,1,0:T(8,128)(2,1)S(1)}, bf16[16,128,128]{2,1,0:T(8,128)(2,1)S(1)}, u32[]{:S(2)}, u32[]{:S(2)}) %collective-permute-start.3) | collective-permute-done | bytes 524320 | tf_op jit(solution)/shard_map/ppermute | solution.py:47
  29.7 2.2 %collective-permute-start.13 = (bf16[12,128,128]{2,1,0:T(8,128)(2,1)S(1)}, bf16[12,128,128]{2,1,0:T(8,128)(2,1)S(1)}, u32[]{:S(2)}, u32[]{:S(2)}) collective-permute-start(bf16[12,128,128]{2,1,0:T(8,128)(2,1)S(1)} %get-tuple-element.51), channel_id=1, source_target_pairs={{0,8},{8,0},{16,24},{24,16},{1,9},{9,1},{17,25},{25,17},{2,10},{10... | collective-permute-start | bytes 1179656 | tf_op jit(solution)/shard_map/ppermute | solution.py:47
  31.9 0.4 own_states.2
  32.4 1.4 %collective-permute-done.6.partner = bf16[2,5,64,128]{3,2,1,0:T(8,128)(2,1)S(1)} collective-permute-done((bf16[2,5,64,128]{3,2,1,0:T(8,128)(2,1)S(1)}, bf16[2,5,64,128]{3,2,1,0:T(8,128)(2,1)S(1)}, u32[]{:S(2)}, u32[]{:S(2)}) %collective-permute-start.6) | collective-permute-done | bytes 163872 | tf_op jit(solution)/shard_map/ppermute | solution.py:47
  33.9 1.6 %collective-permute-start.7 = (bf16[5,64,128]{2,1,0:T(8,128)(2,1)S(1)}, bf16[5,64,128]{2,1,0:T(8,128)(2,1)S(1)}, u32[]{:S(2)}, u32[]{:S(2)}) collective-permute-start(bf16[5,64,128]{2,1,0:T(8,128)(2,1)S(1)} %get-tuple-element.44), channel_id=1, source_target_pairs={{0,2},{1,3},{2,4},{3,5},{4,6},{5,7},{6,0},{7,1},{8,10},{9,11},{10,... | collective-permute-start | bytes 245768 | tf_op jit(solution)/shard_map/ppermute | solution.py:47
  35.5 2.6 %collective-permute-start.8 = (bf16[5,64,128]{2,1,0:T(8,128)(2,1)S(1)}, bf16[5,64,128]{2,1,0:T(8,128)(2,1)S(1)}, u32[]{:S(2)}, u32[]{:S(2)}) collective-permute-start(bf16[5,64,128]{2,1,0:T(8,128)(2,1)S(1)} %get-tuple-element.45), channel_id=1, source_target_pairs={{0,4},{1,5},{2,6},{3,7},{4,0},{5,1},{6,2},{7,3},{8,12},{9,13},{10,... | collective-permute-start | bytes 245768 | tf_op jit(solution)/shard_map/ppermute | solution.py:47
  38.1 2.7 %collective-permute-done.7.refs_0_ = bf16[5,64,128]{2,1,0:T(8,128)(2,1)S(1)} collective-permute-done((bf16[5,64,128]{2,1,0:T(8,128)(2,1)S(1)}, bf16[5,64,128]{2,1,0:T(8,128)(2,1)S(1)}, u32[]{:S(2)}, u32[]{:S(2)}) %collective-permute-start.7) | collective-permute-done | bytes 81952 | tf_op jit(solution)/shard_map/ppermute | solution.py:47
  40.9 1.8 %collective-permute-start.9 = (bf16[5,64,128]{2,1,0:T(8,128)(2,1)S(1)}, bf16[5,64,128]{2,1,0:T(8,128)(2,1)S(1)}, u32[]{:S(2)}, u32[]{:S(2)}) collective-permute-start(bf16[5,64,128]{2,1,0:T(8,128)(2,1)S(1)} %chip_states.7), channel_id=1, source_target_pairs={{0,6},{1,7},{2,0},{3,1},{4,2},{5,3},{6,4},{7,5},{8,14},{9,15},{10,... | collective-permute-start | bytes 245768 | tf_op jit(solution)/shard_map/ppermute | solution.py:47
  42.7 1.2 %collective-permute-done.8.refs_1_ = bf16[5,64,128]{2,1,0:T(8,128)(2,1)S(1)} collective-permute-done((bf16[5,64,128]{2,1,0:T(8,128)(2,1)S(1)}, bf16[5,64,128]{2,1,0:T(8,128)(2,1)S(1)}, u32[]{:S(2)}, u32[]{:S(2)}) %collective-permute-start.8) | collective-permute-done | bytes 81952 | tf_op jit(solution)/shard_map/ppermute | solution.py:47
  43.9 1.6 %collective-permute-done.9.refs_2_ = bf16[5,64,128]{2,1,0:T(8,128)(2,1)S(1)} collective-permute-done((bf16[5,64,128]{2,1,0:T(8,128)(2,1)S(1)}, bf16[5,64,128]{2,1,0:T(8,128)(2,1)S(1)}, u32[]{:S(2)}, u32[]{:S(2)}) %collective-permute-start.9) | collective-permute-done | bytes 81952 | tf_op jit(solution)/shard_map/ppermute | solution.py:47
  45.6 0.2 chip_states.8
  45.7 0.1 collective-permute-start.10
  45.8 1.1 %collective-permute-done.13.refs_3_.refs_9_ = bf16[12,128,128]{2,1,0:T(8,128)(2,1)S(1)} collective-permute-done((bf16[12,128,128]{2,1,0:T(8,128)(2,1)S(1)}, bf16[12,128,128]{2,1,0:T(8,128)(2,1)S(1)}, u32[]{:S(2)}, u32[]{:S(2)}) %collective-permute-start.13) | collective-permute-done | bytes 393248 | tf_op jit(solution)/shard_map/ppermute | solution.py:47
  46.9 0.4 own_states.3
  47.4 1.9 %collective-permute-start = (bf16[8,128,128]{2,1,0:T(8,128)(2,1)S(1)}, bf16[8,128,128]{2,1,0:T(8,128)(2,1)S(1)}, u32[]{:S(2)}, u32[]{:S(2)}) collective-permute-start(bf16[8,128,128]{2,1,0:T(8,128)(2,1)S(1)} %get-tuple-element.35), channel_id=1, source_target_pairs={{0,16},{8,24},{16,0},{24,8},{1,17},{9,25},{17,1},{25,9},{2,18},{10... | collective-permute-start | bytes 786440 | tf_op jit(solution)/shard_map/ppermute | solution.py:47
  49.3 1.2 %collective-permute-start.1 = (bf16[8,128,128]{2,1,0:T(8,128)(2,1)S(1)}, bf16[8,128,128]{2,1,0:T(8,128)(2,1)S(1)}, u32[]{:S(2)}, u32[]{:S(2)}) collective-permute-start(bf16[8,128,128]{2,1,0:T(8,128)(2,1)S(1)} %get-tuple-element.36), channel_id=1, source_target_pairs={{0,24},{8,16},{16,8},{24,0},{1,25},{9,17},{17,9},{25,1},{2,26},{10... | collective-permute-start | bytes 786440 | tf_op jit(solution)/shard_map/ppermute | solution.py:47
  50.5 0.4 collective-permute-start.2
  51.0 1.8 %collective-permute-start.15 = (bf16[3,64,128]{2,1,0:T(8,128)(2,1)S(1)}, bf16[3,64,128]{2,1,0:T(8,128)(2,1)S(1)}, u32[]{:S(2)}, u32[]{:S(2)}) collective-permute-start(bf16[3,64,128]{2,1,0:T(8,128)(2,1)S(1)} %get-tuple-element.54), channel_id=1, source_target_pairs={{0,2},{1,3},{2,4},{3,5},{4,6},{5,7},{6,0},{7,1},{8,10},{9,11},{10,... | collective-permute-start | bytes 147464 | tf_op jit(solution)/shard_map/ppermute | solution.py:47
  52.8 2.6 %collective-permute-start.16 = (bf16[3,64,128]{2,1,0:T(8,128)(2,1)S(1)}, bf16[3,64,128]{2,1,0:T(8,128)(2,1)S(1)}, u32[]{:S(2)}, u32[]{:S(2)}) collective-permute-start(bf16[3,64,128]{2,1,0:T(8,128)(2,1)S(1)} %get-tuple-element.55), channel_id=1, source_target_pairs={{0,4},{1,5},{2,6},{3,7},{4,0},{5,1},{6,2},{7,3},{8,12},{9,13},{10,... | collective-permute-start | bytes 147464 | tf_op jit(solution)/shard_map/ppermute | solution.py:47
  55.3 4.4 %gradients.2 = (bf16[1,512,1024]{2,1,0:T(8,128)(2,1)}, bf16[1,512,1024]{2,1,0:T(8,128)(2,1)}, bf16[1,512,1024]{2,1,0:T(8,128)(2,1)}, f32[8,128]{1,0:T(8,128)S(1)}) custom-call(bf16[16,128,128]{2,1,0:T(8,128)(2,1)S(1)} %get-tuple-element.38.refs_0_, bf16[16,128,128]{2,1,0:T(8,128)(2,1)S(1)} %collective-permute-done.3.refs_1_, ...), custom_call_target="tpu_custom_call" | custom-call | flops 1000 | bytes 2048 | tf_op jit(solution)/shard_map/gradients/pallas_call | solution.py:348
  59.8 1.6 %collective-permute-start.17 = (bf16[3,64,128]{2,1,0:T(8,128)(2,1)S(1)}, bf16[3,64,128]{2,1,0:T(8,128)(2,1)S(1)}, u32[]{:S(2)}, u32[]{:S(2)}) collective-permute-start(bf16[3,64,128]{2,1,0:T(8,128)(2,1)S(1)} %chip_states.10), channel_id=1, source_target_pairs={{0,6},{1,7},{2,0},{3,1},{4,2},{5,3},{6,4},{7,5},{8,14},{9,15},{10,... | collective-permute-start | bytes 147464 | tf_op jit(solution)/shard_map/ppermute | solution.py:47
  61.3 2.7 %collective-permute-done.17.refs_2_ = bf16[3,64,128]{2,1,0:T(8,128)(2,1)S(1)} collective-permute-done((bf16[3,64,128]{2,1,0:T(8,128)(2,1)S(1)}, bf16[3,64,128]{2,1,0:T(8,128)(2,1)S(1)}, u32[]{:S(2)}, u32[]{:S(2)}) %collective-permute-start.17) | collective-permute-done | bytes 49184 | tf_op jit(solution)/shard_map/ppermute | solution.py:47
  64.1 0.1 chip_states.11
  64.3 1.3 %collective-permute-done.18.refs_11_ = bf16[2,3,64,128]{3,2,1,0:T(8,128)(2,1)S(1)} collective-permute-done((bf16[2,3,64,128]{3,2,1,0:T(8,128)(2,1)S(1)}, bf16[2,3,64,128]{3,2,1,0:T(8,128)(2,1)S(1)}, u32[]{:S(2)}, u32[]{:S(2)}) %collective-permute-start.18) | collective-permute-done | bytes 98336 | tf_op jit(solution)/shard_map/ppermute | solution.py:47
  65.6 7.2 %gradients.3 = (bf16[1,512,1024]{2,1,0:T(8,128)(2,1)}, bf16[1,512,1024]{2,1,0:T(8,128)(2,1)}, bf16[1,512,1024]{2,1,0:T(8,128)(2,1)}, f32[8,128]{1,0:T(8,128)}) custom-call(bf16[8,128,128]{2,1,0:T(8,128)(2,1)S(1)} %get-tuple-element.34.refs_0_, ...), custom_call_target="tpu_custom_call", output_to_operand_aliasing={{0}: (12, {}), {1}: (13, {}), {2}: (14, {})} | custom-call | flops 1000 | bytes 2048 | tf_op jit(solution)/shard_map/gradients/pallas_call | solution.py:348
  (18 shorter events, 0.4 us)
Async XLA Ops:
  2.5 27.2 %collective-permute-start.3 = (bf16[16,128,128]{2,1,0:T(8,128)(2,1)S(1)}, bf16[16,128,128]{2,1,0:T(8,128)(2,1)S(1)}, u32[]{:S(2)}, u32[]{:S(2)}) collective-permute-start(bf16[16,128,128]{2,1,0:T(8,128)(2,1)S(1)} %get-tuple-element.39), channel_id=1, source_target_pairs={{0,16},{8,24},{16,0},{24,8},{1,17},{9,25},{17,1},{25,9},{2,18},{10... | collective-permute-start | bytes 1572872 | tf_op jit(solution)/shard_map/ppermute | solution.py:47
  5.5 26.4 %collective-permute-start.4 = (bf16[16,128,128]{2,1,0:T(8,128)(2,1)S(1)}, bf16[16,128,128]{2,1,0:T(8,128)(2,1)S(1)}, u32[]{:S(2)}, u32[]{:S(2)}) collective-permute-start(bf16[16,128,128]{2,1,0:T(8,128)(2,1)S(1)} %get-tuple-element.40), channel_id=1, source_target_pairs={{0,24},{8,16},{16,8},{24,0},{1,25},{9,17},{17,9},{25,1},{2,26},{10... | collective-permute-start | bytes 1572872 | tf_op jit(solution)/shard_map/ppermute | solution.py:47
  7.0 25.0 %collective-permute-start.5 = (bf16[16,128,128]{2,1,0:T(8,128)(2,1)S(1)}, bf16[16,128,128]{2,1,0:T(8,128)(2,1)S(1)}, u32[]{:S(2)}, u32[]{:S(2)}) collective-permute-start(bf16[16,128,128]{2,1,0:T(8,128)(2,1)S(1)} %get-tuple-element.41), channel_id=1, source_target_pairs={{0,8},{8,0},{16,24},{24,16},{1,9},{9,1},{17,25},{25,17},{2,10},{10... | collective-permute-start | bytes 1572872 | tf_op jit(solution)/shard_map/ppermute | solution.py:47
  9.2 36.6 %collective-permute-start.11 = (bf16[12,128,128]{2,1,0:T(8,128)(2,1)S(1)}, bf16[12,128,128]{2,1,0:T(8,128)(2,1)S(1)}, u32[]{:S(2)}, u32[]{:S(2)}) collective-permute-start(bf16[12,128,128]{2,1,0:T(8,128)(2,1)S(1)} %get-tuple-element.49), channel_id=1, source_target_pairs={{0,16},{8,24},{16,0},{24,8},{1,17},{9,25},{17,1},{25,9},{2,18},{10... | collective-permute-start | bytes 1179656 | tf_op jit(solution)/shard_map/ppermute | solution.py:47
  11.2 34.6 %collective-permute-start.12 = (bf16[12,128,128]{2,1,0:T(8,128)(2,1)S(1)}, bf16[12,128,128]{2,1,0:T(8,128)(2,1)S(1)}, u32[]{:S(2)}, u32[]{:S(2)}) collective-permute-start(bf16[12,128,128]{2,1,0:T(8,128)(2,1)S(1)} %get-tuple-element.50), channel_id=1, source_target_pairs={{0,24},{8,16},{16,8},{24,0},{1,25},{9,17},{17,9},{25,1},{2,26},{10... | collective-permute-start | bytes 1179656 | tf_op jit(solution)/shard_map/ppermute | solution.py:47
  29.7 17.2 %collective-permute-start.13 = (bf16[12,128,128]{2,1,0:T(8,128)(2,1)S(1)}, bf16[12,128,128]{2,1,0:T(8,128)(2,1)S(1)}, u32[]{:S(2)}, u32[]{:S(2)}) collective-permute-start(bf16[12,128,128]{2,1,0:T(8,128)(2,1)S(1)} %get-tuple-element.51), channel_id=1, source_target_pairs={{0,8},{8,0},{16,24},{24,16},{1,9},{9,1},{17,25},{25,17},{2,10},{10... | collective-permute-start | bytes 1179656 | tf_op jit(solution)/shard_map/ppermute | solution.py:47
  32.4 1.5 %collective-permute-start.6 = (bf16[2,5,64,128]{3,2,1,0:T(8,128)(2,1)S(1)}, bf16[2,5,64,128]{3,2,1,0:T(8,128)(2,1)S(1)}, u32[]{:S(2)}, u32[]{:S(2)}) collective-permute-start(bf16[2,5,64,128]{3,2,1,0:T(8,128)(2,1)S(1)} %get-tuple-element.43), channel_id=1, source_target_pairs={{0,1},{1,0},{2,3},{3,2},{4,5},{5,4},{6,7},{7,6},{8,9},{9,8},{10,11... | collective-permute-start | bytes 491528 | tf_op jit(solution)/shard_map/ppermute | solution.py:47
  33.9 7.0 %collective-permute-start.7 = (bf16[5,64,128]{2,1,0:T(8,128)(2,1)S(1)}, bf16[5,64,128]{2,1,0:T(8,128)(2,1)S(1)}, u32[]{:S(2)}, u32[]{:S(2)}) collective-permute-start(bf16[5,64,128]{2,1,0:T(8,128)(2,1)S(1)} %get-tuple-element.44), channel_id=1, source_target_pairs={{0,2},{1,3},{2,4},{3,5},{4,6},{5,7},{6,0},{7,1},{8,10},{9,11},{10,... | collective-permute-start | bytes 245768 | tf_op jit(solution)/shard_map/ppermute | solution.py:47
  35.5 8.4 %collective-permute-start.8 = (bf16[5,64,128]{2,1,0:T(8,128)(2,1)S(1)}, bf16[5,64,128]{2,1,0:T(8,128)(2,1)S(1)}, u32[]{:S(2)}, u32[]{:S(2)}) collective-permute-start(bf16[5,64,128]{2,1,0:T(8,128)(2,1)S(1)} %get-tuple-element.45), channel_id=1, source_target_pairs={{0,4},{1,5},{2,6},{3,7},{4,0},{5,1},{6,2},{7,3},{8,12},{9,13},{10,... | collective-permute-start | bytes 245768 | tf_op jit(solution)/shard_map/ppermute | solution.py:47
  40.9 4.7 %collective-permute-start.9 = (bf16[5,64,128]{2,1,0:T(8,128)(2,1)S(1)}, bf16[5,64,128]{2,1,0:T(8,128)(2,1)S(1)}, u32[]{:S(2)}, u32[]{:S(2)}) collective-permute-start(bf16[5,64,128]{2,1,0:T(8,128)(2,1)S(1)} %chip_states.7), channel_id=1, source_target_pairs={{0,6},{1,7},{2,0},{3,1},{4,2},{5,3},{6,4},{7,5},{8,14},{9,15},{10,... | collective-permute-start | bytes 245768 | tf_op jit(solution)/shard_map/ppermute | solution.py:47
  45.7 7.0 %collective-permute-start.10 = (bf16[2,5,64,128]{3,2,1,0:T(8,128)(2,1)S(1)}, bf16[2,5,64,128]{3,2,1,0:T(8,128)(2,1)S(1)}, u32[]{:S(2)}, u32[]{:S(2)}) collective-permute-start(bf16[2,5,64,128]{3,2,1,0:T(8,128)(2,1)S(1)} %get-tuple-element.47), channel_id=1, source_target_pairs={{0,1},{1,0},{2,3},{3,2},{4,5},{5,4},{6,7},{7,6},{8,9},{9,8},{10,11... | collective-permute-start | bytes 491528 | tf_op jit(solution)/shard_map/ppermute | solution.py:47
  47.3 3.6 %collective-permute-start.14 = (bf16[2,3,64,128]{3,2,1,0:T(8,128)(2,1)S(1)}, bf16[2,3,64,128]{3,2,1,0:T(8,128)(2,1)S(1)}, u32[]{:S(2)}, u32[]{:S(2)}) collective-permute-start(bf16[2,3,64,128]{3,2,1,0:T(8,128)(2,1)S(1)} %get-tuple-element.53), channel_id=1, source_target_pairs={{0,1},{1,0},{2,3},{3,2},{4,5},{5,4},{6,7},{7,6},{8,9},{9,8},{10,11... | collective-permute-start | bytes 294920 | tf_op jit(solution)/shard_map/ppermute | solution.py:47
  47.4 16.9 %collective-permute-start = (bf16[8,128,128]{2,1,0:T(8,128)(2,1)S(1)}, bf16[8,128,128]{2,1,0:T(8,128)(2,1)S(1)}, u32[]{:S(2)}, u32[]{:S(2)}) collective-permute-start(bf16[8,128,128]{2,1,0:T(8,128)(2,1)S(1)} %get-tuple-element.35), channel_id=1, source_target_pairs={{0,16},{8,24},{16,0},{24,8},{1,17},{9,25},{17,1},{25,9},{2,18},{10... | collective-permute-start | bytes 786440 | tf_op jit(solution)/shard_map/ppermute | solution.py:47
  49.3 15.0 %collective-permute-start.1 = (bf16[8,128,128]{2,1,0:T(8,128)(2,1)S(1)}, bf16[8,128,128]{2,1,0:T(8,128)(2,1)S(1)}, u32[]{:S(2)}, u32[]{:S(2)}) collective-permute-start(bf16[8,128,128]{2,1,0:T(8,128)(2,1)S(1)} %get-tuple-element.36), channel_id=1, source_target_pairs={{0,24},{8,16},{16,8},{24,0},{1,25},{9,17},{17,9},{25,1},{2,26},{10... | collective-permute-start | bytes 786440 | tf_op jit(solution)/shard_map/ppermute | solution.py:47
  50.5 13.8 %collective-permute-start.2 = (bf16[8,128,128]{2,1,0:T(8,128)(2,1)S(1)}, bf16[8,128,128]{2,1,0:T(8,128)(2,1)S(1)}, u32[]{:S(2)}, u32[]{:S(2)}) collective-permute-start(bf16[8,128,128]{2,1,0:T(8,128)(2,1)S(1)} %get-tuple-element.37), channel_id=1, source_target_pairs={{0,8},{8,0},{16,24},{24,16},{1,9},{9,1},{17,25},{25,17},{2,10},{10... | collective-permute-start | bytes 786440 | tf_op jit(solution)/shard_map/ppermute | solution.py:47
  51.0 8.7 %collective-permute-start.15 = (bf16[3,64,128]{2,1,0:T(8,128)(2,1)S(1)}, bf16[3,64,128]{2,1,0:T(8,128)(2,1)S(1)}, u32[]{:S(2)}, u32[]{:S(2)}) collective-permute-start(bf16[3,64,128]{2,1,0:T(8,128)(2,1)S(1)} %get-tuple-element.54), channel_id=1, source_target_pairs={{0,2},{1,3},{2,4},{3,5},{4,6},{5,7},{6,0},{7,1},{8,10},{9,11},{10,... | collective-permute-start | bytes 147464 | tf_op jit(solution)/shard_map/ppermute | solution.py:47
  52.8 8.6 %collective-permute-start.16 = (bf16[3,64,128]{2,1,0:T(8,128)(2,1)S(1)}, bf16[3,64,128]{2,1,0:T(8,128)(2,1)S(1)}, u32[]{:S(2)}, u32[]{:S(2)}) collective-permute-start(bf16[3,64,128]{2,1,0:T(8,128)(2,1)S(1)} %get-tuple-element.55), channel_id=1, source_target_pairs={{0,4},{1,5},{2,6},{3,7},{4,0},{5,1},{6,2},{7,3},{8,12},{9,13},{10,... | collective-permute-start | bytes 147464 | tf_op jit(solution)/shard_map/ppermute | solution.py:47
  59.8 4.3 %collective-permute-start.17 = (bf16[3,64,128]{2,1,0:T(8,128)(2,1)S(1)}, bf16[3,64,128]{2,1,0:T(8,128)(2,1)S(1)}, u32[]{:S(2)}, u32[]{:S(2)}) collective-permute-start(bf16[3,64,128]{2,1,0:T(8,128)(2,1)S(1)} %chip_states.10), channel_id=1, source_target_pairs={{0,6},{1,7},{2,0},{3,1},{4,2},{5,3},{6,4},{7,5},{8,14},{9,15},{10,... | collective-permute-start | bytes 147464 | tf_op jit(solution)/shard_map/ppermute | solution.py:47
  64.2 1.4 %collective-permute-start.18 = (bf16[2,3,64,128]{3,2,1,0:T(8,128)(2,1)S(1)}, bf16[2,3,64,128]{3,2,1,0:T(8,128)(2,1)S(1)}, u32[]{:S(2)}, u32[]{:S(2)}) collective-permute-start(bf16[2,3,64,128]{3,2,1,0:T(8,128)(2,1)S(1)} %get-tuple-element.58), channel_id=1, source_target_pairs={{0,1},{1,0},{2,3},{3,2},{4,5},{5,4},{6,7},{7,6},{8,9},{9,8},{10,11... | collective-permute-start | bytes 294920 | tf_op jit(solution)/shard_map/ppermute | solution.py:47

commit v5 on v4

--- a/solution.py
+++ b/solution.py
@@ -214,7 +214,7 @@
 
 
 def finish_kernel(chips, own, partner, *refs):
-    others, (mine, give) = refs[:-2], refs[-2:]
+    others, (mine, give) = refs[: chips - 1], refs[-2:]
     me = lax.axis_index("ctx")
     chip, core = me // 2, me % 2
     half = HD // 2
@@ -231,17 +231,19 @@
 
 
 @jax.named_scope("chip_states")
-def finished(own, partner, others):
+def finished(own, partner, others, before):
     _, heads, rows, _ = own.shape
     return pl.pallas_call(
         functools.partial(finish_kernel, len(others) + 1),
+        in_specs=[pl.BlockSpec(memory_space=pltpu.VMEM)] * (2 + len(others))
+        + [pl.BlockSpec(memory_space=pl.ANY)] * len(before),
         out_shape=[jax.ShapeDtypeStruct((2, heads, rows // 2, HD), BF16)] * 2,
         compiler_params=PARAMS,
         cost_estimate=cost(1000, 1024),
-    )(own, partner, *others)
-
-
-def exchanged(own, give, *before):
+    )(own, partner, *others, *before)
+
+
+def exchanged(own, give, before=(), last=()):
     spans = lax.axis_size("ctx")
     chips = spans // 2
     partner = send(give, "ctx", lambda index: index ^ 1)
@@ -250,7 +252,7 @@
         steps = list(range(first, min(first + 2, chips)))
         for step, value in zip(steps, chip_states(own, partner, chips, steps, others[-2:][:1] + list(before if others else ()))):
             others.append(send(value, "ctx", lambda index: (index + 2 * step) % spans))
-    mine, half = finished(own, partner, others)
+    mine, half = finished(own, partner, others, last)
     return mine, send(half, "ctx", lambda index: index ^ 1)
 
 
@@ -386,7 +388,7 @@
     received = [exchange(own, first)] + [exchange(values[0], values[1:]) for values in packed]
     early = exchanged(*own_states(received[0], chunks[0], late, []))
     *held, token = gradients([(received[0], early, 0, 0, chunks[0])], (), group, factor)
-    second = exchanged(*own_states(received[1], middle, 0, [early[0]]), token)
+    second = exchanged(*own_states(received[1], middle, 0, [early[0]]), [token], received[2][1:])
     *held, _ = gradients(
         [
             (received[2], early, chunks[0], heads - late, late),

time: 73.3 us -> 73.6 us (level)
  transfers between devices with their start and end apart: 19 -> 19, of which waited for: 8 -> 7; matrix products, arithmetic and copies ran while one was open for 0% -> 0% of each run, Pallas kernels for 11% -> 10%
where the time goes in v5:
time: 73.6 us; the launch traced here: 73.3 us
  waiting for transfers between devices  28.9 us (39%)
  starting transfers between devices  26.6 us (36%)
  Pallas kernels  16.8 us (23%)
  between operations  0.93 us (1%)
    ppermute x19, waiting for transfers between devices, send(): lax.ppermute(value, axis, [(index, target(index)) for index in range(coun...  28.9 us
    ppermute x19, starting transfers between devices, send(): lax.ppermute(value, axis, [(index, target(index)) for index in range(coun...  26.6 us
    pallas_call x2, Pallas kernels, gradients(): pl.pallas_call(functools.partial(grads_kernel, parts, factor, [item[2:] f...  11.6 us
    pallas_call x1, Pallas kernels, pack_rest(): pl.pallas_call(functools.partial(rest_kernel, parts, heads, chunks), in_s...  2.15 us
    pallas_call x1, Pallas kernels, pack_first(): pl.pallas_call(functools.partial(first_kernel, parts, heads, count, late)...  1.85 us
  transfers between devices with their start and end apart: 19, of which 7 were waited for; matrix products, arithmetic and copies ran while one was open for 0% of the time, Pallas kernels for 10%

profile of v5, /device:TPU:0, one launch (start us, length us, event | category | flops | bytes accessed | tf_op | source)
XLA Modules:
  0.0 73.3 jit_solution(4607704335348558696)
XLA Ops:
  0.6 1.9 %pack.3 = (bf16[16,128,128]{2,1,0:T(8,128)(2,1)S(1)}, bf16[16,128,128]{2,1,0:T(8,128)(2,1)S(1)}, bf16[16,128,128]{2,1,0:T(8,128)(2,1)S(1)}) custom-call(bf16[1,128,4096]{2,1,0:T(8,128)(2,1)} %refs_0_.3, bf16[1,128,4096]{2,1,0:T(8,128)(2,1)} %refs_1_.3, bf16[1,128,4096]{2,1,0:T(8,128)(2,1)} %refs_2_.3, bf16[1,128,4096]{2,1,0:T(8,128)(2,1)} %refs_3_.3), custom_call_target="tpu_custom_call" | custom-call | flops 1000 | bytes 2048 | tf_op jit(solution)/shard_map/pack/pallas_call | solution.py:92
  2.5 3.0 %collective-permute-start.3 = (bf16[16,128,128]{2,1,0:T(8,128)(2,1)S(1)}, bf16[16,128,128]{2,1,0:T(8,128)(2,1)S(1)}, u32[]{:S(2)}, u32[]{:S(2)}) collective-permute-start(bf16[16,128,128]{2,1,0:T(8,128)(2,1)S(1)} %get-tuple-element.39), channel_id=1, source_target_pairs={{0,16},{8,24},{16,0},{24,8},{1,17},{9,25},{17,1},{25,9},{2,18},{10... | collective-permute-start | bytes 1572872 | tf_op jit(solution)/shard_map/ppermute | solution.py:47
  5.5 1.4 %collective-permute-start.4 = (bf16[16,128,128]{2,1,0:T(8,128)(2,1)S(1)}, bf16[16,128,128]{2,1,0:T(8,128)(2,1)S(1)}, u32[]{:S(2)}, u32[]{:S(2)}) collective-permute-start(bf16[16,128,128]{2,1,0:T(8,128)(2,1)S(1)} %get-tuple-element.40), channel_id=1, source_target_pairs={{0,24},{8,16},{16,8},{24,0},{1,25},{9,17},{17,9},{25,1},{2,26},{10... | collective-permute-start | bytes 1572872 | tf_op jit(solution)/shard_map/ppermute | solution.py:47
  7.0 0.1 collective-permute-start.5
  7.1 2.1 %pack.2 = (bf16[16,128,128]{2,1,0:T(8,128)(2,1)S(1)}, bf16[12,128,128]{2,1,0:T(8,128)(2,1)S(1)}, bf16[12,128,128]{2,1,0:T(8,128)(2,1)S(1)}, bf16[12,128,128]{2,1...) custom-call(bf16[1,128,4096]{2,1,0:T(8,128)(2,1)} %refs_0_.3, ...), custom_call_target="tpu_custom_call" | custom-call | flops 1000 | bytes 2048 | tf_op jit(solution)/shard_map/pack/pallas_call | solution.py:135
  9.2 2.0 %collective-permute-start.11 = (bf16[12,128,128]{2,1,0:T(8,128)(2,1)S(1)}, bf16[12,128,128]{2,1,0:T(8,128)(2,1)S(1)}, u32[]{:S(2)}, u32[]{:S(2)}) collective-permute-start(bf16[12,128,128]{2,1,0:T(8,128)(2,1)S(1)} %get-tuple-element.49), channel_id=1, source_target_pairs={{0,16},{8,24},{16,0},{24,8},{1,17},{9,25},{17,1},{25,9},{2,18},{10... | collective-permute-start | bytes 1179656 | tf_op jit(solution)/shard_map/ppermute | solution.py:47
  11.2 1.5 %collective-permute-start.12 = (bf16[12,128,128]{2,1,0:T(8,128)(2,1)S(1)}, bf16[12,128,128]{2,1,0:T(8,128)(2,1)S(1)}, u32[]{:S(2)}, u32[]{:S(2)}) collective-permute-start(bf16[12,128,128]{2,1,0:T(8,128)(2,1)S(1)} %get-tuple-element.50), channel_id=1, source_target_pairs={{0,24},{8,16},{16,8},{24,0},{1,25},{9,17},{17,9},{25,1},{2,26},{10... | collective-permute-start | bytes 1179656 | tf_op jit(solution)/shard_map/ppermute | solution.py:47
  12.7 17.0 %collective-permute-done.3.refs_1_ = bf16[16,128,128]{2,1,0:T(8,128)(2,1)S(1)} collective-permute-done((bf16[16,128,128]{2,1,0:T(8,128)(2,1)S(1)}, bf16[16,128,128]{2,1,0:T(8,128)(2,1)S(1)}, u32[]{:S(2)}, u32[]{:S(2)}) %collective-permute-start.3) | collective-permute-done | bytes 524320 | tf_op jit(solution)/shard_map/ppermute | solution.py:47
  29.7 2.2 %collective-permute-start.13 = (bf16[12,128,128]{2,1,0:T(8,128)(2,1)S(1)}, bf16[12,128,128]{2,1,0:T(8,128)(2,1)S(1)}, u32[]{:S(2)}, u32[]{:S(2)}) collective-permute-start(bf16[12,128,128]{2,1,0:T(8,128)(2,1)S(1)} %get-tuple-element.51), channel_id=1, source_target_pairs={{0,8},{8,0},{16,24},{24,16},{1,9},{9,1},{17,25},{25,17},{2,10},{10... | collective-permute-start | bytes 1179656 | tf_op jit(solution)/shard_map/ppermute | solution.py:47
  31.9 0.4 own_states.2
  32.4 0.1 collective-permute-start.6
  32.4 1.4 %collective-permute-done.6.partner = bf16[2,5,64,128]{3,2,1,0:T(8,128)(2,1)S(1)} collective-permute-done((bf16[2,5,64,128]{3,2,1,0:T(8,128)(2,1)S(1)}, bf16[2,5,64,128]{3,2,1,0:T(8,128)(2,1)S(1)}, u32[]{:S(2)}, u32[]{:S(2)}) %collective-permute-start.6) | collective-permute-done | bytes 163872 | tf_op jit(solution)/shard_map/ppermute | solution.py:47
  33.9 1.6 %collective-permute-start.7 = (bf16[5,64,128]{2,1,0:T(8,128)(2,1)S(1)}, bf16[5,64,128]{2,1,0:T(8,128)(2,1)S(1)}, u32[]{:S(2)}, u32[]{:S(2)}) collective-permute-start(bf16[5,64,128]{2,1,0:T(8,128)(2,1)S(1)} %get-tuple-element.44), channel_id=1, source_target_pairs={{0,2},{1,3},{2,4},{3,5},{4,6},{5,7},{6,0},{7,1},{8,10},{9,11},{10,... | collective-permute-start | bytes 245768 | tf_op jit(solution)/shard_map/ppermute | solution.py:47
  35.5 2.6 %collective-permute-start.8 = (bf16[5,64,128]{2,1,0:T(8,128)(2,1)S(1)}, bf16[5,64,128]{2,1,0:T(8,128)(2,1)S(1)}, u32[]{:S(2)}, u32[]{:S(2)}) collective-permute-start(bf16[5,64,128]{2,1,0:T(8,128)(2,1)S(1)} %get-tuple-element.45), channel_id=1, source_target_pairs={{0,4},{1,5},{2,6},{3,7},{4,0},{5,1},{6,2},{7,3},{8,12},{9,13},{10,... | collective-permute-start | bytes 245768 | tf_op jit(solution)/shard_map/ppermute | solution.py:47
  38.1 2.7 %collective-permute-done.7.refs_0_ = bf16[5,64,128]{2,1,0:T(8,128)(2,1)S(1)} collective-permute-done((bf16[5,64,128]{2,1,0:T(8,128)(2,1)S(1)}, bf16[5,64,128]{2,1,0:T(8,128)(2,1)S(1)}, u32[]{:S(2)}, u32[]{:S(2)}) %collective-permute-start.7) | collective-permute-done | bytes 81952 | tf_op jit(solution)/shard_map/ppermute | solution.py:47
  40.9 1.8 %collective-permute-start.9 = (bf16[5,64,128]{2,1,0:T(8,128)(2,1)S(1)}, bf16[5,64,128]{2,1,0:T(8,128)(2,1)S(1)}, u32[]{:S(2)}, u32[]{:S(2)}) collective-permute-start(bf16[5,64,128]{2,1,0:T(8,128)(2,1)S(1)} %chip_states.7), channel_id=1, source_target_pairs={{0,6},{1,7},{2,0},{3,1},{4,2},{5,3},{6,4},{7,5},{8,14},{9,15},{10,... | collective-permute-start | bytes 245768 | tf_op jit(solution)/shard_map/ppermute | solution.py:47
  42.7 2.8 %collective-permute-done.11.refs_1_.refs_7_ = bf16[12,128,128]{2,1,0:T(8,128)(2,1)S(1)} collective-permute-done((bf16[12,128,128]{2,1,0:T(8,128)(2,1)S(1)}, bf16[12,128,128]{2,1,0:T(8,128)(2,1)S(1)}, u32[]{:S(2)}, u32[]{:S(2)}) %collective-permute-start.11) | collective-permute-done | bytes 393248 | tf_op jit(solution)/shard_map/ppermute | solution.py:47
  45.5 1.7 %collective-permute-start = (bf16[8,128,128]{2,1,0:T(8,128)(2,1)S(1)}, bf16[8,128,128]{2,1,0:T(8,128)(2,1)S(1)}, u32[]{:S(2)}, u32[]{:S(2)}) collective-permute-start(bf16[8,128,128]{2,1,0:T(8,128)(2,1)S(1)} %get-tuple-element.35), channel_id=1, source_target_pairs={{0,16},{8,24},{16,0},{24,8},{1,17},{9,25},{17,1},{25,9},{2,18},{10... | collective-permute-start | bytes 786440 | tf_op jit(solution)/shard_map/ppermute | solution.py:47
  47.3 1.4 %collective-permute-start.1 = (bf16[8,128,128]{2,1,0:T(8,128)(2,1)S(1)}, bf16[8,128,128]{2,1,0:T(8,128)(2,1)S(1)}, u32[]{:S(2)}, u32[]{:S(2)}) collective-permute-start(bf16[8,128,128]{2,1,0:T(8,128)(2,1)S(1)} %get-tuple-element.36), channel_id=1, source_target_pairs={{0,24},{8,16},{16,8},{24,0},{1,25},{9,17},{17,9},{25,1},{2,26},{10... | collective-permute-start | bytes 786440 | tf_op jit(solution)/shard_map/ppermute | solution.py:47
  48.7 0.3 collective-permute-start.2
  49.0 0.2 chip_states.8
  49.3 0.4 own_states.3
  49.7 0.6 collective-permute-start.14
  50.3 0.9 %collective-permute-done.14.partner = bf16[2,3,64,128]{3,2,1,0:T(8,128)(2,1)S(1)} collective-permute-done((bf16[2,3,64,128]{3,2,1,0:T(8,128)(2,1)S(1)}, bf16[2,3,64,128]{3,2,1,0:T(8,128)(2,1)S(1)}, u32[]{:S(2)}, u32[]{:S(2)}) %collective-permute-start.14) | collective-permute-done | bytes 98336 | tf_op jit(solution)/shard_map/ppermute | solution.py:47
  51.3 1.9 %collective-permute-start.15 = (bf16[3,64,128]{2,1,0:T(8,128)(2,1)S(1)}, bf16[3,64,128]{2,1,0:T(8,128)(2,1)S(1)}, u32[]{:S(2)}, u32[]{:S(2)}) collective-permute-start(bf16[3,64,128]{2,1,0:T(8,128)(2,1)S(1)} %get-tuple-element.54), channel_id=1, source_target_pairs={{0,2},{1,3},{2,4},{3,5},{4,6},{5,7},{6,0},{7,1},{8,10},{9,11},{10,... | collective-permute-start | bytes 147464 | tf_op jit(solution)/shard_map/ppermute | solution.py:47
  53.1 2.6 %collective-permute-start.16 = (bf16[3,64,128]{2,1,0:T(8,128)(2,1)S(1)}, bf16[3,64,128]{2,1,0:T(8,128)(2,1)S(1)}, u32[]{:S(2)}, u32[]{:S(2)}) collective-permute-start(bf16[3,64,128]{2,1,0:T(8,128)(2,1)S(1)} %get-tuple-element.55), channel_id=1, source_target_pairs={{0,4},{1,5},{2,6},{3,7},{4,0},{5,1},{6,2},{7,3},{8,12},{9,13},{10,... | collective-permute-start | bytes 147464 | tf_op jit(solution)/shard_map/ppermute | solution.py:47
  55.7 4.4 %gradients.2 = (bf16[1,512,1024]{2,1,0:T(8,128)(2,1)}, bf16[1,512,1024]{2,1,0:T(8,128)(2,1)}, bf16[1,512,1024]{2,1,0:T(8,128)(2,1)}, f32[8,128]{1,0:T(8,128)S(1)}) custom-call(bf16[16,128,128]{2,1,0:T(8,128)(2,1)S(1)} %get-tuple-element.38.refs_0_, bf16[16,128,128]{2,1,0:T(8,128)(2,1)S(1)} %collective-permute-done.3.refs_1_, ...), custom_call_target="tpu_custom_call" | custom-call | flops 1000 | bytes 2048 | tf_op jit(solution)/shard_map/gradients/pallas_call | solution.py:350
  60.1 1.6 %collective-permute-start.17 = (bf16[3,64,128]{2,1,0:T(8,128)(2,1)S(1)}, bf16[3,64,128]{2,1,0:T(8,128)(2,1)S(1)}, u32[]{:S(2)}, u32[]{:S(2)}) collective-permute-start(bf16[3,64,128]{2,1,0:T(8,128)(2,1)S(1)} %chip_states.10), channel_id=1, source_target_pairs={{0,6},{1,7},{2,0},{3,1},{4,2},{5,3},{6,4},{7,5},{8,14},{9,15},{10,... | collective-permute-start | bytes 147464 | tf_op jit(solution)/shard_map/ppermute | solution.py:47
  61.7 2.7 %collective-permute-done.17.refs_2_ = bf16[3,64,128]{2,1,0:T(8,128)(2,1)S(1)} collective-permute-done((bf16[3,64,128]{2,1,0:T(8,128)(2,1)S(1)}, bf16[3,64,128]{2,1,0:T(8,128)(2,1)S(1)}, u32[]{:S(2)}, u32[]{:S(2)}) %collective-permute-start.17) | collective-permute-done | bytes 49184 | tf_op jit(solution)/shard_map/ppermute | solution.py:47
  64.4 0.1 chip_states.11
  64.6 1.3 %collective-permute-done.18.refs_11_ = bf16[2,3,64,128]{3,2,1,0:T(8,128)(2,1)S(1)} collective-permute-done((bf16[2,3,64,128]{3,2,1,0:T(8,128)(2,1)S(1)}, bf16[2,3,64,128]{3,2,1,0:T(8,128)(2,1)S(1)}, u32[]{:S(2)}, u32[]{:S(2)}) %collective-permute-start.18) | collective-permute-done | bytes 98336 | tf_op jit(solution)/shard_map/ppermute | solution.py:47
  65.9 7.2 %gradients.3 = (bf16[1,512,1024]{2,1,0:T(8,128)(2,1)}, bf16[1,512,1024]{2,1,0:T(8,128)(2,1)}, bf16[1,512,1024]{2,1,0:T(8,128)(2,1)}, f32[8,128]{1,0:T(8,128)}) custom-call(bf16[8,128,128]{2,1,0:T(8,128)(2,1)S(1)} %get-tuple-element.34.refs_0_, ...), custom_call_target="tpu_custom_call", output_to_operand_aliasing={{0}: (12, {}), {1}: (13, {}), {2}: (14, {})} | custom-call | flops 1000 | bytes 2048 | tf_op jit(solution)/shard_map/gradients/pallas_call | solution.py:350
  (18 shorter events, 0.3 us)
Async XLA Ops:
  2.5 27.2 %collective-permute-start.3 = (bf16[16,128,128]{2,1,0:T(8,128)(2,1)S(1)}, bf16[16,128,128]{2,1,0:T(8,128)(2,1)S(1)}, u32[]{:S(2)}, u32[]{:S(2)}) collective-permute-start(bf16[16,128,128]{2,1,0:T(8,128)(2,1)S(1)} %get-tuple-element.39), channel_id=1, source_target_pairs={{0,16},{8,24},{16,0},{24,8},{1,17},{9,25},{17,1},{25,9},{2,18},{10... | collective-permute-start | bytes 1572872 | tf_op jit(solution)/shard_map/ppermute | solution.py:47
  5.5 26.4 %collective-permute-start.4 = (bf16[16,128,128]{2,1,0:T(8,128)(2,1)S(1)}, bf16[16,128,128]{2,1,0:T(8,128)(2,1)S(1)}, u32[]{:S(2)}, u32[]{:S(2)}) collective-permute-start(bf16[16,128,128]{2,1,0:T(8,128)(2,1)S(1)} %get-tuple-element.40), channel_id=1, source_target_pairs={{0,24},{8,16},{16,8},{24,0},{1,25},{9,17},{17,9},{25,1},{2,26},{10... | collective-permute-start | bytes 1572872 | tf_op jit(solution)/shard_map/ppermute | solution.py:47
  7.0 25.0 %collective-permute-start.5 = (bf16[16,128,128]{2,1,0:T(8,128)(2,1)S(1)}, bf16[16,128,128]{2,1,0:T(8,128)(2,1)S(1)}, u32[]{:S(2)}, u32[]{:S(2)}) collective-permute-start(bf16[16,128,128]{2,1,0:T(8,128)(2,1)S(1)} %get-tuple-element.41), channel_id=1, source_target_pairs={{0,8},{8,0},{16,24},{24,16},{1,9},{9,1},{17,25},{25,17},{2,10},{10... | collective-permute-start | bytes 1572872 | tf_op jit(solution)/shard_map/ppermute | solution.py:47
  9.2 36.3 %collective-permute-start.11 = (bf16[12,128,128]{2,1,0:T(8,128)(2,1)S(1)}, bf16[12,128,128]{2,1,0:T(8,128)(2,1)S(1)}, u32[]{:S(2)}, u32[]{:S(2)}) collective-permute-start(bf16[12,128,128]{2,1,0:T(8,128)(2,1)S(1)} %get-tuple-element.49), channel_id=1, source_target_pairs={{0,16},{8,24},{16,0},{24,8},{1,17},{9,25},{17,1},{25,9},{2,18},{10... | collective-permute-start | bytes 1179656 | tf_op jit(solution)/shard_map/ppermute | solution.py:47
  11.2 38.0 %collective-permute-start.12 = (bf16[12,128,128]{2,1,0:T(8,128)(2,1)S(1)}, bf16[12,128,128]{2,1,0:T(8,128)(2,1)S(1)}, u32[]{:S(2)}, u32[]{:S(2)}) collective-permute-start(bf16[12,128,128]{2,1,0:T(8,128)(2,1)S(1)} %get-tuple-element.50), channel_id=1, source_target_pairs={{0,24},{8,16},{16,8},{24,0},{1,25},{9,17},{17,9},{25,1},{2,26},{10... | collective-permute-start | bytes 1179656 | tf_op jit(solution)/shard_map/ppermute | solution.py:47
  29.7 19.6 %collective-permute-start.13 = (bf16[12,128,128]{2,1,0:T(8,128)(2,1)S(1)}, bf16[12,128,128]{2,1,0:T(8,128)(2,1)S(1)}, u32[]{:S(2)}, u32[]{:S(2)}) collective-permute-start(bf16[12,128,128]{2,1,0:T(8,128)(2,1)S(1)} %get-tuple-element.51), channel_id=1, source_target_pairs={{0,8},{8,0},{16,24},{24,16},{1,9},{9,1},{17,25},{25,17},{2,10},{10... | collective-permute-start | bytes 1179656 | tf_op jit(solution)/shard_map/ppermute | solution.py:47
  32.4 1.5 %collective-permute-start.6 = (bf16[2,5,64,128]{3,2,1,0:T(8,128)(2,1)S(1)}, bf16[2,5,64,128]{3,2,1,0:T(8,128)(2,1)S(1)}, u32[]{:S(2)}, u32[]{:S(2)}) collective-permute-start(bf16[2,5,64,128]{3,2,1,0:T(8,128)(2,1)S(1)} %get-tuple-element.43), channel_id=1, source_target_pairs={{0,1},{1,0},{2,3},{3,2},{4,5},{5,4},{6,7},{7,6},{8,9},{9,8},{10,11... | collective-permute-start | bytes 491528 | tf_op jit(solution)/shard_map/ppermute | solution.py:47
  33.9 7.0 %collective-permute-start.7 = (bf16[5,64,128]{2,1,0:T(8,128)(2,1)S(1)}, bf16[5,64,128]{2,1,0:T(8,128)(2,1)S(1)}, u32[]{:S(2)}, u32[]{:S(2)}) collective-permute-start(bf16[5,64,128]{2,1,0:T(8,128)(2,1)S(1)} %get-tuple-element.44), channel_id=1, source_target_pairs={{0,2},{1,3},{2,4},{3,5},{4,6},{5,7},{6,0},{7,1},{8,10},{9,11},{10,... | collective-permute-start | bytes 245768 | tf_op jit(solution)/shard_map/ppermute | solution.py:47
  35.5 11.7 %collective-permute-start.8 = (bf16[5,64,128]{2,1,0:T(8,128)(2,1)S(1)}, bf16[5,64,128]{2,1,0:T(8,128)(2,1)S(1)}, u32[]{:S(2)}, u32[]{:S(2)}) collective-permute-start(bf16[5,64,128]{2,1,0:T(8,128)(2,1)S(1)} %get-tuple-element.45), channel_id=1, source_target_pairs={{0,4},{1,5},{2,6},{3,7},{4,0},{5,1},{6,2},{7,3},{8,12},{9,13},{10,... | collective-permute-start | bytes 245768 | tf_op jit(solution)/shard_map/ppermute | solution.py:47
  40.9 7.8 %collective-permute-start.9 = (bf16[5,64,128]{2,1,0:T(8,128)(2,1)S(1)}, bf16[5,64,128]{2,1,0:T(8,128)(2,1)S(1)}, u32[]{:S(2)}, u32[]{:S(2)}) collective-permute-start(bf16[5,64,128]{2,1,0:T(8,128)(2,1)S(1)} %chip_states.7), channel_id=1, source_target_pairs={{0,6},{1,7},{2,0},{3,1},{4,2},{5,3},{6,4},{7,5},{8,14},{9,15},{10,... | collective-permute-start | bytes 245768 | tf_op jit(solution)/shard_map/ppermute | solution.py:47
  45.5 16.2 %collective-permute-start = (bf16[8,128,128]{2,1,0:T(8,128)(2,1)S(1)}, bf16[8,128,128]{2,1,0:T(8,128)(2,1)S(1)}, u32[]{:S(2)}, u32[]{:S(2)}) collective-permute-start(bf16[8,128,128]{2,1,0:T(8,128)(2,1)S(1)} %get-tuple-element.35), channel_id=1, source_target_pairs={{0,16},{8,24},{16,0},{24,8},{1,17},{9,25},{17,1},{25,9},{2,18},{10... | collective-permute-start | bytes 786440 | tf_op jit(solution)/shard_map/ppermute | solution.py:47
  47.3 14.4 %collective-permute-start.1 = (bf16[8,128,128]{2,1,0:T(8,128)(2,1)S(1)}, bf16[8,128,128]{2,1,0:T(8,128)(2,1)S(1)}, u32[]{:S(2)}, u32[]{:S(2)}) collective-permute-start(bf16[8,128,128]{2,1,0:T(8,128)(2,1)S(1)} %get-tuple-element.36), channel_id=1, source_target_pairs={{0,24},{8,16},{16,8},{24,0},{1,25},{9,17},{17,9},{25,1},{2,26},{10... | collective-permute-start | bytes 786440 | tf_op jit(solution)/shard_map/ppermute | solution.py:47
  48.7 13.0 %collective-permute-start.2 = (bf16[8,128,128]{2,1,0:T(8,128)(2,1)S(1)}, bf16[8,128,128]{2,1,0:T(8,128)(2,1)S(1)}, u32[]{:S(2)}, u32[]{:S(2)}) collective-permute-start(bf16[8,128,128]{2,1,0:T(8,128)(2,1)S(1)} %get-tuple-element.37), channel_id=1, source_target_pairs={{0,8},{8,0},{16,24},{24,16},{1,9},{9,1},{17,25},{25,17},{2,10},{10... | collective-permute-start | bytes 786440 | tf_op jit(solution)/shard_map/ppermute | solution.py:47
  49.2 3.9 %collective-permute-start.10 = (bf16[2,5,64,128]{3,2,1,0:T(8,128)(2,1)S(1)}, bf16[2,5,64,128]{3,2,1,0:T(8,128)(2,1)S(1)}, u32[]{:S(2)}, u32[]{:S(2)}) collective-permute-start(bf16[2,5,64,128]{3,2,1,0:T(8,128)(2,1)S(1)} %get-tuple-element.47), channel_id=1, source_target_pairs={{0,1},{1,0},{2,3},{3,2},{4,5},{5,4},{6,7},{7,6},{8,9},{9,8},{10,11... | collective-permute-start | bytes 491528 | tf_op jit(solution)/shard_map/ppermute | solution.py:47
  49.7 1.5 %collective-permute-start.14 = (bf16[2,3,64,128]{3,2,1,0:T(8,128)(2,1)S(1)}, bf16[2,3,64,128]{3,2,1,0:T(8,128)(2,1)S(1)}, u32[]{:S(2)}, u32[]{:S(2)}) collective-permute-start(bf16[2,3,64,128]{3,2,1,0:T(8,128)(2,1)S(1)} %get-tuple-element.53), channel_id=1, source_target_pairs={{0,1},{1,0},{2,3},{3,2},{4,5},{5,4},{6,7},{7,6},{8,9},{9,8},{10,11... | collective-permute-start | bytes 294920 | tf_op jit(solution)/shard_map/ppermute | solution.py:47
  51.3 8.8 %collective-permute-start.15 = (bf16[3,64,128]{2,1,0:T(8,128)(2,1)S(1)}, bf16[3,64,128]{2,1,0:T(8,128)(2,1)S(1)}, u32[]{:S(2)}, u32[]{:S(2)}) collective-permute-start(bf16[3,64,128]{2,1,0:T(8,128)(2,1)S(1)} %get-tuple-element.54), channel_id=1, source_target_pairs={{0,2},{1,3},{2,4},{3,5},{4,6},{5,7},{6,0},{7,1},{8,10},{9,11},{10,... | collective-permute-start | bytes 147464 | tf_op jit(solution)/shard_map/ppermute | solution.py:47
  53.1 8.6 %collective-permute-start.16 = (bf16[3,64,128]{2,1,0:T(8,128)(2,1)S(1)}, bf16[3,64,128]{2,1,0:T(8,128)(2,1)S(1)}, u32[]{:S(2)}, u32[]{:S(2)}) collective-permute-start(bf16[3,64,128]{2,1,0:T(8,128)(2,1)S(1)} %get-tuple-element.55), channel_id=1, source_target_pairs={{0,4},{1,5},{2,6},{3,7},{4,0},{5,1},{6,2},{7,3},{8,12},{9,13},{10,... | collective-permute-start | bytes 147464 | tf_op jit(solution)/shard_map/ppermute | solution.py:47
  60.1 4.3 %collective-permute-start.17 = (bf16[3,64,128]{2,1,0:T(8,128)(2,1)S(1)}, bf16[3,64,128]{2,1,0:T(8,128)(2,1)S(1)}, u32[]{:S(2)}, u32[]{:S(2)}) collective-permute-start(bf16[3,64,128]{2,1,0:T(8,128)(2,1)S(1)} %chip_states.10), channel_id=1, source_target_pairs={{0,6},{1,7},{2,0},{3,1},{4,2},{5,3},{6,4},{7,5},{8,14},{9,15},{10,... | collective-permute-start | bytes 147464 | tf_op jit(solution)/shard_map/ppermute | solution.py:47
  64.6 1.4 %collective-permute-start.18 = (bf16[2,3,64,128]{3,2,1,0:T(8,128)(2,1)S(1)}, bf16[2,3,64,128]{3,2,1,0:T(8,128)(2,1)S(1)}, u32[]{:S(2)}, u32[]{:S(2)}) collective-permute-start(bf16[2,3,64,128]{3,2,1,0:T(8,128)(2,1)S(1)} %get-tuple-element.58), channel_id=1, source_target_pairs={{0,1},{1,0},{2,3},{3,2},{4,5},{5,4},{6,7},{7,6},{8,9},{9,8},{10,11... | collective-permute-start | bytes 294920 | tf_op jit(solution)/shard_map/ppermute | solution.py:47

commit v6 on v5

--- a/solution.py
+++ b/solution.py
@@ -388,16 +388,9 @@
     received = [exchange(own, first)] + [exchange(values[0], values[1:]) for values in packed]
     early = exchanged(*own_states(received[0], chunks[0], late, []))
     *held, token = gradients([(received[0], early, 0, 0, chunks[0])], (), group, factor)
-    second = exchanged(*own_states(received[1], middle, 0, [early[0]]), [token], received[2][1:])
-    *held, _ = gradients(
-        [
-            (received[2], early, chunks[0], heads - late, late),
-            (received[1], second, 0, chunks[0], middle),
-        ],
-        held,
-        group,
-        factor,
-    )
+    *held, ready = gradients([(received[2], early, chunks[0], heads - late, late)], held, group, factor)
+    second = exchanged(*own_states(received[1], middle, 0, [early[0]]), [token], [ready])
+    *held, _ = gradients([(received[1], second, 0, chunks[0], middle)], held, group, factor)
     return tuple(held)
 
 

time: 73.6 us -> 71.9 us (0.977)
  waiting for transfers between devices: 28.9 us -> 26.4 us
  Pallas kernels: 16.8 us -> 17.8 us
    ppermute x19, waiting for transfers between devices: 28.9 us -> 26.4 us  [send(): lax.ppermute(value, axis, [(index, target(index)) for index in range(coun...]
    pallas_call x2 -> x3, Pallas kernels: 11.6 us -> 12.5 us  [gradients(): pl.pallas_call(functools.partial(grads_kernel, parts, factor, [item[2:] f...]
  transfers between devices with their start and end apart: 19 -> 19, of which waited for: 7 -> 6; matrix products, arithmetic and copies ran while one was open for 0% -> 0% of each run, Pallas kernels for 10% -> 15%
where the time goes in v6:
time: 71.9 us; the launch traced here: 71.6 us
  starting transfers between devices  26.4 us (37%)
  waiting for transfers between devices  26.4 us (37%)
  Pallas kernels  17.8 us (25%)
  between operations  0.94 us (1%)
    ppermute x19, starting transfers between devices, send(): lax.ppermute(value, axis, [(index, target(index)) for index in range(coun...  26.4 us
    ppermute x19, waiting for transfers between devices, send(): lax.ppermute(value, axis, [(index, target(index)) for index in range(coun...  26.4 us
    pallas_call x3, Pallas kernels, gradients(): pl.pallas_call(functools.partial(grads_kernel, parts, factor, [item[2:] f...  12.5 us
    pallas_call x1, Pallas kernels, pack_rest(): pl.pallas_call(functools.partial(rest_kernel, parts, heads, chunks), in_s...  2.15 us
    pallas_call x1, Pallas kernels, pack_first(): pl.pallas_call(functools.partial(first_kernel, parts, heads, count, late)...  1.85 us
  transfers between devices with their start and end apart: 19, of which 6 were waited for; matrix products, arithmetic and copies ran while one was open for 0% of the time, Pallas kernels for 15%

profile of v6, /device:TPU:0, one launch (start us, length us, event | category | flops | bytes accessed | tf_op | source)
XLA Modules:
  0.0 71.6 jit_solution(7652369483795887533)
XLA Ops:
  0.6 1.9 %pack.3 = (bf16[16,128,128]{2,1,0:T(8,128)(2,1)S(1)}, bf16[16,128,128]{2,1,0:T(8,128)(2,1)S(1)}, bf16[16,128,128]{2,1,0:T(8,128)(2,1)S(1)}) custom-call(bf16[1,128,4096]{2,1,0:T(8,128)(2,1)} %refs_0_.3, bf16[1,128,4096]{2,1,0:T(8,128)(2,1)} %refs_1_.3, bf16[1,128,4096]{2,1,0:T(8,128)(2,1)} %refs_2_.3, bf16[1,128,4096]{2,1,0:T(8,128)(2,1)} %refs_3_.3), custom_call_target="tpu_custom_call" | custom-call | flops 1000 | bytes 2048 | tf_op jit(solution)/shard_map/pack/pallas_call | solution.py:92
  2.5 3.0 %collective-permute-start.3 = (bf16[16,128,128]{2,1,0:T(8,128)(2,1)S(1)}, bf16[16,128,128]{2,1,0:T(8,128)(2,1)S(1)}, u32[]{:S(2)}, u32[]{:S(2)}) collective-permute-start(bf16[16,128,128]{2,1,0:T(8,128)(2,1)S(1)} %get-tuple-element.43), channel_id=1, source_target_pairs={{0,16},{8,24},{16,0},{24,8},{1,17},{9,25},{17,1},{25,9},{2,18},{10... | collective-permute-start | bytes 1572872 | tf_op jit(solution)/shard_map/ppermute | solution.py:47
  5.5 1.4 %collective-permute-start.4 = (bf16[16,128,128]{2,1,0:T(8,128)(2,1)S(1)}, bf16[16,128,128]{2,1,0:T(8,128)(2,1)S(1)}, u32[]{:S(2)}, u32[]{:S(2)}) collective-permute-start(bf16[16,128,128]{2,1,0:T(8,128)(2,1)S(1)} %get-tuple-element.44), channel_id=1, source_target_pairs={{0,24},{8,16},{16,8},{24,0},{1,25},{9,17},{17,9},{25,1},{2,26},{10... | collective-permute-start | bytes 1572872 | tf_op jit(solution)/shard_map/ppermute | solution.py:47
  7.0 0.1 collective-permute-start.5
  7.1 2.1 %pack.2 = (bf16[16,128,128]{2,1,0:T(8,128)(2,1)S(1)}, bf16[12,128,128]{2,1,0:T(8,128)(2,1)S(1)}, bf16[12,128,128]{2,1,0:T(8,128)(2,1)S(1)}, bf16[12,128,128]{2,1...) custom-call(bf16[1,128,4096]{2,1,0:T(8,128)(2,1)} %refs_0_.3, ...), custom_call_target="tpu_custom_call" | custom-call | flops 1000 | bytes 2048 | tf_op jit(solution)/shard_map/pack/pallas_call | solution.py:135
  9.2 2.0 %collective-permute-start = (bf16[12,128,128]{2,1,0:T(8,128)(2,1)S(1)}, bf16[12,128,128]{2,1,0:T(8,128)(2,1)S(1)}, u32[]{:S(2)}, u32[]{:S(2)}) collective-permute-start(bf16[12,128,128]{2,1,0:T(8,128)(2,1)S(1)} %get-tuple-element.39), channel_id=1, source_target_pairs={{0,16},{8,24},{16,0},{24,8},{1,17},{9,25},{17,1},{25,9},{2,18},{10... | collective-permute-start | bytes 1179656 | tf_op jit(solution)/shard_map/ppermute | solution.py:47
  11.2 1.5 %collective-permute-start.1 = (bf16[12,128,128]{2,1,0:T(8,128)(2,1)S(1)}, bf16[12,128,128]{2,1,0:T(8,128)(2,1)S(1)}, u32[]{:S(2)}, u32[]{:S(2)}) collective-permute-start(bf16[12,128,128]{2,1,0:T(8,128)(2,1)S(1)} %get-tuple-element.40), channel_id=1, source_target_pairs={{0,24},{8,16},{16,8},{24,0},{1,25},{9,17},{17,9},{25,1},{2,26},{10... | collective-permute-start | bytes 1179656 | tf_op jit(solution)/shard_map/ppermute | solution.py:47
  12.7 17.0 %collective-permute-done.3.refs_1_ = bf16[16,128,128]{2,1,0:T(8,128)(2,1)S(1)} collective-permute-done((bf16[16,128,128]{2,1,0:T(8,128)(2,1)S(1)}, bf16[16,128,128]{2,1,0:T(8,128)(2,1)S(1)}, u32[]{:S(2)}, u32[]{:S(2)}) %collective-permute-start.3) | collective-permute-done | bytes 524320 | tf_op jit(solution)/shard_map/ppermute | solution.py:47
  29.7 1.4 %collective-permute-done.5.refs_3_ = bf16[16,128,128]{2,1,0:T(8,128)(2,1)S(1)} collective-permute-done((bf16[16,128,128]{2,1,0:T(8,128)(2,1)S(1)}, bf16[16,128,128]{2,1,0:T(8,128)(2,1)S(1)}, u32[]{:S(2)}, u32[]{:S(2)}) %collective-permute-start.5) | collective-permute-done | bytes 524320 | tf_op jit(solution)/shard_map/ppermute | solution.py:47
  31.1 0.4 own_states.2
  31.6 2.0 %collective-permute-start.2 = (bf16[12,128,128]{2,1,0:T(8,128)(2,1)S(1)}, bf16[12,128,128]{2,1,0:T(8,128)(2,1)S(1)}, u32[]{:S(2)}, u32[]{:S(2)}) collective-permute-start(bf16[12,128,128]{2,1,0:T(8,128)(2,1)S(1)} %get-tuple-element.41), channel_id=1, source_target_pairs={{0,8},{8,0},{16,24},{24,16},{1,9},{9,1},{17,25},{25,17},{2,10},{10... | collective-permute-start | bytes 1179656 | tf_op jit(solution)/shard_map/ppermute | solution.py:47
  33.7 1.6 %collective-permute-start.7 = (bf16[5,64,128]{2,1,0:T(8,128)(2,1)S(1)}, bf16[5,64,128]{2,1,0:T(8,128)(2,1)S(1)}, u32[]{:S(2)}, u32[]{:S(2)}) collective-permute-start(bf16[5,64,128]{2,1,0:T(8,128)(2,1)S(1)} %get-tuple-element.48), channel_id=1, source_target_pairs={{0,2},{1,3},{2,4},{3,5},{4,6},{5,7},{6,0},{7,1},{8,10},{9,11},{10,... | collective-permute-start | bytes 245768 | tf_op jit(solution)/shard_map/ppermute | solution.py:47
  35.3 2.6 %collective-permute-start.8 = (bf16[5,64,128]{2,1,0:T(8,128)(2,1)S(1)}, bf16[5,64,128]{2,1,0:T(8,128)(2,1)S(1)}, u32[]{:S(2)}, u32[]{:S(2)}) collective-permute-start(bf16[5,64,128]{2,1,0:T(8,128)(2,1)S(1)} %get-tuple-element.49), channel_id=1, source_target_pairs={{0,4},{1,5},{2,6},{3,7},{4,0},{5,1},{6,2},{7,3},{8,12},{9,13},{10,... | collective-permute-start | bytes 245768 | tf_op jit(solution)/shard_map/ppermute | solution.py:47
  37.9 2.8 %collective-permute-done.7.refs_0_ = bf16[5,64,128]{2,1,0:T(8,128)(2,1)S(1)} collective-permute-done((bf16[5,64,128]{2,1,0:T(8,128)(2,1)S(1)}, bf16[5,64,128]{2,1,0:T(8,128)(2,1)S(1)}, u32[]{:S(2)}, u32[]{:S(2)}) %collective-permute-start.7) | collective-permute-done | bytes 81952 | tf_op jit(solution)/shard_map/ppermute | solution.py:47
  40.7 1.8 %collective-permute-start.9 = (bf16[5,64,128]{2,1,0:T(8,128)(2,1)S(1)}, bf16[5,64,128]{2,1,0:T(8,128)(2,1)S(1)}, u32[]{:S(2)}, u32[]{:S(2)}) collective-permute-start(bf16[5,64,128]{2,1,0:T(8,128)(2,1)S(1)} %chip_states.7), channel_id=1, source_target_pairs={{0,6},{1,7},{2,0},{3,1},{4,2},{5,3},{6,4},{7,5},{8,14},{9,15},{10,... | collective-permute-start | bytes 245768 | tf_op jit(solution)/shard_map/ppermute | solution.py:47
  42.6 3.0 %collective-permute-done.refs_1_ = bf16[12,128,128]{2,1,0:T(8,128)(2,1)S(1)} collective-permute-done((bf16[12,128,128]{2,1,0:T(8,128)(2,1)S(1)}, bf16[12,128,128]{2,1,0:T(8,128)(2,1)S(1)}, u32[]{:S(2)}, u32[]{:S(2)}) %collective-permute-start) | collective-permute-done | bytes 393248 | tf_op jit(solution)/shard_map/ppermute | solution.py:47
  45.5 1.7 %collective-permute-start.15 = (bf16[8,128,128]{2,1,0:T(8,128)(2,1)S(1)}, bf16[8,128,128]{2,1,0:T(8,128)(2,1)S(1)}, u32[]{:S(2)}, u32[]{:S(2)}) collective-permute-start(bf16[8,128,128]{2,1,0:T(8,128)(2,1)S(1)} %get-tuple-element.58), channel_id=1, source_target_pairs={{0,16},{8,24},{16,0},{24,8},{1,17},{9,25},{17,1},{25,9},{2,18},{10... | collective-permute-start | bytes 786440 | tf_op jit(solution)/shard_map/ppermute | solution.py:47
  47.3 1.4 %collective-permute-start.16 = (bf16[8,128,128]{2,1,0:T(8,128)(2,1)S(1)}, bf16[8,128,128]{2,1,0:T(8,128)(2,1)S(1)}, u32[]{:S(2)}, u32[]{:S(2)}) collective-permute-start(bf16[8,128,128]{2,1,0:T(8,128)(2,1)S(1)} %get-tuple-element.59), channel_id=1, source_target_pairs={{0,24},{8,16},{16,8},{24,0},{1,25},{9,17},{17,9},{25,1},{2,26},{10... | collective-permute-start | bytes 786440 | tf_op jit(solution)/shard_map/ppermute | solution.py:47
  48.7 0.3 collective-permute-start.17
  49.0 0.2 chip_states.8
  49.3 0.4 own_states.3
  49.7 0.6 collective-permute-start.10
  50.3 0.9 %collective-permute-done.10.partner = bf16[2,3,64,128]{3,2,1,0:T(8,128)(2,1)S(1)} collective-permute-done((bf16[2,3,64,128]{3,2,1,0:T(8,128)(2,1)S(1)}, bf16[2,3,64,128]{3,2,1,0:T(8,128)(2,1)S(1)}, u32[]{:S(2)}, u32[]{:S(2)}) %collective-permute-start.10) | collective-permute-done | bytes 98336 | tf_op jit(solution)/shard_map/ppermute | solution.py:47
  51.3 1.9 %collective-permute-start.11 = (bf16[3,64,128]{2,1,0:T(8,128)(2,1)S(1)}, bf16[3,64,128]{2,1,0:T(8,128)(2,1)S(1)}, u32[]{:S(2)}, u32[]{:S(2)}) collective-permute-start(bf16[3,64,128]{2,1,0:T(8,128)(2,1)S(1)} %get-tuple-element.53), channel_id=1, source_target_pairs={{0,2},{1,3},{2,4},{3,5},{4,6},{5,7},{6,0},{7,1},{8,10},{9,11},{10,... | collective-permute-start | bytes 147464 | tf_op jit(solution)/shard_map/ppermute | solution.py:47
  53.1 2.6 %collective-permute-start.12 = (bf16[3,64,128]{2,1,0:T(8,128)(2,1)S(1)}, bf16[3,64,128]{2,1,0:T(8,128)(2,1)S(1)}, u32[]{:S(2)}, u32[]{:S(2)}) collective-permute-start(bf16[3,64,128]{2,1,0:T(8,128)(2,1)S(1)} %get-tuple-element.54), channel_id=1, source_target_pairs={{0,4},{1,5},{2,6},{3,7},{4,0},{5,1},{6,2},{7,3},{8,12},{9,13},{10,... | collective-permute-start | bytes 147464 | tf_op jit(solution)/shard_map/ppermute | solution.py:47
  55.7 4.4 %gradients.3 = (bf16[1,512,1024]{2,1,0:T(8,128)(2,1)}, bf16[1,512,1024]{2,1,0:T(8,128)(2,1)}, bf16[1,512,1024]{2,1,0:T(8,128)(2,1)}, f32[8,128]{1,0:T(8,128)S(1)}) custom-call(bf16[16,128,128]{2,1,0:T(8,128)(2,1)S(1)} %get-tuple-element.42.refs_0_, bf16[16,128,128]{2,1,0:T(8,128)(2,1)S(1)} %collective-permute-done.3.refs_1_, ...), custom_call_target="tpu_custom_call" | custom-call | flops 1000 | bytes 2048 | tf_op jit(solution)/shard_map/gradients/pallas_call | solution.py:350
  60.1 1.6 %collective-permute-start.14 = (bf16[3,64,128]{2,1,0:T(8,128)(2,1)S(1)}, bf16[3,64,128]{2,1,0:T(8,128)(2,1)S(1)}, u32[]{:S(2)}, u32[]{:S(2)}) collective-permute-start(bf16[3,64,128]{2,1,0:T(8,128)(2,1)S(1)} %chip_states.10), channel_id=1, source_target_pairs={{0,6},{1,7},{2,0},{3,1},{4,2},{5,3},{6,4},{7,5},{8,14},{9,15},{10,... | collective-permute-start | bytes 147464 | tf_op jit(solution)/shard_map/ppermute | solution.py:47
  61.7 3.2 %gradients.4 = (bf16[1,512,1024]{2,1,0:T(8,128)(2,1)}, bf16[1,512,1024]{2,1,0:T(8,128)(2,1)}, bf16[1,512,1024]{2,1,0:T(8,128)(2,1)}, f32[8,128]{1,0:T(8,128)S(1)}) custom-call(bf16[8,128,128]{2,1,0:T(8,128)(2,1)S(1)} %get-tuple-element.57.refs_0_, ...), custom_call_target="tpu_custom_call", output_to_operand_aliasing={{0}: (6, {}), {1}: (7, {}), {2}: (8, {})} | custom-call | flops 1000 | bytes 2048 | tf_op jit(solution)/shard_map/gradients/pallas_call | solution.py:350
  65.0 0.1 chip_states.11
  65.1 0.1 collective-permute-start.18
  65.2 1.3 %collective-permute-done.18.refs_5_ = bf16[2,3,64,128]{3,2,1,0:T(8,128)(2,1)S(1)} collective-permute-done((bf16[2,3,64,128]{3,2,1,0:T(8,128)(2,1)S(1)}, bf16[2,3,64,128]{3,2,1,0:T(8,128)(2,1)S(1)}, u32[]{:S(2)}, u32[]{:S(2)}) %collective-permute-start.18) | collective-permute-done | bytes 98336 | tf_op jit(solution)/shard_map/ppermute | solution.py:47
  66.5 5.0 %gradients.5 = (bf16[1,512,1024]{2,1,0:T(8,128)(2,1)}, bf16[1,512,1024]{2,1,0:T(8,128)(2,1)}, bf16[1,512,1024]{2,1,0:T(8,128)(2,1)}, f32[8,128]{1,0:T(8,128)}) custom-call(bf16[12,128,128]{2,1,0:T(8,128)(2,1)S(1)} %get-tuple-element.38.refs_0_, ...), custom_call_target="tpu_custom_call", output_to_operand_aliasing={{0}: (6, {}), {1}: (7, {}), {2}: (8, {})} | custom-call | flops 1000 | bytes 2048 | tf_op jit(solution)/shard_map/gradients/pallas_call | solution.py:350
  (19 shorter events, 0.3 us)
Async XLA Ops:
  2.5 27.2 %collective-permute-start.3 = (bf16[16,128,128]{2,1,0:T(8,128)(2,1)S(1)}, bf16[16,128,128]{2,1,0:T(8,128)(2,1)S(1)}, u32[]{:S(2)}, u32[]{:S(2)}) collective-permute-start(bf16[16,128,128]{2,1,0:T(8,128)(2,1)S(1)} %get-tuple-element.43), channel_id=1, source_target_pairs={{0,16},{8,24},{16,0},{24,8},{1,17},{9,25},{17,1},{25,9},{2,18},{10... | collective-permute-start | bytes 1572872 | tf_op jit(solution)/shard_map/ppermute | solution.py:47
  5.5 24.2 %collective-permute-start.4 = (bf16[16,128,128]{2,1,0:T(8,128)(2,1)S(1)}, bf16[16,128,128]{2,1,0:T(8,128)(2,1)S(1)}, u32[]{:S(2)}, u32[]{:S(2)}) collective-permute-start(bf16[16,128,128]{2,1,0:T(8,128)(2,1)S(1)} %get-tuple-element.44), channel_id=1, source_target_pairs={{0,24},{8,16},{16,8},{24,0},{1,25},{9,17},{17,9},{25,1},{2,26},{10... | collective-permute-start | bytes 1572872 | tf_op jit(solution)/shard_map/ppermute | solution.py:47
  7.0 24.1 %collective-permute-start.5 = (bf16[16,128,128]{2,1,0:T(8,128)(2,1)S(1)}, bf16[16,128,128]{2,1,0:T(8,128)(2,1)S(1)}, u32[]{:S(2)}, u32[]{:S(2)}) collective-permute-start(bf16[16,128,128]{2,1,0:T(8,128)(2,1)S(1)} %get-tuple-element.45), channel_id=1, source_target_pairs={{0,8},{8,0},{16,24},{24,16},{1,9},{9,1},{17,25},{25,17},{2,10},{10... | collective-permute-start | bytes 1572872 | tf_op jit(solution)/shard_map/ppermute | solution.py:47
  9.2 36.3 %collective-permute-start = (bf16[12,128,128]{2,1,0:T(8,128)(2,1)S(1)}, bf16[12,128,128]{2,1,0:T(8,128)(2,1)S(1)}, u32[]{:S(2)}, u32[]{:S(2)}) collective-permute-start(bf16[12,128,128]{2,1,0:T(8,128)(2,1)S(1)} %get-tuple-element.39), channel_id=1, source_target_pairs={{0,16},{8,24},{16,0},{24,8},{1,17},{9,25},{17,1},{25,9},{2,18},{10... | collective-permute-start | bytes 1179656 | tf_op jit(solution)/shard_map/ppermute | solution.py:47
  11.2 38.0 %collective-permute-start.1 = (bf16[12,128,128]{2,1,0:T(8,128)(2,1)S(1)}, bf16[12,128,128]{2,1,0:T(8,128)(2,1)S(1)}, u32[]{:S(2)}, u32[]{:S(2)}) collective-permute-start(bf16[12,128,128]{2,1,0:T(8,128)(2,1)S(1)} %get-tuple-element.40), channel_id=1, source_target_pairs={{0,24},{8,16},{16,8},{24,0},{1,25},{9,17},{17,9},{25,1},{2,26},{10... | collective-permute-start | bytes 1179656 | tf_op jit(solution)/shard_map/ppermute | solution.py:47
  31.5 2.1 %collective-permute-start.6 = (bf16[2,5,64,128]{3,2,1,0:T(8,128)(2,1)S(1)}, bf16[2,5,64,128]{3,2,1,0:T(8,128)(2,1)S(1)}, u32[]{:S(2)}, u32[]{:S(2)}) collective-permute-start(bf16[2,5,64,128]{3,2,1,0:T(8,128)(2,1)S(1)} %get-tuple-element.47), channel_id=1, source_target_pairs={{0,1},{1,0},{2,3},{3,2},{4,5},{5,4},{6,7},{7,6},{8,9},{9,8},{10,11... | collective-permute-start | bytes 491528 | tf_op jit(solution)/shard_map/ppermute | solution.py:47
  31.6 17.7 %collective-permute-start.2 = (bf16[12,128,128]{2,1,0:T(8,128)(2,1)S(1)}, bf16[12,128,128]{2,1,0:T(8,128)(2,1)S(1)}, u32[]{:S(2)}, u32[]{:S(2)}) collective-permute-start(bf16[12,128,128]{2,1,0:T(8,128)(2,1)S(1)} %get-tuple-element.41), channel_id=1, source_target_pairs={{0,8},{8,0},{16,24},{24,16},{1,9},{9,1},{17,25},{25,17},{2,10},{10... | collective-permute-start | bytes 1179656 | tf_op jit(solution)/shard_map/ppermute | solution.py:47
  33.7 7.0 %collective-permute-start.7 = (bf16[5,64,128]{2,1,0:T(8,128)(2,1)S(1)}, bf16[5,64,128]{2,1,0:T(8,128)(2,1)S(1)}, u32[]{:S(2)}, u32[]{:S(2)}) collective-permute-start(bf16[5,64,128]{2,1,0:T(8,128)(2,1)S(1)} %get-tuple-element.48), channel_id=1, source_target_pairs={{0,2},{1,3},{2,4},{3,5},{4,6},{5,7},{6,0},{7,1},{8,10},{9,11},{10,... | collective-permute-start | bytes 245768 | tf_op jit(solution)/shard_map/ppermute | solution.py:47
  35.3 12.0 %collective-permute-start.8 = (bf16[5,64,128]{2,1,0:T(8,128)(2,1)S(1)}, bf16[5,64,128]{2,1,0:T(8,128)(2,1)S(1)}, u32[]{:S(2)}, u32[]{:S(2)}) collective-permute-start(bf16[5,64,128]{2,1,0:T(8,128)(2,1)S(1)} %get-tuple-element.49), channel_id=1, source_target_pairs={{0,4},{1,5},{2,6},{3,7},{4,0},{5,1},{6,2},{7,3},{8,12},{9,13},{10,... | collective-permute-start | bytes 245768 | tf_op jit(solution)/shard_map/ppermute | solution.py:47
  40.7 8.0 %collective-permute-start.9 = (bf16[5,64,128]{2,1,0:T(8,128)(2,1)S(1)}, bf16[5,64,128]{2,1,0:T(8,128)(2,1)S(1)}, u32[]{:S(2)}, u32[]{:S(2)}) collective-permute-start(bf16[5,64,128]{2,1,0:T(8,128)(2,1)S(1)} %chip_states.7), channel_id=1, source_target_pairs={{0,6},{1,7},{2,0},{3,1},{4,2},{5,3},{6,4},{7,5},{8,14},{9,15},{10,... | collective-permute-start | bytes 245768 | tf_op jit(solution)/shard_map/ppermute | solution.py:47
  45.5 16.2 %collective-permute-start.15 = (bf16[8,128,128]{2,1,0:T(8,128)(2,1)S(1)}, bf16[8,128,128]{2,1,0:T(8,128)(2,1)S(1)}, u32[]{:S(2)}, u32[]{:S(2)}) collective-permute-start(bf16[8,128,128]{2,1,0:T(8,128)(2,1)S(1)} %get-tuple-element.58), channel_id=1, source_target_pairs={{0,16},{8,24},{16,0},{24,8},{1,17},{9,25},{17,1},{25,9},{2,18},{10... | collective-permute-start | bytes 786440 | tf_op jit(solution)/shard_map/ppermute | solution.py:47
  47.3 14.4 %collective-permute-start.16 = (bf16[8,128,128]{2,1,0:T(8,128)(2,1)S(1)}, bf16[8,128,128]{2,1,0:T(8,128)(2,1)S(1)}, u32[]{:S(2)}, u32[]{:S(2)}) collective-permute-start(bf16[8,128,128]{2,1,0:T(8,128)(2,1)S(1)} %get-tuple-element.59), channel_id=1, source_target_pairs={{0,24},{8,16},{16,8},{24,0},{1,25},{9,17},{17,9},{25,1},{2,26},{10... | collective-permute-start | bytes 786440 | tf_op jit(solution)/shard_map/ppermute | solution.py:47
  48.7 13.0 %collective-permute-start.17 = (bf16[8,128,128]{2,1,0:T(8,128)(2,1)S(1)}, bf16[8,128,128]{2,1,0:T(8,128)(2,1)S(1)}, u32[]{:S(2)}, u32[]{:S(2)}) collective-permute-start(bf16[8,128,128]{2,1,0:T(8,128)(2,1)S(1)} %get-tuple-element.60), channel_id=1, source_target_pairs={{0,8},{8,0},{16,24},{24,16},{1,9},{9,1},{17,25},{25,17},{2,10},{10... | collective-permute-start | bytes 786440 | tf_op jit(solution)/shard_map/ppermute | solution.py:47
  49.2 3.9 %collective-permute-start.13 = (bf16[2,5,64,128]{3,2,1,0:T(8,128)(2,1)S(1)}, bf16[2,5,64,128]{3,2,1,0:T(8,128)(2,1)S(1)}, u32[]{:S(2)}, u32[]{:S(2)}) collective-permute-start(bf16[2,5,64,128]{3,2,1,0:T(8,128)(2,1)S(1)} %get-tuple-element.55), channel_id=1, source_target_pairs={{0,1},{1,0},{2,3},{3,2},{4,5},{5,4},{6,7},{7,6},{8,9},{9,8},{10,11... | collective-permute-start | bytes 491528 | tf_op jit(solution)/shard_map/ppermute | solution.py:47
  49.7 1.5 %collective-permute-start.10 = (bf16[2,3,64,128]{3,2,1,0:T(8,128)(2,1)S(1)}, bf16[2,3,64,128]{3,2,1,0:T(8,128)(2,1)S(1)}, u32[]{:S(2)}, u32[]{:S(2)}) collective-permute-start(bf16[2,3,64,128]{3,2,1,0:T(8,128)(2,1)S(1)} %get-tuple-element.52), channel_id=1, source_target_pairs={{0,1},{1,0},{2,3},{3,2},{4,5},{5,4},{6,7},{7,6},{8,9},{9,8},{10,11... | collective-permute-start | bytes 294920 | tf_op jit(solution)/shard_map/ppermute | solution.py:47
  51.3 8.8 %collective-permute-start.11 = (bf16[3,64,128]{2,1,0:T(8,128)(2,1)S(1)}, bf16[3,64,128]{2,1,0:T(8,128)(2,1)S(1)}, u32[]{:S(2)}, u32[]{:S(2)}) collective-permute-start(bf16[3,64,128]{2,1,0:T(8,128)(2,1)S(1)} %get-tuple-element.53), channel_id=1, source_target_pairs={{0,2},{1,3},{2,4},{3,5},{4,6},{5,7},{6,0},{7,1},{8,10},{9,11},{10,... | collective-permute-start | bytes 147464 | tf_op jit(solution)/shard_map/ppermute | solution.py:47
  53.1 11.8 %collective-permute-start.12 = (bf16[3,64,128]{2,1,0:T(8,128)(2,1)S(1)}, bf16[3,64,128]{2,1,0:T(8,128)(2,1)S(1)}, u32[]{:S(2)}, u32[]{:S(2)}) collective-permute-start(bf16[3,64,128]{2,1,0:T(8,128)(2,1)S(1)} %get-tuple-element.54), channel_id=1, source_target_pairs={{0,4},{1,5},{2,6},{3,7},{4,0},{5,1},{6,2},{7,3},{8,12},{9,13},{10,... | collective-permute-start | bytes 147464 | tf_op jit(solution)/shard_map/ppermute | solution.py:47
  60.1 4.8 %collective-permute-start.14 = (bf16[3,64,128]{2,1,0:T(8,128)(2,1)S(1)}, bf16[3,64,128]{2,1,0:T(8,128)(2,1)S(1)}, u32[]{:S(2)}, u32[]{:S(2)}) collective-permute-start(bf16[3,64,128]{2,1,0:T(8,128)(2,1)S(1)} %chip_states.10), channel_id=1, source_target_pairs={{0,6},{1,7},{2,0},{3,1},{4,2},{5,3},{6,4},{7,5},{8,14},{9,15},{10,... | collective-permute-start | bytes 147464 | tf_op jit(solution)/shard_map/ppermute | solution.py:47
  65.1 1.4 %collective-permute-start.18 = (bf16[2,3,64,128]{3,2,1,0:T(8,128)(2,1)S(1)}, bf16[2,3,64,128]{3,2,1,0:T(8,128)(2,1)S(1)}, u32[]{:S(2)}, u32[]{:S(2)}) collective-permute-start(bf16[2,3,64,128]{3,2,1,0:T(8,128)(2,1)S(1)} %get-tuple-element.66), channel_id=1, source_target_pairs={{0,1},{1,0},{2,3},{3,2},{4,5},{5,4},{6,7},{7,6},{8,9},{9,8},{10,11... | collective-permute-start | bytes 294920 | tf_op jit(solution)/shard_map/ppermute | solution.py:47

commit v7 on v6

--- a/solution.py
+++ b/solution.py
@@ -189,71 +189,80 @@
     )(*received, *before)
 
 
-def pick_kernel(chips, steps, own, partner, *refs):
-    outputs = refs[-len(steps) :]
+def own_half(own, state):
+    half = HD // 2
+    first = lax.axis_index("ctx") % 2 == 0
+    return jnp.where(first, own[state, :, :half], own[state, :, half:])
+
+
+def group_kernel(bit, final, arrived, own, partner, *refs):
+    others, out = refs[:arrived], refs[-1]
+    chip = lax.axis_index("ctx") // 2
+    totals = [
+        own_half(own, state) + partner[state].astype(F32) + sum(ref[state].astype(F32) for ref in others)
+        for state in range(2)
+    ]
+    if final:
+        out[...] = jnp.where(chip & bit == 0, *totals).astype(BF16)
+    else:
+        for state in range(2):
+            out[state] = totals[state].astype(BF16)
+
+
+@jax.named_scope("chip_states")
+def group_states(own, partner, others, bit, final, before):
+    arrays = (own, partner, *others)
+    shape = partner.shape[1:] if final else partner.shape
+    return pl.pallas_call(
+        functools.partial(group_kernel, bit, final, len(others)),
+        in_specs=[pl.BlockSpec(memory_space=pltpu.VMEM)] * len(arrays)
+        + [pl.BlockSpec(memory_space=pl.ANY)] * len(before),
+        out_shape=jax.ShapeDtypeStruct(shape, BF16),
+        compiler_params=PARAMS,
+        cost_estimate=cost(1000, 1024),
+    )(*arrays, *before)
+
+
+def finish_kernel(arrived, own, partner, *refs):
+    others, (mine, give) = refs[:arrived], refs[-2:]
     me = lax.axis_index("ctx")
     chip, core = me // 2, me % 2
-    half = HD // 2
-    at = pl.ds(pl.multiple_of(core * half, half), half)
-    keys, query = ((own[state, :, at] + partner[state].astype(F32)).astype(BF16) for state in range(2))
-    for step, out in zip(steps, outputs):
-        out[...] = jnp.where(chip + step < chips, keys, query)
-
-
-@jax.named_scope("chip_states")
-def chip_states(own, partner, chips, steps, before=()):
-    _, heads, rows, _ = own.shape
-    return pl.pallas_call(
-        functools.partial(pick_kernel, chips, steps),
-        in_specs=[pl.BlockSpec(memory_space=pltpu.VMEM)] * 2
-        + [pl.BlockSpec(memory_space=pl.ANY)] * len(before),
-        out_shape=[jax.ShapeDtypeStruct((heads, rows // 2, HD), BF16)] * len(steps),
-        compiler_params=PARAMS,
-        cost_estimate=cost(1000, 1024),
-    )(own, partner, *before)
-
-
-def finish_kernel(chips, own, partner, *refs):
-    others, (mine, give) = refs[: chips - 1], refs[-2:]
-    me = lax.axis_index("ctx")
-    chip, core = me // 2, me % 2
-    half = HD // 2
-    at = pl.ds(pl.multiple_of(core * half, half), half)
-    keys = query = jnp.zeros(others[0].shape, F32)
-    for step, ref in enumerate(others, 1):
-        part = ref[...].astype(F32)
-        keys = keys + jnp.where(chip >= step, part, 0.0)
-        query = query + jnp.where(chip < step, part, 0.0)
+    keys = query = jnp.zeros(mine.shape[1:], F32)
+    for step, ref in enumerate(others):
+        upper = chip & (1 << step) != 0
+        pair = (ref, ref) if step == arrived - 1 else (ref.at[0], ref.at[1])
+        keys = keys + jnp.where(upper, pair[0][...].astype(F32), 0.0)
+        query = query + jnp.where(upper, 0.0, pair[1][...].astype(F32))
     mine[0] = (keys + jnp.where(core == 1, partner[0].astype(F32), 0.0)).astype(BF16)
     mine[1] = (query + jnp.where(core == 0, partner[1].astype(F32), 0.0)).astype(BF16)
-    give[0] = (keys + jnp.where(core == 0, own[0, :, at], 0.0)).astype(BF16)
-    give[1] = (query + jnp.where(core == 1, own[1, :, at], 0.0)).astype(BF16)
+    give[0] = (keys + jnp.where(core == 0, own_half(own, 0), 0.0)).astype(BF16)
+    give[1] = (query + jnp.where(core == 1, own_half(own, 1), 0.0)).astype(BF16)
 
 
 @jax.named_scope("chip_states")
 def finished(own, partner, others, before):
-    _, heads, rows, _ = own.shape
     return pl.pallas_call(
-        functools.partial(finish_kernel, len(others) + 1),
+        functools.partial(finish_kernel, len(others)),
         in_specs=[pl.BlockSpec(memory_space=pltpu.VMEM)] * (2 + len(others))
         + [pl.BlockSpec(memory_space=pl.ANY)] * len(before),
-        out_shape=[jax.ShapeDtypeStruct((2, heads, rows // 2, HD), BF16)] * 2,
+        out_shape=[jax.ShapeDtypeStruct(partner.shape, BF16)] * 2,
         compiler_params=PARAMS,
         cost_estimate=cost(1000, 1024),
     )(own, partner, *others, *before)
 
 
 def exchanged(own, give, before=(), last=()):
-    spans = lax.axis_size("ctx")
-    chips = spans // 2
+    chips = lax.axis_size("ctx") // 2
+    assert chips & (chips - 1) == 0
     partner = send(give, "ctx", lambda index: index ^ 1)
-    others = []
-    for first in range(1, chips, 2):
-        steps = list(range(first, min(first + 2, chips)))
-        for step, value in zip(steps, chip_states(own, partner, chips, steps, others[-2:][:1] + list(before if others else ()))):
-            others.append(send(value, "ctx", lambda index: (index + 2 * step) % spans))
+    others, bit = [], 1
+    while bit < chips:
+        final = 2 * bit == chips
+        moving = group_states(own, partner, others, bit, final, before if final else ())
+        others.append(send(moving, "ctx", lambda index: index ^ (2 * bit)))
+        bit *= 2
     mine, half = finished(own, partner, others, last)
-    return mine, send(half, "ctx", lambda index: index ^ 1)
+    return (mine, send(half, "ctx", lambda index: index ^ 1)), others
 
 
 def read_states(refs, head):
@@ -386,10 +395,10 @@
         ]
 
     received = [exchange(own, first)] + [exchange(values[0], values[1:]) for values in packed]
-    early = exchanged(*own_states(received[0], chunks[0], late, []))
+    early, arrived = exchanged(*own_states(received[0], chunks[0], late, []))
     *held, token = gradients([(received[0], early, 0, 0, chunks[0])], (), group, factor)
     *held, ready = gradients([(received[2], early, chunks[0], heads - late, late)], held, group, factor)
-    second = exchanged(*own_states(received[1], middle, 0, [early[0]]), [token], [ready])
+    second, _ = exchanged(*own_states(received[1], middle, 0, [arrived[0]]), [token], [ready])
     *held, _ = gradients([(received[1], second, 0, chunks[0], middle)], held, group, factor)
     return tuple(held)
 

time: 71.9 us -> 70.4 us (0.979)
  waiting for transfers between devices: 26.4 us -> 25.2 us
    ppermute x19 -> x17, waiting for transfers between devices: 26.4 us -> 25.2 us  [send(): lax.ppermute(value, axis, [(index, target(index)) for index in range(coun...]
    ppermute x19 -> x17, starting transfers between devices: 26.4 us -> 26.4 us  [send(): lax.ppermute(value, axis, [(index, target(index)) for index in range(coun...]
  transfers between devices with their start and end apart: 19 -> 17, of which waited for: 6 -> 6; matrix products, arithmetic and copies ran while one was open for 0% -> 0% of each run, Pallas kernels for 15% -> 16%
where the time goes in v7:
time: 70.4 us; the launch traced here: 70.1 us
  starting transfers between devices  26.4 us (38%)
  waiting for transfers between devices  25.2 us (36%)
  Pallas kernels  17.8 us (25%)
  between operations  0.77 us (1%)
    ppermute x17, starting transfers between devices, send(): lax.ppermute(value, axis, [(index, target(index)) for index in range(coun...  26.4 us
    ppermute x17, waiting for transfers between devices, send(): lax.ppermute(value, axis, [(index, target(index)) for index in range(coun...  25.2 us
    pallas_call x3, Pallas kernels, gradients(): pl.pallas_call(functools.partial(grads_kernel, parts, factor, [item[2:] f...  12.5 us
    pallas_call x1, Pallas kernels, pack_rest(): pl.pallas_call(functools.partial(rest_kernel, parts, heads, chunks), in_s...  2.15 us
    pallas_call x1, Pallas kernels, pack_first(): pl.pallas_call(functools.partial(first_kernel, parts, heads, count, late)...  1.85 us
  transfers between devices with their start and end apart: 17, of which 6 were waited for; matrix products, arithmetic and copies ran while one was open for 0% of the time, Pallas kernels for 16%

profile of v7, /device:TPU:0, one launch (start us, length us, event | category | flops | bytes accessed | tf_op | source)
XLA Modules:
  0.0 70.1 jit_solution(6896971525870225159)
XLA Ops:
  0.6 1.9 %pack.3 = (bf16[16,128,128]{2,1,0:T(8,128)(2,1)S(1)}, bf16[16,128,128]{2,1,0:T(8,128)(2,1)S(1)}, bf16[16,128,128]{2,1,0:T(8,128)(2,1)S(1)}) custom-call(bf16[1,128,4096]{2,1,0:T(8,128)(2,1)} %refs_0_.3, bf16[1,128,4096]{2,1,0:T(8,128)(2,1)} %refs_1_.3, bf16[1,128,4096]{2,1,0:T(8,128)(2,1)} %refs_2_.3, bf16[1,128,4096]{2,1,0:T(8,128)(2,1)} %refs_3_.3), custom_call_target="tpu_custom_call" | custom-call | flops 1000 | bytes 2048 | tf_op jit(solution)/shard_map/pack/pallas_call | solution.py:92
  2.5 3.0 %collective-permute-start.3 = (bf16[16,128,128]{2,1,0:T(8,128)(2,1)S(1)}, bf16[16,128,128]{2,1,0:T(8,128)(2,1)S(1)}, u32[]{:S(2)}, u32[]{:S(2)}) collective-permute-start(bf16[16,128,128]{2,1,0:T(8,128)(2,1)S(1)} %get-tuple-element.39), channel_id=1, source_target_pairs={{0,16},{8,24},{16,0},{24,8},{1,17},{9,25},{17,1},{25,9},{2,18},{10... | collective-permute-start | bytes 1572872 | tf_op jit(solution)/shard_map/ppermute | solution.py:47
  5.5 1.4 %collective-permute-start.4 = (bf16[16,128,128]{2,1,0:T(8,128)(2,1)S(1)}, bf16[16,128,128]{2,1,0:T(8,128)(2,1)S(1)}, u32[]{:S(2)}, u32[]{:S(2)}) collective-permute-start(bf16[16,128,128]{2,1,0:T(8,128)(2,1)S(1)} %get-tuple-element.40), channel_id=1, source_target_pairs={{0,24},{8,16},{16,8},{24,0},{1,25},{9,17},{17,9},{25,1},{2,26},{10... | collective-permute-start | bytes 1572872 | tf_op jit(solution)/shard_map/ppermute | solution.py:47
  7.0 0.1 collective-permute-start.5
  7.1 2.1 %pack.2 = (bf16[16,128,128]{2,1,0:T(8,128)(2,1)S(1)}, bf16[12,128,128]{2,1,0:T(8,128)(2,1)S(1)}, bf16[12,128,128]{2,1,0:T(8,128)(2,1)S(1)}, bf16[12,128,128]{2,1...) custom-call(bf16[1,128,4096]{2,1,0:T(8,128)(2,1)} %refs_0_.3, ...), custom_call_target="tpu_custom_call" | custom-call | flops 1000 | bytes 2048 | tf_op jit(solution)/shard_map/pack/pallas_call | solution.py:135
  9.2 2.0 %collective-permute-start = (bf16[12,128,128]{2,1,0:T(8,128)(2,1)S(1)}, bf16[12,128,128]{2,1,0:T(8,128)(2,1)S(1)}, u32[]{:S(2)}, u32[]{:S(2)}) collective-permute-start(bf16[12,128,128]{2,1,0:T(8,128)(2,1)S(1)} %get-tuple-element.35), channel_id=1, source_target_pairs={{0,16},{8,24},{16,0},{24,8},{1,17},{9,25},{17,1},{25,9},{2,18},{10... | collective-permute-start | bytes 1179656 | tf_op jit(solution)/shard_map/ppermute | solution.py:47
  11.2 1.5 %collective-permute-start.1 = (bf16[12,128,128]{2,1,0:T(8,128)(2,1)S(1)}, bf16[12,128,128]{2,1,0:T(8,128)(2,1)S(1)}, u32[]{:S(2)}, u32[]{:S(2)}) collective-permute-start(bf16[12,128,128]{2,1,0:T(8,128)(2,1)S(1)} %get-tuple-element.36), channel_id=1, source_target_pairs={{0,24},{8,16},{16,8},{24,0},{1,25},{9,17},{17,9},{25,1},{2,26},{10... | collective-permute-start | bytes 1179656 | tf_op jit(solution)/shard_map/ppermute | solution.py:47
  12.7 17.0 %collective-permute-done.3.refs_1_ = bf16[16,128,128]{2,1,0:T(8,128)(2,1)S(1)} collective-permute-done((bf16[16,128,128]{2,1,0:T(8,128)(2,1)S(1)}, bf16[16,128,128]{2,1,0:T(8,128)(2,1)S(1)}, u32[]{:S(2)}, u32[]{:S(2)}) %collective-permute-start.3) | collective-permute-done | bytes 524320 | tf_op jit(solution)/shard_map/ppermute | solution.py:47
  29.7 2.2 %collective-permute-start.2 = (bf16[12,128,128]{2,1,0:T(8,128)(2,1)S(1)}, bf16[12,128,128]{2,1,0:T(8,128)(2,1)S(1)}, u32[]{:S(2)}, u32[]{:S(2)}) collective-permute-start(bf16[12,128,128]{2,1,0:T(8,128)(2,1)S(1)} %get-tuple-element.37), channel_id=1, source_target_pairs={{0,8},{8,0},{16,24},{24,16},{1,9},{9,1},{17,25},{25,17},{2,10},{10... | collective-permute-start | bytes 1179656 | tf_op jit(solution)/shard_map/ppermute | solution.py:47
  31.9 0.4 own_states.2
  32.4 0.1 collective-permute-start.6
  32.4 1.4 %collective-permute-done.6.partner = bf16[2,5,64,128]{3,2,1,0:T(8,128)(2,1)S(1)} collective-permute-done((bf16[2,5,64,128]{3,2,1,0:T(8,128)(2,1)S(1)}, bf16[2,5,64,128]{3,2,1,0:T(8,128)(2,1)S(1)}, u32[]{:S(2)}, u32[]{:S(2)}) %collective-permute-start.6) | collective-permute-done | bytes 163872 | tf_op jit(solution)/shard_map/ppermute | solution.py:47
  33.9 1.6 %collective-permute-start.7 = (bf16[2,5,64,128]{3,2,1,0:T(8,128)(2,1)S(1)}, bf16[2,5,64,128]{3,2,1,0:T(8,128)(2,1)S(1)}, u32[]{:S(2)}, u32[]{:S(2)}) collective-permute-start(bf16[2,5,64,128]{3,2,1,0:T(8,128)(2,1)S(1)} %chip_states.6), channel_id=1, source_target_pairs={{0,2},{1,3},{2,0},{3,1},{4,6},{5,7},{6,4},{7,5},{8,10},{9,11},{10,... | collective-permute-start | bytes 491528 | tf_op jit(solution)/shard_map/ppermute | solution.py:47
  35.5 4.7 %collective-permute-done.7.refs_4_.refs_0_ = bf16[2,5,64,128]{3,2,1,0:T(8,128)(2,1)S(1)} collective-permute-done((bf16[2,5,64,128]{3,2,1,0:T(8,128)(2,1)S(1)}, bf16[2,5,64,128]{3,2,1,0:T(8,128)(2,1)S(1)}, u32[]{:S(2)}, u32[]{:S(2)}) %collective-permute-start.7) | collective-permute-done | bytes 163872 | tf_op jit(solution)/shard_map/ppermute | solution.py:47
  40.2 0.1 chip_states.8
  40.3 2.7 %collective-permute-start.10 = (bf16[5,64,128]{2,1,0:T(8,128)(2,1)S(1)}, bf16[5,64,128]{2,1,0:T(8,128)(2,1)S(1)}, u32[]{:S(2)}, u32[]{:S(2)}) collective-permute-start(bf16[5,64,128]{2,1,0:T(8,128)(2,1)S(1)} %chip_states.8), channel_id=1, source_target_pairs={{0,4},{1,5},{2,6},{3,7},{4,0},{5,1},{6,2},{7,3},{8,12},{9,13},{10,... | collective-permute-start | bytes 245768 | tf_op jit(solution)/shard_map/ppermute | solution.py:47
  42.9 2.5 %collective-permute-start.13 = (bf16[8,128,128]{2,1,0:T(8,128)(2,1)S(1)}, bf16[8,128,128]{2,1,0:T(8,128)(2,1)S(1)}, u32[]{:S(2)}, u32[]{:S(2)}) collective-permute-start(bf16[8,128,128]{2,1,0:T(8,128)(2,1)S(1)} %get-tuple-element.50), channel_id=1, source_target_pairs={{0,16},{8,24},{16,0},{24,8},{1,17},{9,25},{17,1},{25,9},{2,18},{10... | collective-permute-start | bytes 786440 | tf_op jit(solution)/shard_map/ppermute | solution.py:47
  45.4 0.2 collective-permute-done.refs_1_
  45.7 3.7 %collective-permute-start.14 = (bf16[8,128,128]{2,1,0:T(8,128)(2,1)S(1)}, bf16[8,128,128]{2,1,0:T(8,128)(2,1)S(1)}, u32[]{:S(2)}, u32[]{:S(2)}) collective-permute-start(bf16[8,128,128]{2,1,0:T(8,128)(2,1)S(1)} %get-tuple-element.51), channel_id=1, source_target_pairs={{0,24},{8,16},{16,8},{24,0},{1,25},{9,17},{17,9},{25,1},{2,26},{10... | collective-permute-start | bytes 786440 | tf_op jit(solution)/shard_map/ppermute | solution.py:47
  49.4 0.4 own_states.3
  49.8 0.1 collective-permute-start.8
  49.9 0.1 chip_states.9
  50.0 0.5 collective-permute-start.11
  50.6 0.6 collective-permute-done.8.partner
  51.2 1.6 %collective-permute-start.9 = (bf16[2,3,64,128]{3,2,1,0:T(8,128)(2,1)S(1)}, bf16[2,3,64,128]{3,2,1,0:T(8,128)(2,1)S(1)}, u32[]{:S(2)}, u32[]{:S(2)}) collective-permute-start(bf16[2,3,64,128]{3,2,1,0:T(8,128)(2,1)S(1)} %chip_states.7), channel_id=1, source_target_pairs={{0,2},{1,3},{2,0},{3,1},{4,6},{5,7},{6,4},{7,5},{8,10},{9,11},{10,... | collective-permute-start | bytes 294920 | tf_op jit(solution)/shard_map/ppermute | solution.py:47
  52.8 4.4 %gradients.3 = (bf16[1,512,1024]{2,1,0:T(8,128)(2,1)}, bf16[1,512,1024]{2,1,0:T(8,128)(2,1)}, bf16[1,512,1024]{2,1,0:T(8,128)(2,1)}, f32[8,128]{1,0:T(8,128)S(1)}) custom-call(bf16[16,128,128]{2,1,0:T(8,128)(2,1)S(1)} %get-tuple-element.38.refs_0_, bf16[16,128,128]{2,1,0:T(8,128)(2,1)S(1)} %collective-permute-done.3.refs_1_, ...), custom_call_target="tpu_custom_call" | custom-call | flops 1000 | bytes 2048 | tf_op jit(solution)/shard_map/gradients/pallas_call | solution.py:359
  57.3 3.2 %collective-permute-start.12 = (bf16[3,64,128]{2,1,0:T(8,128)(2,1)S(1)}, bf16[3,64,128]{2,1,0:T(8,128)(2,1)S(1)}, u32[]{:S(2)}, u32[]{:S(2)}) collective-permute-start(bf16[3,64,128]{2,1,0:T(8,128)(2,1)S(1)} %chip_states.10), channel_id=1, source_target_pairs={{0,4},{1,5},{2,6},{3,7},{4,0},{5,1},{6,2},{7,3},{8,12},{9,13},{10,... | collective-permute-start | bytes 147464 | tf_op jit(solution)/shard_map/ppermute | solution.py:47
  60.5 3.2 %gradients.4 = (bf16[1,512,1024]{2,1,0:T(8,128)(2,1)}, bf16[1,512,1024]{2,1,0:T(8,128)(2,1)}, bf16[1,512,1024]{2,1,0:T(8,128)(2,1)}, f32[8,128]{1,0:T(8,128)S(1)}) custom-call(bf16[8,128,128]{2,1,0:T(8,128)(2,1)S(1)} %get-tuple-element.49.refs_0_, ...), custom_call_target="tpu_custom_call", output_to_operand_aliasing={{0}: (6, {}), {1}: (7, {}), {2}: (8, {})} | custom-call | flops 1000 | bytes 2048 | tf_op jit(solution)/shard_map/gradients/pallas_call | solution.py:359
  63.7 0.1 chip_states.11
  63.8 0.1 collective-permute-start.16
  63.9 1.3 %collective-permute-done.16.refs_5_ = bf16[2,3,64,128]{3,2,1,0:T(8,128)(2,1)S(1)} collective-permute-done((bf16[2,3,64,128]{3,2,1,0:T(8,128)(2,1)S(1)}, bf16[2,3,64,128]{3,2,1,0:T(8,128)(2,1)S(1)}, u32[]{:S(2)}, u32[]{:S(2)}) %collective-permute-start.16) | collective-permute-done | bytes 98336 | tf_op jit(solution)/shard_map/ppermute | solution.py:47
  65.2 4.9 %gradients.5 = (bf16[1,512,1024]{2,1,0:T(8,128)(2,1)}, bf16[1,512,1024]{2,1,0:T(8,128)(2,1)}, bf16[1,512,1024]{2,1,0:T(8,128)(2,1)}, f32[8,128]{1,0:T(8,128)}) custom-call(bf16[12,128,128]{2,1,0:T(8,128)(2,1)S(1)} %get-tuple-element.34.refs_0_, ...), custom_call_target="tpu_custom_call", output_to_operand_aliasing={{0}: (6, {}), {1}: (7, {}), {2}: (8, {})} | custom-call | flops 1000 | bytes 2048 | tf_op jit(solution)/shard_map/gradients/pallas_call | solution.py:359
  (15 shorter events, 0.2 us)
Async XLA Ops:
  2.5 27.2 %collective-permute-start.3 = (bf16[16,128,128]{2,1,0:T(8,128)(2,1)S(1)}, bf16[16,128,128]{2,1,0:T(8,128)(2,1)S(1)}, u32[]{:S(2)}, u32[]{:S(2)}) collective-permute-start(bf16[16,128,128]{2,1,0:T(8,128)(2,1)S(1)} %get-tuple-element.39), channel_id=1, source_target_pairs={{0,16},{8,24},{16,0},{24,8},{1,17},{9,25},{17,1},{25,9},{2,18},{10... | collective-permute-start | bytes 1572872 | tf_op jit(solution)/shard_map/ppermute | solution.py:47
  5.5 26.4 %collective-permute-start.4 = (bf16[16,128,128]{2,1,0:T(8,128)(2,1)S(1)}, bf16[16,128,128]{2,1,0:T(8,128)(2,1)S(1)}, u32[]{:S(2)}, u32[]{:S(2)}) collective-permute-start(bf16[16,128,128]{2,1,0:T(8,128)(2,1)S(1)} %get-tuple-element.40), channel_id=1, source_target_pairs={{0,24},{8,16},{16,8},{24,0},{1,25},{9,17},{17,9},{25,1},{2,26},{10... | collective-permute-start | bytes 1572872 | tf_op jit(solution)/shard_map/ppermute | solution.py:47
  7.0 25.0 %collective-permute-start.5 = (bf16[16,128,128]{2,1,0:T(8,128)(2,1)S(1)}, bf16[16,128,128]{2,1,0:T(8,128)(2,1)S(1)}, u32[]{:S(2)}, u32[]{:S(2)}) collective-permute-start(bf16[16,128,128]{2,1,0:T(8,128)(2,1)S(1)} %get-tuple-element.41), channel_id=1, source_target_pairs={{0,8},{8,0},{16,24},{24,16},{1,9},{9,1},{17,25},{25,17},{2,10},{10... | collective-permute-start | bytes 1572872 | tf_op jit(solution)/shard_map/ppermute | solution.py:47
  9.2 36.5 %collective-permute-start = (bf16[12,128,128]{2,1,0:T(8,128)(2,1)S(1)}, bf16[12,128,128]{2,1,0:T(8,128)(2,1)S(1)}, u32[]{:S(2)}, u32[]{:S(2)}) collective-permute-start(bf16[12,128,128]{2,1,0:T(8,128)(2,1)S(1)} %get-tuple-element.35), channel_id=1, source_target_pairs={{0,16},{8,24},{16,0},{24,8},{1,17},{9,25},{17,1},{25,9},{2,18},{10... | collective-permute-start | bytes 1179656 | tf_op jit(solution)/shard_map/ppermute | solution.py:47
  11.2 38.1 %collective-permute-start.1 = (bf16[12,128,128]{2,1,0:T(8,128)(2,1)S(1)}, bf16[12,128,128]{2,1,0:T(8,128)(2,1)S(1)}, u32[]{:S(2)}, u32[]{:S(2)}) collective-permute-start(bf16[12,128,128]{2,1,0:T(8,128)(2,1)S(1)} %get-tuple-element.36), channel_id=1, source_target_pairs={{0,24},{8,16},{16,8},{24,0},{1,25},{9,17},{17,9},{25,1},{2,26},{10... | collective-permute-start | bytes 1179656 | tf_op jit(solution)/shard_map/ppermute | solution.py:47
  29.7 19.6 %collective-permute-start.2 = (bf16[12,128,128]{2,1,0:T(8,128)(2,1)S(1)}, bf16[12,128,128]{2,1,0:T(8,128)(2,1)S(1)}, u32[]{:S(2)}, u32[]{:S(2)}) collective-permute-start(bf16[12,128,128]{2,1,0:T(8,128)(2,1)S(1)} %get-tuple-element.37), channel_id=1, source_target_pairs={{0,8},{8,0},{16,24},{24,16},{1,9},{9,1},{17,25},{25,17},{2,10},{10... | collective-permute-start | bytes 1179656 | tf_op jit(solution)/shard_map/ppermute | solution.py:47
  32.4 1.5 %collective-permute-start.6 = (bf16[2,5,64,128]{3,2,1,0:T(8,128)(2,1)S(1)}, bf16[2,5,64,128]{3,2,1,0:T(8,128)(2,1)S(1)}, u32[]{:S(2)}, u32[]{:S(2)}) collective-permute-start(bf16[2,5,64,128]{3,2,1,0:T(8,128)(2,1)S(1)} %get-tuple-element.43), channel_id=1, source_target_pairs={{0,1},{1,0},{2,3},{3,2},{4,5},{5,4},{6,7},{7,6},{8,9},{9,8},{10,11... | collective-permute-start | bytes 491528 | tf_op jit(solution)/shard_map/ppermute | solution.py:47
  33.9 6.3 %collective-permute-start.7 = (bf16[2,5,64,128]{3,2,1,0:T(8,128)(2,1)S(1)}, bf16[2,5,64,128]{3,2,1,0:T(8,128)(2,1)S(1)}, u32[]{:S(2)}, u32[]{:S(2)}) collective-permute-start(bf16[2,5,64,128]{3,2,1,0:T(8,128)(2,1)S(1)} %chip_states.6), channel_id=1, source_target_pairs={{0,2},{1,3},{2,0},{3,1},{4,6},{5,7},{6,4},{7,5},{8,10},{9,11},{10,... | collective-permute-start | bytes 491528 | tf_op jit(solution)/shard_map/ppermute | solution.py:47
  40.3 9.6 %collective-permute-start.10 = (bf16[5,64,128]{2,1,0:T(8,128)(2,1)S(1)}, bf16[5,64,128]{2,1,0:T(8,128)(2,1)S(1)}, u32[]{:S(2)}, u32[]{:S(2)}) collective-permute-start(bf16[5,64,128]{2,1,0:T(8,128)(2,1)S(1)} %chip_states.8), channel_id=1, source_target_pairs={{0,4},{1,5},{2,6},{3,7},{4,0},{5,1},{6,2},{7,3},{8,12},{9,13},{10,... | collective-permute-start | bytes 245768 | tf_op jit(solution)/shard_map/ppermute | solution.py:47
  42.9 17.5 %collective-permute-start.13 = (bf16[8,128,128]{2,1,0:T(8,128)(2,1)S(1)}, bf16[8,128,128]{2,1,0:T(8,128)(2,1)S(1)}, u32[]{:S(2)}, u32[]{:S(2)}) collective-permute-start(bf16[8,128,128]{2,1,0:T(8,128)(2,1)S(1)} %get-tuple-element.50), channel_id=1, source_target_pairs={{0,16},{8,24},{16,0},{24,8},{1,17},{9,25},{17,1},{25,9},{2,18},{10... | collective-permute-start | bytes 786440 | tf_op jit(solution)/shard_map/ppermute | solution.py:47
  45.7 14.8 %collective-permute-start.14 = (bf16[8,128,128]{2,1,0:T(8,128)(2,1)S(1)}, bf16[8,128,128]{2,1,0:T(8,128)(2,1)S(1)}, u32[]{:S(2)}, u32[]{:S(2)}) collective-permute-start(bf16[8,128,128]{2,1,0:T(8,128)(2,1)S(1)} %get-tuple-element.51), channel_id=1, source_target_pairs={{0,24},{8,16},{16,8},{24,0},{1,25},{9,17},{17,9},{25,1},{2,26},{10... | collective-permute-start | bytes 786440 | tf_op jit(solution)/shard_map/ppermute | solution.py:47
  49.3 11.1 %collective-permute-start.15 = (bf16[8,128,128]{2,1,0:T(8,128)(2,1)S(1)}, bf16[8,128,128]{2,1,0:T(8,128)(2,1)S(1)}, u32[]{:S(2)}, u32[]{:S(2)}) collective-permute-start(bf16[8,128,128]{2,1,0:T(8,128)(2,1)S(1)} %get-tuple-element.52), channel_id=1, source_target_pairs={{0,8},{8,0},{16,24},{24,16},{1,9},{9,1},{17,25},{25,17},{2,10},{10... | collective-permute-start | bytes 786440 | tf_op jit(solution)/shard_map/ppermute | solution.py:47
  49.8 1.4 %collective-permute-start.8 = (bf16[2,3,64,128]{3,2,1,0:T(8,128)(2,1)S(1)}, bf16[2,3,64,128]{3,2,1,0:T(8,128)(2,1)S(1)}, u32[]{:S(2)}, u32[]{:S(2)}) collective-permute-start(bf16[2,3,64,128]{3,2,1,0:T(8,128)(2,1)S(1)} %get-tuple-element.45), channel_id=1, source_target_pairs={{0,1},{1,0},{2,3},{3,2},{4,5},{5,4},{6,7},{7,6},{8,9},{9,8},{10,11... | collective-permute-start | bytes 294920 | tf_op jit(solution)/shard_map/ppermute | solution.py:47
  50.0 2.8 %collective-permute-start.11 = (bf16[2,5,64,128]{3,2,1,0:T(8,128)(2,1)S(1)}, bf16[2,5,64,128]{3,2,1,0:T(8,128)(2,1)S(1)}, u32[]{:S(2)}, u32[]{:S(2)}) collective-permute-start(bf16[2,5,64,128]{3,2,1,0:T(8,128)(2,1)S(1)} %get-tuple-element.47), channel_id=1, source_target_pairs={{0,1},{1,0},{2,3},{3,2},{4,5},{5,4},{6,7},{7,6},{8,9},{9,8},{10,11... | collective-permute-start | bytes 491528 | tf_op jit(solution)/shard_map/ppermute | solution.py:47
  51.2 6.0 %collective-permute-start.9 = (bf16[2,3,64,128]{3,2,1,0:T(8,128)(2,1)S(1)}, bf16[2,3,64,128]{3,2,1,0:T(8,128)(2,1)S(1)}, u32[]{:S(2)}, u32[]{:S(2)}) collective-permute-start(bf16[2,3,64,128]{3,2,1,0:T(8,128)(2,1)S(1)} %chip_states.7), channel_id=1, source_target_pairs={{0,2},{1,3},{2,0},{3,1},{4,6},{5,7},{6,4},{7,5},{8,10},{9,11},{10,... | collective-permute-start | bytes 294920 | tf_op jit(solution)/shard_map/ppermute | solution.py:47
  57.3 6.4 %collective-permute-start.12 = (bf16[3,64,128]{2,1,0:T(8,128)(2,1)S(1)}, bf16[3,64,128]{2,1,0:T(8,128)(2,1)S(1)}, u32[]{:S(2)}, u32[]{:S(2)}) collective-permute-start(bf16[3,64,128]{2,1,0:T(8,128)(2,1)S(1)} %chip_states.10), channel_id=1, source_target_pairs={{0,4},{1,5},{2,6},{3,7},{4,0},{5,1},{6,2},{7,3},{8,12},{9,13},{10,... | collective-permute-start | bytes 147464 | tf_op jit(solution)/shard_map/ppermute | solution.py:47
  63.8 1.4 %collective-permute-start.16 = (bf16[2,3,64,128]{3,2,1,0:T(8,128)(2,1)S(1)}, bf16[2,3,64,128]{3,2,1,0:T(8,128)(2,1)S(1)}, u32[]{:S(2)}, u32[]{:S(2)}) collective-permute-start(bf16[2,3,64,128]{3,2,1,0:T(8,128)(2,1)S(1)} %get-tuple-element.58), channel_id=1, source_target_pairs={{0,1},{1,0},{2,3},{3,2},{4,5},{5,4},{6,7},{7,6},{8,9},{9,8},{10,11... | collective-permute-start | bytes 294920 | tf_op jit(solution)/shard_map/ppermute | solution.py:47

commit v8 on v7

--- a/solution.py
+++ b/solution.py
@@ -290,11 +290,11 @@
     column = lax.broadcasted_iota(jnp.int32, (TILE, TILE), 1)
     low, high = column <= row, row <= column
 
-    def scores(a, b, keep):
-        value = dot(a, b, (1, 1))
-        if keep is not None:
-            value = jnp.where(keep, value, 0.0)
-        return value.astype(BF16)
+    def scores(a, others, diagonal, keep):
+        value = dot(a, jnp.concatenate(others, 0), (1, 1))
+        pieces = [value[:, j * TILE : (j + 1) * TILE] for j in range(len(others))]
+        pieces[diagonal] = jnp.where(keep, pieces[diagonal], 0.0)
+        return [piece.astype(BF16) for piece in pieces]
 
     def total(lefts, rights):
         value = dot(jnp.concatenate(lefts, 1), jnp.concatenate(rights, 0), (1, 0))
@@ -332,15 +332,15 @@
                 before, after = range(i + 1), range(i, tiles)
                 column = first + head
                 store(slot, column, 0, i, total(
-                    [scores(grads[i], values[j], low if i == j else None) for j in before] + [grads[i]],
+                    scores(grads[i], [values[j] for j in before], i, low) + [grads[i]],
                     [keys[j] for j in before] + [key_state],
                 ))
                 store(slot, column, 1, i, total(
-                    [scores(values[i], grads[j], high if i == j else None) for j in after] + [values[i]],
+                    scores(values[i], [grads[j] for j in after], 0, high) + [values[i]],
                     [query[j] for j in after] + [query_turned],
                 ))
                 store(slot, column, 2, i, total(
-                    [scores(keys[i], query[j], high if i == j else None) for j in after] + [keys[i]],
+                    scores(keys[i], [query[j] for j in after], 0, high) + [keys[i]],
                     [grads[j] for j in after] + [query_state],
                 ))
             slot += 1

time: 70.4 us -> 70.4 us (level)
  no operation moved by 1% of the time
where the time goes in v8:
time: 70.4 us; the launch traced here: 70.1 us
  starting transfers between devices  26.4 us (38%)
  waiting for transfers between devices  25.2 us (36%)
  Pallas kernels  17.8 us (25%)
  between operations  0.77 us (1%)
    ppermute x17, starting transfers between devices, send(): lax.ppermute(value, axis, [(index, target(index)) for index in range(coun...  26.4 us
    ppermute x17, waiting for transfers between devices, send(): lax.ppermute(value, axis, [(index, target(index)) for index in range(coun...  25.2 us
    pallas_call x3, Pallas kernels, gradients(): pl.pallas_call(functools.partial(grads_kernel, parts, factor, [item[2:] f...  12.5 us
    pallas_call x1, Pallas kernels, pack_rest(): pl.pallas_call(functools.partial(rest_kernel, parts, heads, chunks), in_s...  2.15 us
    pallas_call x1, Pallas kernels, pack_first(): pl.pallas_call(functools.partial(first_kernel, parts, heads, count, late)...  1.85 us
  transfers between devices with their start and end apart: 17, of which 6 were waited for; matrix products, arithmetic and copies ran while one was open for 0% of the time, Pallas kernels for 16%

profile of v8, /device:TPU:0, one launch (start us, length us, event | category | flops | bytes accessed | tf_op | source)
XLA Modules:
  0.0 70.1 jit_solution(6896971525870225159)
XLA Ops:
  0.6 1.9 %pack.3 = (bf16[16,128,128]{2,1,0:T(8,128)(2,1)S(1)}, bf16[16,128,128]{2,1,0:T(8,128)(2,1)S(1)}, bf16[16,128,128]{2,1,0:T(8,128)(2,1)S(1)}) custom-call(bf16[1,128,4096]{2,1,0:T(8,128)(2,1)} %refs_0_.3, bf16[1,128,4096]{2,1,0:T(8,128)(2,1)} %refs_1_.3, bf16[1,128,4096]{2,1,0:T(8,128)(2,1)} %refs_2_.3, bf16[1,128,4096]{2,1,0:T(8,128)(2,1)} %refs_3_.3), custom_call_target="tpu_custom_call" | custom-call | flops 1000 | bytes 2048 | tf_op jit(solution)/shard_map/pack/pallas_call | solution.py:92
  2.5 3.0 %collective-permute-start.3 = (bf16[16,128,128]{2,1,0:T(8,128)(2,1)S(1)}, bf16[16,128,128]{2,1,0:T(8,128)(2,1)S(1)}, u32[]{:S(2)}, u32[]{:S(2)}) collective-permute-start(bf16[16,128,128]{2,1,0:T(8,128)(2,1)S(1)} %get-tuple-element.39), channel_id=1, source_target_pairs={{0,16},{8,24},{16,0},{24,8},{1,17},{9,25},{17,1},{25,9},{2,18},{10... | collective-permute-start | bytes 1572872 | tf_op jit(solution)/shard_map/ppermute | solution.py:47
  5.5 1.4 %collective-permute-start.4 = (bf16[16,128,128]{2,1,0:T(8,128)(2,1)S(1)}, bf16[16,128,128]{2,1,0:T(8,128)(2,1)S(1)}, u32[]{:S(2)}, u32[]{:S(2)}) collective-permute-start(bf16[16,128,128]{2,1,0:T(8,128)(2,1)S(1)} %get-tuple-element.40), channel_id=1, source_target_pairs={{0,24},{8,16},{16,8},{24,0},{1,25},{9,17},{17,9},{25,1},{2,26},{10... | collective-permute-start | bytes 1572872 | tf_op jit(solution)/shard_map/ppermute | solution.py:47
  7.0 0.1 collective-permute-start.5
  7.1 2.1 %pack.2 = (bf16[16,128,128]{2,1,0:T(8,128)(2,1)S(1)}, bf16[12,128,128]{2,1,0:T(8,128)(2,1)S(1)}, bf16[12,128,128]{2,1,0:T(8,128)(2,1)S(1)}, bf16[12,128,128]{2,1...) custom-call(bf16[1,128,4096]{2,1,0:T(8,128)(2,1)} %refs_0_.3, ...), custom_call_target="tpu_custom_call" | custom-call | flops 1000 | bytes 2048 | tf_op jit(solution)/shard_map/pack/pallas_call | solution.py:135
  9.2 2.0 %collective-permute-start = (bf16[12,128,128]{2,1,0:T(8,128)(2,1)S(1)}, bf16[12,128,128]{2,1,0:T(8,128)(2,1)S(1)}, u32[]{:S(2)}, u32[]{:S(2)}) collective-permute-start(bf16[12,128,128]{2,1,0:T(8,128)(2,1)S(1)} %get-tuple-element.35), channel_id=1, source_target_pairs={{0,16},{8,24},{16,0},{24,8},{1,17},{9,25},{17,1},{25,9},{2,18},{10... | collective-permute-start | bytes 1179656 | tf_op jit(solution)/shard_map/ppermute | solution.py:47
  11.2 1.5 %collective-permute-start.1 = (bf16[12,128,128]{2,1,0:T(8,128)(2,1)S(1)}, bf16[12,128,128]{2,1,0:T(8,128)(2,1)S(1)}, u32[]{:S(2)}, u32[]{:S(2)}) collective-permute-start(bf16[12,128,128]{2,1,0:T(8,128)(2,1)S(1)} %get-tuple-element.36), channel_id=1, source_target_pairs={{0,24},{8,16},{16,8},{24,0},{1,25},{9,17},{17,9},{25,1},{2,26},{10... | collective-permute-start | bytes 1179656 | tf_op jit(solution)/shard_map/ppermute | solution.py:47
  12.7 17.0 %collective-permute-done.3.refs_1_ = bf16[16,128,128]{2,1,0:T(8,128)(2,1)S(1)} collective-permute-done((bf16[16,128,128]{2,1,0:T(8,128)(2,1)S(1)}, bf16[16,128,128]{2,1,0:T(8,128)(2,1)S(1)}, u32[]{:S(2)}, u32[]{:S(2)}) %collective-permute-start.3) | collective-permute-done | bytes 524320 | tf_op jit(solution)/shard_map/ppermute | solution.py:47
  29.7 2.2 %collective-permute-start.2 = (bf16[12,128,128]{2,1,0:T(8,128)(2,1)S(1)}, bf16[12,128,128]{2,1,0:T(8,128)(2,1)S(1)}, u32[]{:S(2)}, u32[]{:S(2)}) collective-permute-start(bf16[12,128,128]{2,1,0:T(8,128)(2,1)S(1)} %get-tuple-element.37), channel_id=1, source_target_pairs={{0,8},{8,0},{16,24},{24,16},{1,9},{9,1},{17,25},{25,17},{2,10},{10... | collective-permute-start | bytes 1179656 | tf_op jit(solution)/shard_map/ppermute | solution.py:47
  31.9 0.4 own_states.2
  32.4 0.1 collective-permute-start.6
  32.4 1.4 %collective-permute-done.6.partner = bf16[2,5,64,128]{3,2,1,0:T(8,128)(2,1)S(1)} collective-permute-done((bf16[2,5,64,128]{3,2,1,0:T(8,128)(2,1)S(1)}, bf16[2,5,64,128]{3,2,1,0:T(8,128)(2,1)S(1)}, u32[]{:S(2)}, u32[]{:S(2)}) %collective-permute-start.6) | collective-permute-done | bytes 163872 | tf_op jit(solution)/shard_map/ppermute | solution.py:47
  33.9 1.6 %collective-permute-start.7 = (bf16[2,5,64,128]{3,2,1,0:T(8,128)(2,1)S(1)}, bf16[2,5,64,128]{3,2,1,0:T(8,128)(2,1)S(1)}, u32[]{:S(2)}, u32[]{:S(2)}) collective-permute-start(bf16[2,5,64,128]{3,2,1,0:T(8,128)(2,1)S(1)} %chip_states.6), channel_id=1, source_target_pairs={{0,2},{1,3},{2,0},{3,1},{4,6},{5,7},{6,4},{7,5},{8,10},{9,11},{10,... | collective-permute-start | bytes 491528 | tf_op jit(solution)/shard_map/ppermute | solution.py:47
  35.5 4.7 %collective-permute-done.7.refs_4_.refs_0_ = bf16[2,5,64,128]{3,2,1,0:T(8,128)(2,1)S(1)} collective-permute-done((bf16[2,5,64,128]{3,2,1,0:T(8,128)(2,1)S(1)}, bf16[2,5,64,128]{3,2,1,0:T(8,128)(2,1)S(1)}, u32[]{:S(2)}, u32[]{:S(2)}) %collective-permute-start.7) | collective-permute-done | bytes 163872 | tf_op jit(solution)/shard_map/ppermute | solution.py:47
  40.2 0.1 chip_states.8
  40.3 2.7 %collective-permute-start.10 = (bf16[5,64,128]{2,1,0:T(8,128)(2,1)S(1)}, bf16[5,64,128]{2,1,0:T(8,128)(2,1)S(1)}, u32[]{:S(2)}, u32[]{:S(2)}) collective-permute-start(bf16[5,64,128]{2,1,0:T(8,128)(2,1)S(1)} %chip_states.8), channel_id=1, source_target_pairs={{0,4},{1,5},{2,6},{3,7},{4,0},{5,1},{6,2},{7,3},{8,12},{9,13},{10,... | collective-permute-start | bytes 245768 | tf_op jit(solution)/shard_map/ppermute | solution.py:47
  42.9 2.5 %collective-permute-start.13 = (bf16[8,128,128]{2,1,0:T(8,128)(2,1)S(1)}, bf16[8,128,128]{2,1,0:T(8,128)(2,1)S(1)}, u32[]{:S(2)}, u32[]{:S(2)}) collective-permute-start(bf16[8,128,128]{2,1,0:T(8,128)(2,1)S(1)} %get-tuple-element.50), channel_id=1, source_target_pairs={{0,16},{8,24},{16,0},{24,8},{1,17},{9,25},{17,1},{25,9},{2,18},{10... | collective-permute-start | bytes 786440 | tf_op jit(solution)/shard_map/ppermute | solution.py:47
  45.4 0.2 collective-permute-done.refs_1_
  45.7 3.7 %collective-permute-start.14 = (bf16[8,128,128]{2,1,0:T(8,128)(2,1)S(1)}, bf16[8,128,128]{2,1,0:T(8,128)(2,1)S(1)}, u32[]{:S(2)}, u32[]{:S(2)}) collective-permute-start(bf16[8,128,128]{2,1,0:T(8,128)(2,1)S(1)} %get-tuple-element.51), channel_id=1, source_target_pairs={{0,24},{8,16},{16,8},{24,0},{1,25},{9,17},{17,9},{25,1},{2,26},{10... | collective-permute-start | bytes 786440 | tf_op jit(solution)/shard_map/ppermute | solution.py:47
  49.4 0.4 own_states.3
  49.8 0.1 collective-permute-start.8
  49.9 0.1 chip_states.9
  50.0 0.5 collective-permute-start.11
  50.6 0.6 collective-permute-done.8.partner
  51.2 1.6 %collective-permute-start.9 = (bf16[2,3,64,128]{3,2,1,0:T(8,128)(2,1)S(1)}, bf16[2,3,64,128]{3,2,1,0:T(8,128)(2,1)S(1)}, u32[]{:S(2)}, u32[]{:S(2)}) collective-permute-start(bf16[2,3,64,128]{3,2,1,0:T(8,128)(2,1)S(1)} %chip_states.7), channel_id=1, source_target_pairs={{0,2},{1,3},{2,0},{3,1},{4,6},{5,7},{6,4},{7,5},{8,10},{9,11},{10,... | collective-permute-start | bytes 294920 | tf_op jit(solution)/shard_map/ppermute | solution.py:47
  52.8 4.4 %gradients.3 = (bf16[1,512,1024]{2,1,0:T(8,128)(2,1)}, bf16[1,512,1024]{2,1,0:T(8,128)(2,1)}, bf16[1,512,1024]{2,1,0:T(8,128)(2,1)}, f32[8,128]{1,0:T(8,128)S(1)}) custom-call(bf16[16,128,128]{2,1,0:T(8,128)(2,1)S(1)} %get-tuple-element.38.refs_0_, bf16[16,128,128]{2,1,0:T(8,128)(2,1)S(1)} %collective-permute-done.3.refs_1_, ...), custom_call_target="tpu_custom_call" | custom-call | flops 1000 | bytes 2048 | tf_op jit(solution)/shard_map/gradients/pallas_call | solution.py:359
  57.3 3.2 %collective-permute-start.12 = (bf16[3,64,128]{2,1,0:T(8,128)(2,1)S(1)}, bf16[3,64,128]{2,1,0:T(8,128)(2,1)S(1)}, u32[]{:S(2)}, u32[]{:S(2)}) collective-permute-start(bf16[3,64,128]{2,1,0:T(8,128)(2,1)S(1)} %chip_states.10), channel_id=1, source_target_pairs={{0,4},{1,5},{2,6},{3,7},{4,0},{5,1},{6,2},{7,3},{8,12},{9,13},{10,... | collective-permute-start | bytes 147464 | tf_op jit(solution)/shard_map/ppermute | solution.py:47
  60.5 3.2 %gradients.4 = (bf16[1,512,1024]{2,1,0:T(8,128)(2,1)}, bf16[1,512,1024]{2,1,0:T(8,128)(2,1)}, bf16[1,512,1024]{2,1,0:T(8,128)(2,1)}, f32[8,128]{1,0:T(8,128)S(1)}) custom-call(bf16[8,128,128]{2,1,0:T(8,128)(2,1)S(1)} %get-tuple-element.49.refs_0_, ...), custom_call_target="tpu_custom_call", output_to_operand_aliasing={{0}: (6, {}), {1}: (7, {}), {2}: (8, {})} | custom-call | flops 1000 | bytes 2048 | tf_op jit(solution)/shard_map/gradients/pallas_call | solution.py:359
  63.7 0.1 chip_states.11
  63.8 0.1 collective-permute-start.16
  63.9 1.3 %collective-permute-done.16.refs_5_ = bf16[2,3,64,128]{3,2,1,0:T(8,128)(2,1)S(1)} collective-permute-done((bf16[2,3,64,128]{3,2,1,0:T(8,128)(2,1)S(1)}, bf16[2,3,64,128]{3,2,1,0:T(8,128)(2,1)S(1)}, u32[]{:S(2)}, u32[]{:S(2)}) %collective-permute-start.16) | collective-permute-done | bytes 98336 | tf_op jit(solution)/shard_map/ppermute | solution.py:47
  65.2 4.9 %gradients.5 = (bf16[1,512,1024]{2,1,0:T(8,128)(2,1)}, bf16[1,512,1024]{2,1,0:T(8,128)(2,1)}, bf16[1,512,1024]{2,1,0:T(8,128)(2,1)}, f32[8,128]{1,0:T(8,128)}) custom-call(bf16[12,128,128]{2,1,0:T(8,128)(2,1)S(1)} %get-tuple-element.34.refs_0_, ...), custom_call_target="tpu_custom_call", output_to_operand_aliasing={{0}: (6, {}), {1}: (7, {}), {2}: (8, {})} | custom-call | flops 1000 | bytes 2048 | tf_op jit(solution)/shard_map/gradients/pallas_call | solution.py:359
  (15 shorter events, 0.2 us)
Async XLA Ops:
  2.5 27.2 %collective-permute-start.3 = (bf16[16,128,128]{2,1,0:T(8,128)(2,1)S(1)}, bf16[16,128,128]{2,1,0:T(8,128)(2,1)S(1)}, u32[]{:S(2)}, u32[]{:S(2)}) collective-permute-start(bf16[16,128,128]{2,1,0:T(8,128)(2,1)S(1)} %get-tuple-element.39), channel_id=1, source_target_pairs={{0,16},{8,24},{16,0},{24,8},{1,17},{9,25},{17,1},{25,9},{2,18},{10... | collective-permute-start | bytes 1572872 | tf_op jit(solution)/shard_map/ppermute | solution.py:47
  5.5 26.4 %collective-permute-start.4 = (bf16[16,128,128]{2,1,0:T(8,128)(2,1)S(1)}, bf16[16,128,128]{2,1,0:T(8,128)(2,1)S(1)}, u32[]{:S(2)}, u32[]{:S(2)}) collective-permute-start(bf16[16,128,128]{2,1,0:T(8,128)(2,1)S(1)} %get-tuple-element.40), channel_id=1, source_target_pairs={{0,24},{8,16},{16,8},{24,0},{1,25},{9,17},{17,9},{25,1},{2,26},{10... | collective-permute-start | bytes 1572872 | tf_op jit(solution)/shard_map/ppermute | solution.py:47
  7.0 25.0 %collective-permute-start.5 = (bf16[16,128,128]{2,1,0:T(8,128)(2,1)S(1)}, bf16[16,128,128]{2,1,0:T(8,128)(2,1)S(1)}, u32[]{:S(2)}, u32[]{:S(2)}) collective-permute-start(bf16[16,128,128]{2,1,0:T(8,128)(2,1)S(1)} %get-tuple-element.41), channel_id=1, source_target_pairs={{0,8},{8,0},{16,24},{24,16},{1,9},{9,1},{17,25},{25,17},{2,10},{10... | collective-permute-start | bytes 1572872 | tf_op jit(solution)/shard_map/ppermute | solution.py:47
  9.2 36.5 %collective-permute-start = (bf16[12,128,128]{2,1,0:T(8,128)(2,1)S(1)}, bf16[12,128,128]{2,1,0:T(8,128)(2,1)S(1)}, u32[]{:S(2)}, u32[]{:S(2)}) collective-permute-start(bf16[12,128,128]{2,1,0:T(8,128)(2,1)S(1)} %get-tuple-element.35), channel_id=1, source_target_pairs={{0,16},{8,24},{16,0},{24,8},{1,17},{9,25},{17,1},{25,9},{2,18},{10... | collective-permute-start | bytes 1179656 | tf_op jit(solution)/shard_map/ppermute | solution.py:47
  11.2 38.1 %collective-permute-start.1 = (bf16[12,128,128]{2,1,0:T(8,128)(2,1)S(1)}, bf16[12,128,128]{2,1,0:T(8,128)(2,1)S(1)}, u32[]{:S(2)}, u32[]{:S(2)}) collective-permute-start(bf16[12,128,128]{2,1,0:T(8,128)(2,1)S(1)} %get-tuple-element.36), channel_id=1, source_target_pairs={{0,24},{8,16},{16,8},{24,0},{1,25},{9,17},{17,9},{25,1},{2,26},{10... | collective-permute-start | bytes 1179656 | tf_op jit(solution)/shard_map/ppermute | solution.py:47
  29.7 19.6 %collective-permute-start.2 = (bf16[12,128,128]{2,1,0:T(8,128)(2,1)S(1)}, bf16[12,128,128]{2,1,0:T(8,128)(2,1)S(1)}, u32[]{:S(2)}, u32[]{:S(2)}) collective-permute-start(bf16[12,128,128]{2,1,0:T(8,128)(2,1)S(1)} %get-tuple-element.37), channel_id=1, source_target_pairs={{0,8},{8,0},{16,24},{24,16},{1,9},{9,1},{17,25},{25,17},{2,10},{10... | collective-permute-start | bytes 1179656 | tf_op jit(solution)/shard_map/ppermute | solution.py:47
  32.4 1.5 %collective-permute-start.6 = (bf16[2,5,64,128]{3,2,1,0:T(8,128)(2,1)S(1)}, bf16[2,5,64,128]{3,2,1,0:T(8,128)(2,1)S(1)}, u32[]{:S(2)}, u32[]{:S(2)}) collective-permute-start(bf16[2,5,64,128]{3,2,1,0:T(8,128)(2,1)S(1)} %get-tuple-element.43), channel_id=1, source_target_pairs={{0,1},{1,0},{2,3},{3,2},{4,5},{5,4},{6,7},{7,6},{8,9},{9,8},{10,11... | collective-permute-start | bytes 491528 | tf_op jit(solution)/shard_map/ppermute | solution.py:47
  33.9 6.3 %collective-permute-start.7 = (bf16[2,5,64,128]{3,2,1,0:T(8,128)(2,1)S(1)}, bf16[2,5,64,128]{3,2,1,0:T(8,128)(2,1)S(1)}, u32[]{:S(2)}, u32[]{:S(2)}) collective-permute-start(bf16[2,5,64,128]{3,2,1,0:T(8,128)(2,1)S(1)} %chip_states.6), channel_id=1, source_target_pairs={{0,2},{1,3},{2,0},{3,1},{4,6},{5,7},{6,4},{7,5},{8,10},{9,11},{10,... | collective-permute-start | bytes 491528 | tf_op jit(solution)/shard_map/ppermute | solution.py:47
  40.3 9.6 %collective-permute-start.10 = (bf16[5,64,128]{2,1,0:T(8,128)(2,1)S(1)}, bf16[5,64,128]{2,1,0:T(8,128)(2,1)S(1)}, u32[]{:S(2)}, u32[]{:S(2)}) collective-permute-start(bf16[5,64,128]{2,1,0:T(8,128)(2,1)S(1)} %chip_states.8), channel_id=1, source_target_pairs={{0,4},{1,5},{2,6},{3,7},{4,0},{5,1},{6,2},{7,3},{8,12},{9,13},{10,... | collective-permute-start | bytes 245768 | tf_op jit(solution)/shard_map/ppermute | solution.py:47
  42.9 17.5 %collective-permute-start.13 = (bf16[8,128,128]{2,1,0:T(8,128)(2,1)S(1)}, bf16[8,128,128]{2,1,0:T(8,128)(2,1)S(1)}, u32[]{:S(2)}, u32[]{:S(2)}) collective-permute-start(bf16[8,128,128]{2,1,0:T(8,128)(2,1)S(1)} %get-tuple-element.50), channel_id=1, source_target_pairs={{0,16},{8,24},{16,0},{24,8},{1,17},{9,25},{17,1},{25,9},{2,18},{10... | collective-permute-start | bytes 786440 | tf_op jit(solution)/shard_map/ppermute | solution.py:47
  45.7 14.8 %collective-permute-start.14 = (bf16[8,128,128]{2,1,0:T(8,128)(2,1)S(1)}, bf16[8,128,128]{2,1,0:T(8,128)(2,1)S(1)}, u32[]{:S(2)}, u32[]{:S(2)}) collective-permute-start(bf16[8,128,128]{2,1,0:T(8,128)(2,1)S(1)} %get-tuple-element.51), channel_id=1, source_target_pairs={{0,24},{8,16},{16,8},{24,0},{1,25},{9,17},{17,9},{25,1},{2,26},{10... | collective-permute-start | bytes 786440 | tf_op jit(solution)/shard_map/ppermute | solution.py:47
  49.3 11.1 %collective-permute-start.15 = (bf16[8,128,128]{2,1,0:T(8,128)(2,1)S(1)}, bf16[8,128,128]{2,1,0:T(8,128)(2,1)S(1)}, u32[]{:S(2)}, u32[]{:S(2)}) collective-permute-start(bf16[8,128,128]{2,1,0:T(8,128)(2,1)S(1)} %get-tuple-element.52), channel_id=1, source_target_pairs={{0,8},{8,0},{16,24},{24,16},{1,9},{9,1},{17,25},{25,17},{2,10},{10... | collective-permute-start | bytes 786440 | tf_op jit(solution)/shard_map/ppermute | solution.py:47
  49.8 1.4 %collective-permute-start.8 = (bf16[2,3,64,128]{3,2,1,0:T(8,128)(2,1)S(1)}, bf16[2,3,64,128]{3,2,1,0:T(8,128)(2,1)S(1)}, u32[]{:S(2)}, u32[]{:S(2)}) collective-permute-start(bf16[2,3,64,128]{3,2,1,0:T(8,128)(2,1)S(1)} %get-tuple-element.45), channel_id=1, source_target_pairs={{0,1},{1,0},{2,3},{3,2},{4,5},{5,4},{6,7},{7,6},{8,9},{9,8},{10,11... | collective-permute-start | bytes 294920 | tf_op jit(solution)/shard_map/ppermute | solution.py:47
  50.0 2.8 %collective-permute-start.11 = (bf16[2,5,64,128]{3,2,1,0:T(8,128)(2,1)S(1)}, bf16[2,5,64,128]{3,2,1,0:T(8,128)(2,1)S(1)}, u32[]{:S(2)}, u32[]{:S(2)}) collective-permute-start(bf16[2,5,64,128]{3,2,1,0:T(8,128)(2,1)S(1)} %get-tuple-element.47), channel_id=1, source_target_pairs={{0,1},{1,0},{2,3},{3,2},{4,5},{5,4},{6,7},{7,6},{8,9},{9,8},{10,11... | collective-permute-start | bytes 491528 | tf_op jit(solution)/shard_map/ppermute | solution.py:47
  51.2 6.0 %collective-permute-start.9 = (bf16[2,3,64,128]{3,2,1,0:T(8,128)(2,1)S(1)}, bf16[2,3,64,128]{3,2,1,0:T(8,128)(2,1)S(1)}, u32[]{:S(2)}, u32[]{:S(2)}) collective-permute-start(bf16[2,3,64,128]{3,2,1,0:T(8,128)(2,1)S(1)} %chip_states.7), channel_id=1, source_target_pairs={{0,2},{1,3},{2,0},{3,1},{4,6},{5,7},{6,4},{7,5},{8,10},{9,11},{10,... | collective-permute-start | bytes 294920 | tf_op jit(solution)/shard_map/ppermute | solution.py:47
  57.3 6.4 %collective-permute-start.12 = (bf16[3,64,128]{2,1,0:T(8,128)(2,1)S(1)}, bf16[3,64,128]{2,1,0:T(8,128)(2,1)S(1)}, u32[]{:S(2)}, u32[]{:S(2)}) collective-permute-start(bf16[3,64,128]{2,1,0:T(8,128)(2,1)S(1)} %chip_states.10), channel_id=1, source_target_pairs={{0,4},{1,5},{2,6},{3,7},{4,0},{5,1},{6,2},{7,3},{8,12},{9,13},{10,... | collective-permute-start | bytes 147464 | tf_op jit(solution)/shard_map/ppermute | solution.py:47
  63.8 1.4 %collective-permute-start.16 = (bf16[2,3,64,128]{3,2,1,0:T(8,128)(2,1)S(1)}, bf16[2,3,64,128]{3,2,1,0:T(8,128)(2,1)S(1)}, u32[]{:S(2)}, u32[]{:S(2)}) collective-permute-start(bf16[2,3,64,128]{3,2,1,0:T(8,128)(2,1)S(1)} %get-tuple-element.58), channel_id=1, source_target_pairs={{0,1},{1,0},{2,3},{3,2},{4,5},{5,4},{6,7},{7,6},{8,9},{9,8},{10,11... | collective-permute-start | bytes 294920 | tf_op jit(solution)/shard_map/ppermute | solution.py:47

commit v9 on v7

--- a/solution.py
+++ b/solution.py
@@ -381,8 +381,7 @@
     group = full // parts
     heads = group // HD
     factor = (HD * rows * parts * spans) ** -0.5
-    late = max(1, heads // 4)
-    middle = (heads - late) // 2
+    late, middle = max(1, heads // 4), max(1, heads * 3 // 8)
     chunks = [heads - late - middle, middle, late]
     arrays = (query, keys, values, grad_out)
     first = pack_first(arrays, parts, heads, chunks[0], late)
@@ -398,7 +397,7 @@
     early, arrived = exchanged(*own_states(received[0], chunks[0], late, []))
     *held, token = gradients([(received[0], early, 0, 0, chunks[0])], (), group, factor)
     *held, ready = gradients([(received[2], early, chunks[0], heads - late, late)], held, group, factor)
-    second, _ = exchanged(*own_states(received[1], middle, 0, [arrived[0]]), [token], [ready])
+    second, _ = exchanged(*own_states(received[1], middle, 0, [arrived[0]]), [token, received[2][1]], [ready])
     *held, _ = gradients([(received[1], second, 0, chunks[0], middle)], held, group, factor)
     return tuple(held)
 

time: 70.4 us -> 70.4 us (level)
  no operation moved by 1% of the time
where the time goes in v9:
time: 70.4 us; the launch traced here: 70.1 us
  waiting for transfers between devices  25.9 us (37%)
  starting transfers between devices  25.7 us (37%)
  Pallas kernels  17.8 us (25%)
  between operations  0.77 us (1%)
    ppermute x17, waiting for transfers between devices, send(): lax.ppermute(value, axis, [(index, target(index)) for index in range(coun...  25.9 us
    ppermute x17, starting transfers between devices, send(): lax.ppermute(value, axis, [(index, target(index)) for index in range(coun...  25.7 us
    pallas_call x3, Pallas kernels, gradients(): pl.pallas_call(functools.partial(grads_kernel, parts, factor, [item[2:] f...  12.5 us
    pallas_call x1, Pallas kernels, pack_rest(): pl.pallas_call(functools.partial(rest_kernel, parts, heads, chunks), in_s...  2.15 us
    pallas_call x1, Pallas kernels, pack_first(): pl.pallas_call(functools.partial(first_kernel, parts, heads, count, late)...  1.85 us
  transfers between devices with their start and end apart: 17, of which 6 were waited for; matrix products, arithmetic and copies ran while one was open for 0% of the time, Pallas kernels for 16%

profile of v9, /device:TPU:0, one launch (start us, length us, event | category | flops | bytes accessed | tf_op | source)
XLA Modules:
  0.0 70.1 jit_solution(8853013704050505868)
XLA Ops:
  0.6 1.9 %pack.3 = (bf16[16,128,128]{2,1,0:T(8,128)(2,1)S(1)}, bf16[16,128,128]{2,1,0:T(8,128)(2,1)S(1)}, bf16[16,128,128]{2,1,0:T(8,128)(2,1)S(1)}) custom-call(bf16[1,128,4096]{2,1,0:T(8,128)(2,1)} %refs_0_.3, bf16[1,128,4096]{2,1,0:T(8,128)(2,1)} %refs_1_.3, bf16[1,128,4096]{2,1,0:T(8,128)(2,1)} %refs_2_.3, bf16[1,128,4096]{2,1,0:T(8,128)(2,1)} %refs_3_.3), custom_call_target="tpu_custom_call" | custom-call | flops 1000 | bytes 2048 | tf_op jit(solution)/shard_map/pack/pallas_call | solution.py:92
  2.5 3.0 %collective-permute-start.3 = (bf16[16,128,128]{2,1,0:T(8,128)(2,1)S(1)}, bf16[16,128,128]{2,1,0:T(8,128)(2,1)S(1)}, u32[]{:S(2)}, u32[]{:S(2)}) collective-permute-start(bf16[16,128,128]{2,1,0:T(8,128)(2,1)S(1)} %get-tuple-element.39), channel_id=1, source_target_pairs={{0,16},{8,24},{16,0},{24,8},{1,17},{9,25},{17,1},{25,9},{2,18},{10... | collective-permute-start | bytes 1572872 | tf_op jit(solution)/shard_map/ppermute | solution.py:47
  5.5 1.4 %collective-permute-start.4 = (bf16[16,128,128]{2,1,0:T(8,128)(2,1)S(1)}, bf16[16,128,128]{2,1,0:T(8,128)(2,1)S(1)}, u32[]{:S(2)}, u32[]{:S(2)}) collective-permute-start(bf16[16,128,128]{2,1,0:T(8,128)(2,1)S(1)} %get-tuple-element.40), channel_id=1, source_target_pairs={{0,24},{8,16},{16,8},{24,0},{1,25},{9,17},{17,9},{25,1},{2,26},{10... | collective-permute-start | bytes 1572872 | tf_op jit(solution)/shard_map/ppermute | solution.py:47
  7.0 0.1 collective-permute-start.5
  7.1 2.1 %pack.2 = (bf16[16,128,128]{2,1,0:T(8,128)(2,1)S(1)}, bf16[12,128,128]{2,1,0:T(8,128)(2,1)S(1)}, bf16[12,128,128]{2,1,0:T(8,128)(2,1)S(1)}, bf16[12,128,128]{2,1...) custom-call(bf16[1,128,4096]{2,1,0:T(8,128)(2,1)} %refs_0_.3, ...), custom_call_target="tpu_custom_call" | custom-call | flops 1000 | bytes 2048 | tf_op jit(solution)/shard_map/pack/pallas_call | solution.py:135
  9.2 2.0 %collective-permute-start = (bf16[12,128,128]{2,1,0:T(8,128)(2,1)S(1)}, bf16[12,128,128]{2,1,0:T(8,128)(2,1)S(1)}, u32[]{:S(2)}, u32[]{:S(2)}) collective-permute-start(bf16[12,128,128]{2,1,0:T(8,128)(2,1)S(1)} %get-tuple-element.35), channel_id=1, source_target_pairs={{0,16},{8,24},{16,0},{24,8},{1,17},{9,25},{17,1},{25,9},{2,18},{10... | collective-permute-start | bytes 1179656 | tf_op jit(solution)/shard_map/ppermute | solution.py:47
  11.2 1.5 %collective-permute-start.1 = (bf16[12,128,128]{2,1,0:T(8,128)(2,1)S(1)}, bf16[12,128,128]{2,1,0:T(8,128)(2,1)S(1)}, u32[]{:S(2)}, u32[]{:S(2)}) collective-permute-start(bf16[12,128,128]{2,1,0:T(8,128)(2,1)S(1)} %get-tuple-element.36), channel_id=1, source_target_pairs={{0,24},{8,16},{16,8},{24,0},{1,25},{9,17},{17,9},{25,1},{2,26},{10... | collective-permute-start | bytes 1179656 | tf_op jit(solution)/shard_map/ppermute | solution.py:47
  12.7 17.0 %collective-permute-done.3.refs_1_ = bf16[16,128,128]{2,1,0:T(8,128)(2,1)S(1)} collective-permute-done((bf16[16,128,128]{2,1,0:T(8,128)(2,1)S(1)}, bf16[16,128,128]{2,1,0:T(8,128)(2,1)S(1)}, u32[]{:S(2)}, u32[]{:S(2)}) %collective-permute-start.3) | collective-permute-done | bytes 524320 | tf_op jit(solution)/shard_map/ppermute | solution.py:47
  29.7 2.2 %collective-permute-start.2 = (bf16[12,128,128]{2,1,0:T(8,128)(2,1)S(1)}, bf16[12,128,128]{2,1,0:T(8,128)(2,1)S(1)}, u32[]{:S(2)}, u32[]{:S(2)}) collective-permute-start(bf16[12,128,128]{2,1,0:T(8,128)(2,1)S(1)} %get-tuple-element.37), channel_id=1, source_target_pairs={{0,8},{8,0},{16,24},{24,16},{1,9},{9,1},{17,25},{25,17},{2,10},{10... | collective-permute-start | bytes 1179656 | tf_op jit(solution)/shard_map/ppermute | solution.py:47
  31.9 0.4 own_states.2
  32.4 0.1 collective-permute-start.6
  32.4 1.4 %collective-permute-done.6.partner = bf16[2,5,64,128]{3,2,1,0:T(8,128)(2,1)S(1)} collective-permute-done((bf16[2,5,64,128]{3,2,1,0:T(8,128)(2,1)S(1)}, bf16[2,5,64,128]{3,2,1,0:T(8,128)(2,1)S(1)}, u32[]{:S(2)}, u32[]{:S(2)}) %collective-permute-start.6) | collective-permute-done | bytes 163872 | tf_op jit(solution)/shard_map/ppermute | solution.py:47
  33.9 1.6 %collective-permute-start.7 = (bf16[2,5,64,128]{3,2,1,0:T(8,128)(2,1)S(1)}, bf16[2,5,64,128]{3,2,1,0:T(8,128)(2,1)S(1)}, u32[]{:S(2)}, u32[]{:S(2)}) collective-permute-start(bf16[2,5,64,128]{3,2,1,0:T(8,128)(2,1)S(1)} %chip_states.6), channel_id=1, source_target_pairs={{0,2},{1,3},{2,0},{3,1},{4,6},{5,7},{6,4},{7,5},{8,10},{9,11},{10,... | collective-permute-start | bytes 491528 | tf_op jit(solution)/shard_map/ppermute | solution.py:47
  35.5 2.5 %collective-permute-start.12 = (bf16[8,128,128]{2,1,0:T(8,128)(2,1)S(1)}, bf16[8,128,128]{2,1,0:T(8,128)(2,1)S(1)}, u32[]{:S(2)}, u32[]{:S(2)}) collective-permute-start(bf16[8,128,128]{2,1,0:T(8,128)(2,1)S(1)} %get-tuple-element.49), channel_id=1, source_target_pairs={{0,16},{8,24},{16,0},{24,8},{1,17},{9,25},{17,1},{25,9},{2,18},{10... | collective-permute-start | bytes 786440 | tf_op jit(solution)/shard_map/ppermute | solution.py:47
  38.0 2.2 %collective-permute-done.7.refs_4_.refs_0_ = bf16[2,5,64,128]{3,2,1,0:T(8,128)(2,1)S(1)} collective-permute-done((bf16[2,5,64,128]{3,2,1,0:T(8,128)(2,1)S(1)}, bf16[2,5,64,128]{3,2,1,0:T(8,128)(2,1)S(1)}, u32[]{:S(2)}, u32[]{:S(2)}) %collective-permute-start.7) | collective-permute-done | bytes 163872 | tf_op jit(solution)/shard_map/ppermute | solution.py:47
  40.2 0.1 chip_states.8
  40.3 2.7 %collective-permute-start.10 = (bf16[5,64,128]{2,1,0:T(8,128)(2,1)S(1)}, bf16[5,64,128]{2,1,0:T(8,128)(2,1)S(1)}, u32[]{:S(2)}, u32[]{:S(2)}) collective-permute-start(bf16[5,64,128]{2,1,0:T(8,128)(2,1)S(1)} %chip_states.8), channel_id=1, source_target_pairs={{0,4},{1,5},{2,6},{3,7},{4,0},{5,1},{6,2},{7,3},{8,12},{9,13},{10,... | collective-permute-start | bytes 245768 | tf_op jit(solution)/shard_map/ppermute | solution.py:47
  42.9 3.4 %collective-permute-done.refs_1_ = bf16[12,128,128]{2,1,0:T(8,128)(2,1)S(1)} collective-permute-done((bf16[12,128,128]{2,1,0:T(8,128)(2,1)S(1)}, bf16[12,128,128]{2,1,0:T(8,128)(2,1)S(1)}, u32[]{:S(2)}, u32[]{:S(2)}) %collective-permute-start) | collective-permute-done | bytes 393248 | tf_op jit(solution)/shard_map/ppermute | solution.py:47
  46.4 3.0 %collective-permute-start.14 = (bf16[8,128,128]{2,1,0:T(8,128)(2,1)S(1)}, bf16[8,128,128]{2,1,0:T(8,128)(2,1)S(1)}, u32[]{:S(2)}, u32[]{:S(2)}) collective-permute-start(bf16[8,128,128]{2,1,0:T(8,128)(2,1)S(1)} %get-tuple-element.51), channel_id=1, source_target_pairs={{0,24},{8,16},{16,8},{24,0},{1,25},{9,17},{17,9},{25,1},{2,26},{10... | collective-permute-start | bytes 786440 | tf_op jit(solution)/shard_map/ppermute | solution.py:47
  49.3 0.5 collective-permute-start.15
  49.8 0.4 own_states.3
  50.3 0.1 collective-permute-start.8
  50.3 0.1 chip_states.9
  50.5 0.5 collective-permute-start.11
  51.0 0.6 collective-permute-done.8.partner
  51.7 1.7 %collective-permute-start.9 = (bf16[2,3,64,128]{3,2,1,0:T(8,128)(2,1)S(1)}, bf16[2,3,64,128]{3,2,1,0:T(8,128)(2,1)S(1)}, u32[]{:S(2)}, u32[]{:S(2)}) collective-permute-start(bf16[2,3,64,128]{3,2,1,0:T(8,128)(2,1)S(1)} %chip_states.7), channel_id=1, source_target_pairs={{0,2},{1,3},{2,0},{3,1},{4,6},{5,7},{6,4},{7,5},{8,10},{9,11},{10,... | collective-permute-start | bytes 294920 | tf_op jit(solution)/shard_map/ppermute | solution.py:47
  53.4 4.4 %gradients.3 = (bf16[1,512,1024]{2,1,0:T(8,128)(2,1)}, bf16[1,512,1024]{2,1,0:T(8,128)(2,1)}, bf16[1,512,1024]{2,1,0:T(8,128)(2,1)}, f32[8,128]{1,0:T(8,128)S(1)}) custom-call(bf16[16,128,128]{2,1,0:T(8,128)(2,1)S(1)} %get-tuple-element.38.refs_0_, bf16[16,128,128]{2,1,0:T(8,128)(2,1)S(1)} %collective-permute-done.3.refs_1_, ...), custom_call_target="tpu_custom_call" | custom-call | flops 1000 | bytes 2048 | tf_op jit(solution)/shard_map/gradients/pallas_call | solution.py:359
  57.8 2.7 %collective-permute-start.13 = (bf16[3,64,128]{2,1,0:T(8,128)(2,1)S(1)}, bf16[3,64,128]{2,1,0:T(8,128)(2,1)S(1)}, u32[]{:S(2)}, u32[]{:S(2)}) collective-permute-start(bf16[3,64,128]{2,1,0:T(8,128)(2,1)S(1)} %chip_states.10), channel_id=1, source_target_pairs={{0,4},{1,5},{2,6},{3,7},{4,0},{5,1},{6,2},{7,3},{8,12},{9,13},{10,... | collective-permute-start | bytes 147464 | tf_op jit(solution)/shard_map/ppermute | solution.py:47
  60.5 3.2 %gradients.4 = (bf16[1,512,1024]{2,1,0:T(8,128)(2,1)}, bf16[1,512,1024]{2,1,0:T(8,128)(2,1)}, bf16[1,512,1024]{2,1,0:T(8,128)(2,1)}, f32[8,128]{1,0:T(8,128)S(1)}) custom-call(bf16[8,128,128]{2,1,0:T(8,128)(2,1)S(1)} %get-tuple-element.50.refs_0_, ...), custom_call_target="tpu_custom_call", output_to_operand_aliasing={{0}: (6, {}), {1}: (7, {}), {2}: (8, {})} | custom-call | flops 1000 | bytes 2048 | tf_op jit(solution)/shard_map/gradients/pallas_call | solution.py:359
  63.7 0.1 chip_states.11
  63.9 1.3 %collective-permute-done.16.refs_5_ = bf16[2,3,64,128]{3,2,1,0:T(8,128)(2,1)S(1)} collective-permute-done((bf16[2,3,64,128]{3,2,1,0:T(8,128)(2,1)S(1)}, bf16[2,3,64,128]{3,2,1,0:T(8,128)(2,1)S(1)}, u32[]{:S(2)}, u32[]{:S(2)}) %collective-permute-start.16) | collective-permute-done | bytes 98336 | tf_op jit(solution)/shard_map/ppermute | solution.py:47
  65.2 4.9 %gradients.5 = (bf16[1,512,1024]{2,1,0:T(8,128)(2,1)}, bf16[1,512,1024]{2,1,0:T(8,128)(2,1)}, bf16[1,512,1024]{2,1,0:T(8,128)(2,1)}, f32[8,128]{1,0:T(8,128)}) custom-call(bf16[12,128,128]{2,1,0:T(8,128)(2,1)S(1)} %get-tuple-element.34.refs_0_, ...), custom_call_target="tpu_custom_call", output_to_operand_aliasing={{0}: (6, {}), {1}: (7, {}), {2}: (8, {})} | custom-call | flops 1000 | bytes 2048 | tf_op jit(solution)/shard_map/gradients/pallas_call | solution.py:359
  (15 shorter events, 0.2 us)
Async XLA Ops:
  2.5 27.2 %collective-permute-start.3 = (bf16[16,128,128]{2,1,0:T(8,128)(2,1)S(1)}, bf16[16,128,128]{2,1,0:T(8,128)(2,1)S(1)}, u32[]{:S(2)}, u32[]{:S(2)}) collective-permute-start(bf16[16,128,128]{2,1,0:T(8,128)(2,1)S(1)} %get-tuple-element.39), channel_id=1, source_target_pairs={{0,16},{8,24},{16,0},{24,8},{1,17},{9,25},{17,1},{25,9},{2,18},{10... | collective-permute-start | bytes 1572872 | tf_op jit(solution)/shard_map/ppermute | solution.py:47
  5.5 26.4 %collective-permute-start.4 = (bf16[16,128,128]{2,1,0:T(8,128)(2,1)S(1)}, bf16[16,128,128]{2,1,0:T(8,128)(2,1)S(1)}, u32[]{:S(2)}, u32[]{:S(2)}) collective-permute-start(bf16[16,128,128]{2,1,0:T(8,128)(2,1)S(1)} %get-tuple-element.40), channel_id=1, source_target_pairs={{0,24},{8,16},{16,8},{24,0},{1,25},{9,17},{17,9},{25,1},{2,26},{10... | collective-permute-start | bytes 1572872 | tf_op jit(solution)/shard_map/ppermute | solution.py:47
  7.0 25.0 %collective-permute-start.5 = (bf16[16,128,128]{2,1,0:T(8,128)(2,1)S(1)}, bf16[16,128,128]{2,1,0:T(8,128)(2,1)S(1)}, u32[]{:S(2)}, u32[]{:S(2)}) collective-permute-start(bf16[16,128,128]{2,1,0:T(8,128)(2,1)S(1)} %get-tuple-element.41), channel_id=1, source_target_pairs={{0,8},{8,0},{16,24},{24,16},{1,9},{9,1},{17,25},{25,17},{2,10},{10... | collective-permute-start | bytes 1572872 | tf_op jit(solution)/shard_map/ppermute | solution.py:47
  9.2 37.1 %collective-permute-start = (bf16[12,128,128]{2,1,0:T(8,128)(2,1)S(1)}, bf16[12,128,128]{2,1,0:T(8,128)(2,1)S(1)}, u32[]{:S(2)}, u32[]{:S(2)}) collective-permute-start(bf16[12,128,128]{2,1,0:T(8,128)(2,1)S(1)} %get-tuple-element.35), channel_id=1, source_target_pairs={{0,16},{8,24},{16,0},{24,8},{1,17},{9,25},{17,1},{25,9},{2,18},{10... | collective-permute-start | bytes 1179656 | tf_op jit(solution)/shard_map/ppermute | solution.py:47
  11.2 38.1 %collective-permute-start.1 = (bf16[12,128,128]{2,1,0:T(8,128)(2,1)S(1)}, bf16[12,128,128]{2,1,0:T(8,128)(2,1)S(1)}, u32[]{:S(2)}, u32[]{:S(2)}) collective-permute-start(bf16[12,128,128]{2,1,0:T(8,128)(2,1)S(1)} %get-tuple-element.36), channel_id=1, source_target_pairs={{0,24},{8,16},{16,8},{24,0},{1,25},{9,17},{17,9},{25,1},{2,26},{10... | collective-permute-start | bytes 1179656 | tf_op jit(solution)/shard_map/ppermute | solution.py:47
  29.7 20.1 %collective-permute-start.2 = (bf16[12,128,128]{2,1,0:T(8,128)(2,1)S(1)}, bf16[12,128,128]{2,1,0:T(8,128)(2,1)S(1)}, u32[]{:S(2)}, u32[]{:S(2)}) collective-permute-start(bf16[12,128,128]{2,1,0:T(8,128)(2,1)S(1)} %get-tuple-element.37), channel_id=1, source_target_pairs={{0,8},{8,0},{16,24},{24,16},{1,9},{9,1},{17,25},{25,17},{2,10},{10... | collective-permute-start | bytes 1179656 | tf_op jit(solution)/shard_map/ppermute | solution.py:47
  32.4 1.5 %collective-permute-start.6 = (bf16[2,5,64,128]{3,2,1,0:T(8,128)(2,1)S(1)}, bf16[2,5,64,128]{3,2,1,0:T(8,128)(2,1)S(1)}, u32[]{:S(2)}, u32[]{:S(2)}) collective-permute-start(bf16[2,5,64,128]{3,2,1,0:T(8,128)(2,1)S(1)} %get-tuple-element.43), channel_id=1, source_target_pairs={{0,1},{1,0},{2,3},{3,2},{4,5},{5,4},{6,7},{7,6},{8,9},{9,8},{10,11... | collective-permute-start | bytes 491528 | tf_op jit(solution)/shard_map/ppermute | solution.py:47
  33.9 6.3 %collective-permute-start.7 = (bf16[2,5,64,128]{3,2,1,0:T(8,128)(2,1)S(1)}, bf16[2,5,64,128]{3,2,1,0:T(8,128)(2,1)S(1)}, u32[]{:S(2)}, u32[]{:S(2)}) collective-permute-start(bf16[2,5,64,128]{3,2,1,0:T(8,128)(2,1)S(1)} %chip_states.6), channel_id=1, source_target_pairs={{0,2},{1,3},{2,0},{3,1},{4,6},{5,7},{6,4},{7,5},{8,10},{9,11},{10,... | collective-permute-start | bytes 491528 | tf_op jit(solution)/shard_map/ppermute | solution.py:47
  35.5 22.2 %collective-permute-start.12 = (bf16[8,128,128]{2,1,0:T(8,128)(2,1)S(1)}, bf16[8,128,128]{2,1,0:T(8,128)(2,1)S(1)}, u32[]{:S(2)}, u32[]{:S(2)}) collective-permute-start(bf16[8,128,128]{2,1,0:T(8,128)(2,1)S(1)} %get-tuple-element.49), channel_id=1, source_target_pairs={{0,16},{8,24},{16,0},{24,8},{1,17},{9,25},{17,1},{25,9},{2,18},{10... | collective-permute-start | bytes 786440 | tf_op jit(solution)/shard_map/ppermute | solution.py:47
  40.3 10.1 %collective-permute-start.10 = (bf16[5,64,128]{2,1,0:T(8,128)(2,1)S(1)}, bf16[5,64,128]{2,1,0:T(8,128)(2,1)S(1)}, u32[]{:S(2)}, u32[]{:S(2)}) collective-permute-start(bf16[5,64,128]{2,1,0:T(8,128)(2,1)S(1)} %chip_states.8), channel_id=1, source_target_pairs={{0,4},{1,5},{2,6},{3,7},{4,0},{5,1},{6,2},{7,3},{8,12},{9,13},{10,... | collective-permute-start | bytes 245768 | tf_op jit(solution)/shard_map/ppermute | solution.py:47
  46.4 14.1 %collective-permute-start.14 = (bf16[8,128,128]{2,1,0:T(8,128)(2,1)S(1)}, bf16[8,128,128]{2,1,0:T(8,128)(2,1)S(1)}, u32[]{:S(2)}, u32[]{:S(2)}) collective-permute-start(bf16[8,128,128]{2,1,0:T(8,128)(2,1)S(1)} %get-tuple-element.51), channel_id=1, source_target_pairs={{0,24},{8,16},{16,8},{24,0},{1,25},{9,17},{17,9},{25,1},{2,26},{10... | collective-permute-start | bytes 786440 | tf_op jit(solution)/shard_map/ppermute | solution.py:47
  49.3 11.1 %collective-permute-start.15 = (bf16[8,128,128]{2,1,0:T(8,128)(2,1)S(1)}, bf16[8,128,128]{2,1,0:T(8,128)(2,1)S(1)}, u32[]{:S(2)}, u32[]{:S(2)}) collective-permute-start(bf16[8,128,128]{2,1,0:T(8,128)(2,1)S(1)} %get-tuple-element.52), channel_id=1, source_target_pairs={{0,8},{8,0},{16,24},{24,16},{1,9},{9,1},{17,25},{25,17},{2,10},{10... | collective-permute-start | bytes 786440 | tf_op jit(solution)/shard_map/ppermute | solution.py:47
  50.3 1.4 %collective-permute-start.8 = (bf16[2,3,64,128]{3,2,1,0:T(8,128)(2,1)S(1)}, bf16[2,3,64,128]{3,2,1,0:T(8,128)(2,1)S(1)}, u32[]{:S(2)}, u32[]{:S(2)}) collective-permute-start(bf16[2,3,64,128]{3,2,1,0:T(8,128)(2,1)S(1)} %get-tuple-element.45), channel_id=1, source_target_pairs={{0,1},{1,0},{2,3},{3,2},{4,5},{5,4},{6,7},{7,6},{8,9},{9,8},{10,11... | collective-permute-start | bytes 294920 | tf_op jit(solution)/shard_map/ppermute | solution.py:47
  50.5 2.9 %collective-permute-start.11 = (bf16[2,5,64,128]{3,2,1,0:T(8,128)(2,1)S(1)}, bf16[2,5,64,128]{3,2,1,0:T(8,128)(2,1)S(1)}, u32[]{:S(2)}, u32[]{:S(2)}) collective-permute-start(bf16[2,5,64,128]{3,2,1,0:T(8,128)(2,1)S(1)} %get-tuple-element.47), channel_id=1, source_target_pairs={{0,1},{1,0},{2,3},{3,2},{4,5},{5,4},{6,7},{7,6},{8,9},{9,8},{10,11... | collective-permute-start | bytes 491528 | tf_op jit(solution)/shard_map/ppermute | solution.py:47
  51.7 6.1 %collective-permute-start.9 = (bf16[2,3,64,128]{3,2,1,0:T(8,128)(2,1)S(1)}, bf16[2,3,64,128]{3,2,1,0:T(8,128)(2,1)S(1)}, u32[]{:S(2)}, u32[]{:S(2)}) collective-permute-start(bf16[2,3,64,128]{3,2,1,0:T(8,128)(2,1)S(1)} %chip_states.7), channel_id=1, source_target_pairs={{0,2},{1,3},{2,0},{3,1},{4,6},{5,7},{6,4},{7,5},{8,10},{9,11},{10,... | collective-permute-start | bytes 294920 | tf_op jit(solution)/shard_map/ppermute | solution.py:47
  57.8 5.9 %collective-permute-start.13 = (bf16[3,64,128]{2,1,0:T(8,128)(2,1)S(1)}, bf16[3,64,128]{2,1,0:T(8,128)(2,1)S(1)}, u32[]{:S(2)}, u32[]{:S(2)}) collective-permute-start(bf16[3,64,128]{2,1,0:T(8,128)(2,1)S(1)} %chip_states.10), channel_id=1, source_target_pairs={{0,4},{1,5},{2,6},{3,7},{4,0},{5,1},{6,2},{7,3},{8,12},{9,13},{10,... | collective-permute-start | bytes 147464 | tf_op jit(solution)/shard_map/ppermute | solution.py:47
  63.8 1.4 %collective-permute-start.16 = (bf16[2,3,64,128]{3,2,1,0:T(8,128)(2,1)S(1)}, bf16[2,3,64,128]{3,2,1,0:T(8,128)(2,1)S(1)}, u32[]{:S(2)}, u32[]{:S(2)}) collective-permute-start(bf16[2,3,64,128]{3,2,1,0:T(8,128)(2,1)S(1)} %get-tuple-element.58), channel_id=1, source_target_pairs={{0,1},{1,0},{2,3},{3,2},{4,5},{5,4},{6,7},{7,6},{8,9},{9,8},{10,11... | collective-permute-start | bytes 294920 | tf_op jit(solution)/shard_map/ppermute | solution.py:47

commit v10 on v9

--- a/solution.py
+++ b/solution.py
@@ -396,9 +396,16 @@
     received = [exchange(own, first)] + [exchange(values[0], values[1:]) for values in packed]
     early, arrived = exchanged(*own_states(received[0], chunks[0], late, []))
     *held, token = gradients([(received[0], early, 0, 0, chunks[0])], (), group, factor)
-    *held, ready = gradients([(received[2], early, chunks[0], heads - late, late)], held, group, factor)
-    second, _ = exchanged(*own_states(received[1], middle, 0, [arrived[0]]), [token, received[2][1]], [ready])
-    *held, _ = gradients([(received[1], second, 0, chunks[0], middle)], held, group, factor)
+    second, _ = exchanged(*own_states(received[1], middle, 0, [arrived[0]]), [token], received[2][1:2])
+    *held, _ = gradients(
+        [
+            (received[1], second, 0, chunks[0], middle),
+            (received[2], early, chunks[0], heads - late, late),
+        ],
+        held,
+        group,
+        factor,
+    )
     return tuple(held)
 
 

time: 70.4 us -> 71.8 us (1.020)
  waiting for transfers between devices: 25.9 us -> 28.6 us
  Pallas kernels: 17.8 us -> 16.9 us
    ppermute x17, waiting for transfers between devices: 25.9 us -> 28.6 us  [send(): lax.ppermute(value, axis, [(index, target(index)) for index in range(coun...]
    pallas_call x3 -> x2, Pallas kernels: 12.5 us -> 11.6 us  [gradients(): pl.pallas_call(functools.partial(grads_kernel, parts, factor, [item[2:] f...]
  transfers between devices with their start and end apart: 17 -> 17, of which waited for: 6 -> 8; matrix products, arithmetic and copies ran while one was open for 0% -> 0% of each run, Pallas kernels for 16% -> 11%
where the time goes in v10:
time: 71.8 us; the launch traced here: 71.5 us
  waiting for transfers between devices  28.6 us (40%)
  starting transfers between devices  25.3 us (35%)
  Pallas kernels  16.9 us (24%)
  between operations  0.76 us (1%)
    ppermute x17, waiting for transfers between devices, send(): lax.ppermute(value, axis, [(index, target(index)) for index in range(coun...  28.6 us
    ppermute x17, starting transfers between devices, send(): lax.ppermute(value, axis, [(index, target(index)) for index in range(coun...  25.3 us
    pallas_call x2, Pallas kernels, gradients(): pl.pallas_call(functools.partial(grads_kernel, parts, factor, [item[2:] f...  11.6 us
    pallas_call x1, Pallas kernels, pack_rest(): pl.pallas_call(functools.partial(rest_kernel, parts, heads, chunks), in_s...  2.15 us
    pallas_call x1, Pallas kernels, pack_first(): pl.pallas_call(functools.partial(first_kernel, parts, heads, count, late)...  1.85 us
  transfers between devices with their start and end apart: 17, of which 8 were waited for; matrix products, arithmetic and copies ran while one was open for 0% of the time, Pallas kernels for 11%

profile of v10, /device:TPU:0, one launch (start us, length us, event | category | flops | bytes accessed | tf_op | source)
XLA Modules:
  0.0 71.5 jit_solution(12133879649669934820)
XLA Ops:
  0.6 1.9 %pack.3 = (bf16[16,128,128]{2,1,0:T(8,128)(2,1)S(1)}, bf16[16,128,128]{2,1,0:T(8,128)(2,1)S(1)}, bf16[16,128,128]{2,1,0:T(8,128)(2,1)S(1)}) custom-call(bf16[1,128,4096]{2,1,0:T(8,128)(2,1)} %refs_0_.3, bf16[1,128,4096]{2,1,0:T(8,128)(2,1)} %refs_1_.3, bf16[1,128,4096]{2,1,0:T(8,128)(2,1)} %refs_2_.3, bf16[1,128,4096]{2,1,0:T(8,128)(2,1)} %refs_3_.3), custom_call_target="tpu_custom_call" | custom-call | flops 1000 | bytes 2048 | tf_op jit(solution)/shard_map/pack/pallas_call | solution.py:92
  2.5 3.0 %collective-permute-start.3 = (bf16[16,128,128]{2,1,0:T(8,128)(2,1)S(1)}, bf16[16,128,128]{2,1,0:T(8,128)(2,1)S(1)}, u32[]{:S(2)}, u32[]{:S(2)}) collective-permute-start(bf16[16,128,128]{2,1,0:T(8,128)(2,1)S(1)} %get-tuple-element.35), channel_id=1, source_target_pairs={{0,16},{8,24},{16,0},{24,8},{1,17},{9,25},{17,1},{25,9},{2,18},{10... | collective-permute-start | bytes 1572872 | tf_op jit(solution)/shard_map/ppermute | solution.py:47
  5.5 1.4 %collective-permute-start.4 = (bf16[16,128,128]{2,1,0:T(8,128)(2,1)S(1)}, bf16[16,128,128]{2,1,0:T(8,128)(2,1)S(1)}, u32[]{:S(2)}, u32[]{:S(2)}) collective-permute-start(bf16[16,128,128]{2,1,0:T(8,128)(2,1)S(1)} %get-tuple-element.36), channel_id=1, source_target_pairs={{0,24},{8,16},{16,8},{24,0},{1,25},{9,17},{17,9},{25,1},{2,26},{10... | collective-permute-start | bytes 1572872 | tf_op jit(solution)/shard_map/ppermute | solution.py:47
  7.0 0.1 collective-permute-start.5
  7.1 2.1 %pack.2 = (bf16[16,128,128]{2,1,0:T(8,128)(2,1)S(1)}, bf16[12,128,128]{2,1,0:T(8,128)(2,1)S(1)}, bf16[12,128,128]{2,1,0:T(8,128)(2,1)S(1)}, bf16[12,128,128]{2,1...) custom-call(bf16[1,128,4096]{2,1,0:T(8,128)(2,1)} %refs_0_.3, ...), custom_call_target="tpu_custom_call" | custom-call | flops 1000 | bytes 2048 | tf_op jit(solution)/shard_map/pack/pallas_call | solution.py:135
  9.2 2.0 %collective-permute-start = (bf16[12,128,128]{2,1,0:T(8,128)(2,1)S(1)}, bf16[12,128,128]{2,1,0:T(8,128)(2,1)S(1)}, u32[]{:S(2)}, u32[]{:S(2)}) collective-permute-start(bf16[12,128,128]{2,1,0:T(8,128)(2,1)S(1)} %get-tuple-element.31), channel_id=1, source_target_pairs={{0,16},{8,24},{16,0},{24,8},{1,17},{9,25},{17,1},{25,9},{2,18},{10... | collective-permute-start | bytes 1179656 | tf_op jit(solution)/shard_map/ppermute | solution.py:47
  11.2 1.5 %collective-permute-start.1 = (bf16[12,128,128]{2,1,0:T(8,128)(2,1)S(1)}, bf16[12,128,128]{2,1,0:T(8,128)(2,1)S(1)}, u32[]{:S(2)}, u32[]{:S(2)}) collective-permute-start(bf16[12,128,128]{2,1,0:T(8,128)(2,1)S(1)} %get-tuple-element.32), channel_id=1, source_target_pairs={{0,24},{8,16},{16,8},{24,0},{1,25},{9,17},{17,9},{25,1},{2,26},{10... | collective-permute-start | bytes 1179656 | tf_op jit(solution)/shard_map/ppermute | solution.py:47
  12.7 17.0 %collective-permute-done.3.refs_1_ = bf16[16,128,128]{2,1,0:T(8,128)(2,1)S(1)} collective-permute-done((bf16[16,128,128]{2,1,0:T(8,128)(2,1)S(1)}, bf16[16,128,128]{2,1,0:T(8,128)(2,1)S(1)}, u32[]{:S(2)}, u32[]{:S(2)}) %collective-permute-start.3) | collective-permute-done | bytes 524320 | tf_op jit(solution)/shard_map/ppermute | solution.py:47
  29.7 2.2 %collective-permute-start.2 = (bf16[12,128,128]{2,1,0:T(8,128)(2,1)S(1)}, bf16[12,128,128]{2,1,0:T(8,128)(2,1)S(1)}, u32[]{:S(2)}, u32[]{:S(2)}) collective-permute-start(bf16[12,128,128]{2,1,0:T(8,128)(2,1)S(1)} %get-tuple-element.33), channel_id=1, source_target_pairs={{0,8},{8,0},{16,24},{24,16},{1,9},{9,1},{17,25},{25,17},{2,10},{10... | collective-permute-start | bytes 1179656 | tf_op jit(solution)/shard_map/ppermute | solution.py:47
  31.9 0.4 own_states.2
  32.4 1.4 %collective-permute-done.6.partner = bf16[2,5,64,128]{3,2,1,0:T(8,128)(2,1)S(1)} collective-permute-done((bf16[2,5,64,128]{3,2,1,0:T(8,128)(2,1)S(1)}, bf16[2,5,64,128]{3,2,1,0:T(8,128)(2,1)S(1)}, u32[]{:S(2)}, u32[]{:S(2)}) %collective-permute-start.6) | collective-permute-done | bytes 163872 | tf_op jit(solution)/shard_map/ppermute | solution.py:47
  33.9 1.6 %collective-permute-start.7 = (bf16[2,5,64,128]{3,2,1,0:T(8,128)(2,1)S(1)}, bf16[2,5,64,128]{3,2,1,0:T(8,128)(2,1)S(1)}, u32[]{:S(2)}, u32[]{:S(2)}) collective-permute-start(bf16[2,5,64,128]{3,2,1,0:T(8,128)(2,1)S(1)} %chip_states.6), channel_id=1, source_target_pairs={{0,2},{1,3},{2,0},{3,1},{4,6},{5,7},{6,4},{7,5},{8,10},{9,11},{10,... | collective-permute-start | bytes 491528 | tf_op jit(solution)/shard_map/ppermute | solution.py:47
  35.5 4.7 %collective-permute-done.7.refs_4_.refs_0_ = bf16[2,5,64,128]{3,2,1,0:T(8,128)(2,1)S(1)} collective-permute-done((bf16[2,5,64,128]{3,2,1,0:T(8,128)(2,1)S(1)}, bf16[2,5,64,128]{3,2,1,0:T(8,128)(2,1)S(1)}, u32[]{:S(2)}, u32[]{:S(2)}) %collective-permute-start.7) | collective-permute-done | bytes 163872 | tf_op jit(solution)/shard_map/ppermute | solution.py:47
  40.2 0.1 chip_states.8
  40.3 2.7 %collective-permute-start.10 = (bf16[5,64,128]{2,1,0:T(8,128)(2,1)S(1)}, bf16[5,64,128]{2,1,0:T(8,128)(2,1)S(1)}, u32[]{:S(2)}, u32[]{:S(2)}) collective-permute-start(bf16[5,64,128]{2,1,0:T(8,128)(2,1)S(1)} %chip_states.8), channel_id=1, source_target_pairs={{0,4},{1,5},{2,6},{3,7},{4,0},{5,1},{6,2},{7,3},{8,12},{9,13},{10,... | collective-permute-start | bytes 245768 | tf_op jit(solution)/shard_map/ppermute | solution.py:47
  42.9 2.5 %collective-permute-start.13 = (bf16[8,128,128]{2,1,0:T(8,128)(2,1)S(1)}, bf16[8,128,128]{2,1,0:T(8,128)(2,1)S(1)}, u32[]{:S(2)}, u32[]{:S(2)}) collective-permute-start(bf16[8,128,128]{2,1,0:T(8,128)(2,1)S(1)} %get-tuple-element.45), channel_id=1, source_target_pairs={{0,16},{8,24},{16,0},{24,8},{1,17},{9,25},{17,1},{25,9},{2,18},{10... | collective-permute-start | bytes 786440 | tf_op jit(solution)/shard_map/ppermute | solution.py:47
  45.4 0.2 collective-permute-done.refs_1_
  45.7 1.2 %collective-permute-done.2.refs_3_ = bf16[12,128,128]{2,1,0:T(8,128)(2,1)S(1)} collective-permute-done((bf16[12,128,128]{2,1,0:T(8,128)(2,1)S(1)}, bf16[12,128,128]{2,1,0:T(8,128)(2,1)S(1)}, u32[]{:S(2)}, u32[]{:S(2)}) %collective-permute-start.2) | collective-permute-done | bytes 393248 | tf_op jit(solution)/shard_map/ppermute | solution.py:47
  46.9 0.4 own_states.3
  47.3 0.1 collective-permute-start.8
  47.4 0.1 chip_states.9
  47.5 0.5 collective-permute-start.11
  48.1 2.6 %collective-permute-start.15 = (bf16[8,128,128]{2,1,0:T(8,128)(2,1)S(1)}, bf16[8,128,128]{2,1,0:T(8,128)(2,1)S(1)}, u32[]{:S(2)}, u32[]{:S(2)}) collective-permute-start(bf16[8,128,128]{2,1,0:T(8,128)(2,1)S(1)} %get-tuple-element.49), channel_id=1, source_target_pairs={{0,24},{8,16},{16,8},{24,0},{1,25},{9,17},{17,9},{25,1},{2,26},{10... | collective-permute-start | bytes 786440 | tf_op jit(solution)/shard_map/ppermute | solution.py:47
  50.7 0.5 collective-permute-start.16
  51.3 1.6 %collective-permute-start.9 = (bf16[2,3,64,128]{3,2,1,0:T(8,128)(2,1)S(1)}, bf16[2,3,64,128]{3,2,1,0:T(8,128)(2,1)S(1)}, u32[]{:S(2)}, u32[]{:S(2)}) collective-permute-start(bf16[2,3,64,128]{3,2,1,0:T(8,128)(2,1)S(1)} %chip_states.7), channel_id=1, source_target_pairs={{0,2},{1,3},{2,0},{3,1},{4,6},{5,7},{6,4},{7,5},{8,10},{9,11},{10,... | collective-permute-start | bytes 294920 | tf_op jit(solution)/shard_map/ppermute | solution.py:47
  52.9 4.4 %gradients.2 = (bf16[1,512,1024]{2,1,0:T(8,128)(2,1)}, bf16[1,512,1024]{2,1,0:T(8,128)(2,1)}, bf16[1,512,1024]{2,1,0:T(8,128)(2,1)}, f32[8,128]{1,0:T(8,128)S(1)}) custom-call(bf16[16,128,128]{2,1,0:T(8,128)(2,1)S(1)} %get-tuple-element.34.refs_0_, bf16[16,128,128]{2,1,0:T(8,128)(2,1)S(1)} %collective-permute-done.3.refs_1_, ...), custom_call_target="tpu_custom_call" | custom-call | flops 1000 | bytes 2048 | tf_op jit(solution)/shard_map/gradients/pallas_call | solution.py:359
  57.3 2.7 %collective-permute-start.12 = (bf16[3,64,128]{2,1,0:T(8,128)(2,1)S(1)}, bf16[3,64,128]{2,1,0:T(8,128)(2,1)S(1)}, u32[]{:S(2)}, u32[]{:S(2)}) collective-permute-start(bf16[3,64,128]{2,1,0:T(8,128)(2,1)S(1)} %chip_states.10), channel_id=1, source_target_pairs={{0,4},{1,5},{2,6},{3,7},{4,0},{5,1},{6,2},{7,3},{8,12},{9,13},{10,... | collective-permute-start | bytes 147464 | tf_op jit(solution)/shard_map/ppermute | solution.py:47
  60.0 2.8 %collective-permute-done.12.refs_1_ = bf16[3,64,128]{2,1,0:T(8,128)(2,1)S(1)} collective-permute-done((bf16[3,64,128]{2,1,0:T(8,128)(2,1)S(1)}, bf16[3,64,128]{2,1,0:T(8,128)(2,1)S(1)}, u32[]{:S(2)}, u32[]{:S(2)}) %collective-permute-start.12) | collective-permute-done | bytes 49184 | tf_op jit(solution)/shard_map/ppermute | solution.py:47
  62.8 0.1 chip_states.11
  63.0 0.1 collective-permute-done.16.refs_9_
  63.1 1.2 %collective-permute-done.14.refs_5_ = bf16[2,3,64,128]{3,2,1,0:T(8,128)(2,1)S(1)} collective-permute-done((bf16[2,3,64,128]{3,2,1,0:T(8,128)(2,1)S(1)}, bf16[2,3,64,128]{3,2,1,0:T(8,128)(2,1)S(1)}, u32[]{:S(2)}, u32[]{:S(2)}) %collective-permute-start.14) | collective-permute-done | bytes 98336 | tf_op jit(solution)/shard_map/ppermute | solution.py:47
  64.3 7.2 %gradients.3 = (bf16[1,512,1024]{2,1,0:T(8,128)(2,1)}, bf16[1,512,1024]{2,1,0:T(8,128)(2,1)}, bf16[1,512,1024]{2,1,0:T(8,128)(2,1)}, f32[8,128]{1,0:T(8,128)}) custom-call(bf16[12,128,128]{2,1,0:T(8,128)(2,1)S(1)} %get-tuple-element.30.refs_0_, ...), custom_call_target="tpu_custom_call", output_to_operand_aliasing={{0}: (12, {}), {1}: (13, {}), {2}: (14, {})} | custom-call | flops 1000 | bytes 2048 | tf_op jit(solution)/shard_map/gradients/pallas_call | solution.py:359
  (14 shorter events, 0.3 us)
Async XLA Ops:
  2.5 27.2 %collective-permute-start.3 = (bf16[16,128,128]{2,1,0:T(8,128)(2,1)S(1)}, bf16[16,128,128]{2,1,0:T(8,128)(2,1)S(1)}, u32[]{:S(2)}, u32[]{:S(2)}) collective-permute-start(bf16[16,128,128]{2,1,0:T(8,128)(2,1)S(1)} %get-tuple-element.35), channel_id=1, source_target_pairs={{0,16},{8,24},{16,0},{24,8},{1,17},{9,25},{17,1},{25,9},{2,18},{10... | collective-permute-start | bytes 1572872 | tf_op jit(solution)/shard_map/ppermute | solution.py:47
  5.5 26.4 %collective-permute-start.4 = (bf16[16,128,128]{2,1,0:T(8,128)(2,1)S(1)}, bf16[16,128,128]{2,1,0:T(8,128)(2,1)S(1)}, u32[]{:S(2)}, u32[]{:S(2)}) collective-permute-start(bf16[16,128,128]{2,1,0:T(8,128)(2,1)S(1)} %get-tuple-element.36), channel_id=1, source_target_pairs={{0,24},{8,16},{16,8},{24,0},{1,25},{9,17},{17,9},{25,1},{2,26},{10... | collective-permute-start | bytes 1572872 | tf_op jit(solution)/shard_map/ppermute | solution.py:47
  7.0 25.0 %collective-permute-start.5 = (bf16[16,128,128]{2,1,0:T(8,128)(2,1)S(1)}, bf16[16,128,128]{2,1,0:T(8,128)(2,1)S(1)}, u32[]{:S(2)}, u32[]{:S(2)}) collective-permute-start(bf16[16,128,128]{2,1,0:T(8,128)(2,1)S(1)} %get-tuple-element.37), channel_id=1, source_target_pairs={{0,8},{8,0},{16,24},{24,16},{1,9},{9,1},{17,25},{25,17},{2,10},{10... | collective-permute-start | bytes 1572872 | tf_op jit(solution)/shard_map/ppermute | solution.py:47
  9.2 36.5 %collective-permute-start = (bf16[12,128,128]{2,1,0:T(8,128)(2,1)S(1)}, bf16[12,128,128]{2,1,0:T(8,128)(2,1)S(1)}, u32[]{:S(2)}, u32[]{:S(2)}) collective-permute-start(bf16[12,128,128]{2,1,0:T(8,128)(2,1)S(1)} %get-tuple-element.31), channel_id=1, source_target_pairs={{0,16},{8,24},{16,0},{24,8},{1,17},{9,25},{17,1},{25,9},{2,18},{10... | collective-permute-start | bytes 1179656 | tf_op jit(solution)/shard_map/ppermute | solution.py:47
  11.2 34.4 %collective-permute-start.1 = (bf16[12,128,128]{2,1,0:T(8,128)(2,1)S(1)}, bf16[12,128,128]{2,1,0:T(8,128)(2,1)S(1)}, u32[]{:S(2)}, u32[]{:S(2)}) collective-permute-start(bf16[12,128,128]{2,1,0:T(8,128)(2,1)S(1)} %get-tuple-element.32), channel_id=1, source_target_pairs={{0,24},{8,16},{16,8},{24,0},{1,25},{9,17},{17,9},{25,1},{2,26},{10... | collective-permute-start | bytes 1179656 | tf_op jit(solution)/shard_map/ppermute | solution.py:47
  29.7 17.2 %collective-permute-start.2 = (bf16[12,128,128]{2,1,0:T(8,128)(2,1)S(1)}, bf16[12,128,128]{2,1,0:T(8,128)(2,1)S(1)}, u32[]{:S(2)}, u32[]{:S(2)}) collective-permute-start(bf16[12,128,128]{2,1,0:T(8,128)(2,1)S(1)} %get-tuple-element.33), channel_id=1, source_target_pairs={{0,8},{8,0},{16,24},{24,16},{1,9},{9,1},{17,25},{25,17},{2,10},{10... | collective-permute-start | bytes 1179656 | tf_op jit(solution)/shard_map/ppermute | solution.py:47
  32.4 1.5 %collective-permute-start.6 = (bf16[2,5,64,128]{3,2,1,0:T(8,128)(2,1)S(1)}, bf16[2,5,64,128]{3,2,1,0:T(8,128)(2,1)S(1)}, u32[]{:S(2)}, u32[]{:S(2)}) collective-permute-start(bf16[2,5,64,128]{3,2,1,0:T(8,128)(2,1)S(1)} %get-tuple-element.39), channel_id=1, source_target_pairs={{0,1},{1,0},{2,3},{3,2},{4,5},{5,4},{6,7},{7,6},{8,9},{9,8},{10,11... | collective-permute-start | bytes 491528 | tf_op jit(solution)/shard_map/ppermute | solution.py:47
  33.9 6.3 %collective-permute-start.7 = (bf16[2,5,64,128]{3,2,1,0:T(8,128)(2,1)S(1)}, bf16[2,5,64,128]{3,2,1,0:T(8,128)(2,1)S(1)}, u32[]{:S(2)}, u32[]{:S(2)}) collective-permute-start(bf16[2,5,64,128]{3,2,1,0:T(8,128)(2,1)S(1)} %chip_states.6), channel_id=1, source_target_pairs={{0,2},{1,3},{2,0},{3,1},{4,6},{5,7},{6,4},{7,5},{8,10},{9,11},{10,... | collective-permute-start | bytes 491528 | tf_op jit(solution)/shard_map/ppermute | solution.py:47
  40.3 7.1 %collective-permute-start.10 = (bf16[5,64,128]{2,1,0:T(8,128)(2,1)S(1)}, bf16[5,64,128]{2,1,0:T(8,128)(2,1)S(1)}, u32[]{:S(2)}, u32[]{:S(2)}) collective-permute-start(bf16[5,64,128]{2,1,0:T(8,128)(2,1)S(1)} %chip_states.8), channel_id=1, source_target_pairs={{0,4},{1,5},{2,6},{3,7},{4,0},{5,1},{6,2},{7,3},{8,12},{9,13},{10,... | collective-permute-start | bytes 245768 | tf_op jit(solution)/shard_map/ppermute | solution.py:47
  42.9 17.1 %collective-permute-start.13 = (bf16[8,128,128]{2,1,0:T(8,128)(2,1)S(1)}, bf16[8,128,128]{2,1,0:T(8,128)(2,1)S(1)}, u32[]{:S(2)}, u32[]{:S(2)}) collective-permute-start(bf16[8,128,128]{2,1,0:T(8,128)(2,1)S(1)} %get-tuple-element.45), channel_id=1, source_target_pairs={{0,16},{8,24},{16,0},{24,8},{1,17},{9,25},{17,1},{25,9},{2,18},{10... | collective-permute-start | bytes 786440 | tf_op jit(solution)/shard_map/ppermute | solution.py:47
  47.3 3.9 %collective-permute-start.8 = (bf16[2,3,64,128]{3,2,1,0:T(8,128)(2,1)S(1)}, bf16[2,3,64,128]{3,2,1,0:T(8,128)(2,1)S(1)}, u32[]{:S(2)}, u32[]{:S(2)}) collective-permute-start(bf16[2,3,64,128]{3,2,1,0:T(8,128)(2,1)S(1)} %get-tuple-element.41), channel_id=1, source_target_pairs={{0,1},{1,0},{2,3},{3,2},{4,5},{5,4},{6,7},{7,6},{8,9},{9,8},{10,11... | collective-permute-start | bytes 294920 | tf_op jit(solution)/shard_map/ppermute | solution.py:47
  47.5 5.4 %collective-permute-start.11 = (bf16[2,5,64,128]{3,2,1,0:T(8,128)(2,1)S(1)}, bf16[2,5,64,128]{3,2,1,0:T(8,128)(2,1)S(1)}, u32[]{:S(2)}, u32[]{:S(2)}) collective-permute-start(bf16[2,5,64,128]{3,2,1,0:T(8,128)(2,1)S(1)} %get-tuple-element.43), channel_id=1, source_target_pairs={{0,1},{1,0},{2,3},{3,2},{4,5},{5,4},{6,7},{7,6},{8,9},{9,8},{10,11... | collective-permute-start | bytes 491528 | tf_op jit(solution)/shard_map/ppermute | solution.py:47
  48.1 14.9 %collective-permute-start.15 = (bf16[8,128,128]{2,1,0:T(8,128)(2,1)S(1)}, bf16[8,128,128]{2,1,0:T(8,128)(2,1)S(1)}, u32[]{:S(2)}, u32[]{:S(2)}) collective-permute-start(bf16[8,128,128]{2,1,0:T(8,128)(2,1)S(1)} %get-tuple-element.49), channel_id=1, source_target_pairs={{0,24},{8,16},{16,8},{24,0},{1,25},{9,17},{17,9},{25,1},{2,26},{10... | collective-permute-start | bytes 786440 | tf_op jit(solution)/shard_map/ppermute | solution.py:47
  50.7 12.4 %collective-permute-start.16 = (bf16[8,128,128]{2,1,0:T(8,128)(2,1)S(1)}, bf16[8,128,128]{2,1,0:T(8,128)(2,1)S(1)}, u32[]{:S(2)}, u32[]{:S(2)}) collective-permute-start(bf16[8,128,128]{2,1,0:T(8,128)(2,1)S(1)} %get-tuple-element.50), channel_id=1, source_target_pairs={{0,8},{8,0},{16,24},{24,16},{1,9},{9,1},{17,25},{25,17},{2,10},{10... | collective-permute-start | bytes 786440 | tf_op jit(solution)/shard_map/ppermute | solution.py:47
  51.3 6.0 %collective-permute-start.9 = (bf16[2,3,64,128]{3,2,1,0:T(8,128)(2,1)S(1)}, bf16[2,3,64,128]{3,2,1,0:T(8,128)(2,1)S(1)}, u32[]{:S(2)}, u32[]{:S(2)}) collective-permute-start(bf16[2,3,64,128]{3,2,1,0:T(8,128)(2,1)S(1)} %chip_states.7), channel_id=1, source_target_pairs={{0,2},{1,3},{2,0},{3,1},{4,6},{5,7},{6,4},{7,5},{8,10},{9,11},{10,... | collective-permute-start | bytes 294920 | tf_op jit(solution)/shard_map/ppermute | solution.py:47
  57.3 5.5 %collective-permute-start.12 = (bf16[3,64,128]{2,1,0:T(8,128)(2,1)S(1)}, bf16[3,64,128]{2,1,0:T(8,128)(2,1)S(1)}, u32[]{:S(2)}, u32[]{:S(2)}) collective-permute-start(bf16[3,64,128]{2,1,0:T(8,128)(2,1)S(1)} %chip_states.10), channel_id=1, source_target_pairs={{0,4},{1,5},{2,6},{3,7},{4,0},{5,1},{6,2},{7,3},{8,12},{9,13},{10,... | collective-permute-start | bytes 147464 | tf_op jit(solution)/shard_map/ppermute | solution.py:47
  62.9 1.4 %collective-permute-start.14 = (bf16[2,3,64,128]{3,2,1,0:T(8,128)(2,1)S(1)}, bf16[2,3,64,128]{3,2,1,0:T(8,128)(2,1)S(1)}, u32[]{:S(2)}, u32[]{:S(2)}) collective-permute-start(bf16[2,3,64,128]{3,2,1,0:T(8,128)(2,1)S(1)} %get-tuple-element.47), channel_id=1, source_target_pairs={{0,1},{1,0},{2,3},{3,2},{4,5},{5,4},{6,7},{7,6},{8,9},{9,8},{10,11... | collective-permute-start | bytes 294920 | tf_op jit(solution)/shard_map/ppermute | solution.py:47

commit v11 on v7

--- a/solution.py
+++ b/solution.py
@@ -8,7 +8,7 @@
 from jax.sharding import PartitionSpec as P
 
 HD = 128
-TILE = 256
+TILE = 512
 F32 = jnp.float32
 BF16 = jnp.bfloat16
 PARAMS = pltpu.CompilerParams(vmem_limit_bytes=40 * 1024 * 1024)

time: 70.4 us -> 68.9 us (0.979)
  Pallas kernels: 17.8 us -> 16.3 us
    pallas_call x3, Pallas kernels: 12.5 us -> 11 us  [gradients(): pl.pallas_call(functools.partial(grads_kernel, parts, factor, [item[2:] f...]
  transfers between devices with their start and end apart: 17 -> 17, of which waited for: 6 -> 6; matrix products, arithmetic and copies ran while one was open for 0% -> 0% of each run, Pallas kernels for 16% -> 15%
where the time goes in v11:
time: 68.9 us; the launch traced here: 68.6 us
  starting transfers between devices  26.4 us (38%)
  waiting for transfers between devices  25.2 us (37%)
  Pallas kernels  16.3 us (24%)
  between operations  0.77 us (1%)
    ppermute x17, starting transfers between devices, send(): lax.ppermute(value, axis, [(index, target(index)) for index in range(coun...  26.4 us
    ppermute x17, waiting for transfers between devices, send(): lax.ppermute(value, axis, [(index, target(index)) for index in range(coun...  25.2 us
    pallas_call x3, Pallas kernels, gradients(): pl.pallas_call(functools.partial(grads_kernel, parts, factor, [item[2:] f...  11 us
    pallas_call x1, Pallas kernels, pack_rest(): pl.pallas_call(functools.partial(rest_kernel, parts, heads, chunks), in_s...  2.15 us
    pallas_call x1, Pallas kernels, pack_first(): pl.pallas_call(functools.partial(first_kernel, parts, heads, count, late)...  1.85 us
  transfers between devices with their start and end apart: 17, of which 6 were waited for; matrix products, arithmetic and copies ran while one was open for 0% of the time, Pallas kernels for 15%

profile of v11, /device:TPU:0, one launch (start us, length us, event | category | flops | bytes accessed | tf_op | source)
XLA Modules:
  0.0 68.6 jit_solution(17852904745560415122)
XLA Ops:
  0.6 1.9 %pack.3 = (bf16[16,128,128]{2,1,0:T(8,128)(2,1)S(1)}, bf16[16,128,128]{2,1,0:T(8,128)(2,1)S(1)}, bf16[16,128,128]{2,1,0:T(8,128)(2,1)S(1)}) custom-call(bf16[1,128,4096]{2,1,0:T(8,128)(2,1)} %refs_0_.3, bf16[1,128,4096]{2,1,0:T(8,128)(2,1)} %refs_1_.3, bf16[1,128,4096]{2,1,0:T(8,128)(2,1)} %refs_2_.3, bf16[1,128,4096]{2,1,0:T(8,128)(2,1)} %refs_3_.3), custom_call_target="tpu_custom_call" | custom-call | flops 1000 | bytes 2048 | tf_op jit(solution)/shard_map/pack/pallas_call | solution.py:92
  2.5 3.0 %collective-permute-start.3 = (bf16[16,128,128]{2,1,0:T(8,128)(2,1)S(1)}, bf16[16,128,128]{2,1,0:T(8,128)(2,1)S(1)}, u32[]{:S(2)}, u32[]{:S(2)}) collective-permute-start(bf16[16,128,128]{2,1,0:T(8,128)(2,1)S(1)} %get-tuple-element.39), channel_id=1, source_target_pairs={{0,16},{8,24},{16,0},{24,8},{1,17},{9,25},{17,1},{25,9},{2,18},{10... | collective-permute-start | bytes 1572872 | tf_op jit(solution)/shard_map/ppermute | solution.py:47
  5.5 1.4 %collective-permute-start.4 = (bf16[16,128,128]{2,1,0:T(8,128)(2,1)S(1)}, bf16[16,128,128]{2,1,0:T(8,128)(2,1)S(1)}, u32[]{:S(2)}, u32[]{:S(2)}) collective-permute-start(bf16[16,128,128]{2,1,0:T(8,128)(2,1)S(1)} %get-tuple-element.40), channel_id=1, source_target_pairs={{0,24},{8,16},{16,8},{24,0},{1,25},{9,17},{17,9},{25,1},{2,26},{10... | collective-permute-start | bytes 1572872 | tf_op jit(solution)/shard_map/ppermute | solution.py:47
  7.0 0.1 collective-permute-start.5
  7.1 2.1 %pack.2 = (bf16[16,128,128]{2,1,0:T(8,128)(2,1)S(1)}, bf16[12,128,128]{2,1,0:T(8,128)(2,1)S(1)}, bf16[12,128,128]{2,1,0:T(8,128)(2,1)S(1)}, bf16[12,128,128]{2,1...) custom-call(bf16[1,128,4096]{2,1,0:T(8,128)(2,1)} %refs_0_.3, ...), custom_call_target="tpu_custom_call" | custom-call | flops 1000 | bytes 2048 | tf_op jit(solution)/shard_map/pack/pallas_call | solution.py:135
  9.2 2.0 %collective-permute-start = (bf16[12,128,128]{2,1,0:T(8,128)(2,1)S(1)}, bf16[12,128,128]{2,1,0:T(8,128)(2,1)S(1)}, u32[]{:S(2)}, u32[]{:S(2)}) collective-permute-start(bf16[12,128,128]{2,1,0:T(8,128)(2,1)S(1)} %get-tuple-element.35), channel_id=1, source_target_pairs={{0,16},{8,24},{16,0},{24,8},{1,17},{9,25},{17,1},{25,9},{2,18},{10... | collective-permute-start | bytes 1179656 | tf_op jit(solution)/shard_map/ppermute | solution.py:47
  11.2 1.5 %collective-permute-start.1 = (bf16[12,128,128]{2,1,0:T(8,128)(2,1)S(1)}, bf16[12,128,128]{2,1,0:T(8,128)(2,1)S(1)}, u32[]{:S(2)}, u32[]{:S(2)}) collective-permute-start(bf16[12,128,128]{2,1,0:T(8,128)(2,1)S(1)} %get-tuple-element.36), channel_id=1, source_target_pairs={{0,24},{8,16},{16,8},{24,0},{1,25},{9,17},{17,9},{25,1},{2,26},{10... | collective-permute-start | bytes 1179656 | tf_op jit(solution)/shard_map/ppermute | solution.py:47
  12.7 17.0 %collective-permute-done.3.refs_1_ = bf16[16,128,128]{2,1,0:T(8,128)(2,1)S(1)} collective-permute-done((bf16[16,128,128]{2,1,0:T(8,128)(2,1)S(1)}, bf16[16,128,128]{2,1,0:T(8,128)(2,1)S(1)}, u32[]{:S(2)}, u32[]{:S(2)}) %collective-permute-start.3) | collective-permute-done | bytes 524320 | tf_op jit(solution)/shard_map/ppermute | solution.py:47
  29.7 2.2 %collective-permute-start.2 = (bf16[12,128,128]{2,1,0:T(8,128)(2,1)S(1)}, bf16[12,128,128]{2,1,0:T(8,128)(2,1)S(1)}, u32[]{:S(2)}, u32[]{:S(2)}) collective-permute-start(bf16[12,128,128]{2,1,0:T(8,128)(2,1)S(1)} %get-tuple-element.37), channel_id=1, source_target_pairs={{0,8},{8,0},{16,24},{24,16},{1,9},{9,1},{17,25},{25,17},{2,10},{10... | collective-permute-start | bytes 1179656 | tf_op jit(solution)/shard_map/ppermute | solution.py:47
  31.9 0.4 own_states.2
  32.4 0.1 collective-permute-start.6
  32.4 1.4 %collective-permute-done.6.partner = bf16[2,5,64,128]{3,2,1,0:T(8,128)(2,1)S(1)} collective-permute-done((bf16[2,5,64,128]{3,2,1,0:T(8,128)(2,1)S(1)}, bf16[2,5,64,128]{3,2,1,0:T(8,128)(2,1)S(1)}, u32[]{:S(2)}, u32[]{:S(2)}) %collective-permute-start.6) | collective-permute-done | bytes 163872 | tf_op jit(solution)/shard_map/ppermute | solution.py:47
  33.9 1.6 %collective-permute-start.7 = (bf16[2,5,64,128]{3,2,1,0:T(8,128)(2,1)S(1)}, bf16[2,5,64,128]{3,2,1,0:T(8,128)(2,1)S(1)}, u32[]{:S(2)}, u32[]{:S(2)}) collective-permute-start(bf16[2,5,64,128]{3,2,1,0:T(8,128)(2,1)S(1)} %chip_states.6), channel_id=1, source_target_pairs={{0,2},{1,3},{2,0},{3,1},{4,6},{5,7},{6,4},{7,5},{8,10},{9,11},{10,... | collective-permute-start | bytes 491528 | tf_op jit(solution)/shard_map/ppermute | solution.py:47
  35.5 4.7 %collective-permute-done.7.refs_4_.refs_0_ = bf16[2,5,64,128]{3,2,1,0:T(8,128)(2,1)S(1)} collective-permute-done((bf16[2,5,64,128]{3,2,1,0:T(8,128)(2,1)S(1)}, bf16[2,5,64,128]{3,2,1,0:T(8,128)(2,1)S(1)}, u32[]{:S(2)}, u32[]{:S(2)}) %collective-permute-start.7) | collective-permute-done | bytes 163872 | tf_op jit(solution)/shard_map/ppermute | solution.py:47
  40.2 0.1 chip_states.8
  40.3 2.7 %collective-permute-start.10 = (bf16[5,64,128]{2,1,0:T(8,128)(2,1)S(1)}, bf16[5,64,128]{2,1,0:T(8,128)(2,1)S(1)}, u32[]{:S(2)}, u32[]{:S(2)}) collective-permute-start(bf16[5,64,128]{2,1,0:T(8,128)(2,1)S(1)} %chip_states.8), channel_id=1, source_target_pairs={{0,4},{1,5},{2,6},{3,7},{4,0},{5,1},{6,2},{7,3},{8,12},{9,13},{10,... | collective-permute-start | bytes 245768 | tf_op jit(solution)/shard_map/ppermute | solution.py:47
  42.9 2.5 %collective-permute-start.13 = (bf16[8,128,128]{2,1,0:T(8,128)(2,1)S(1)}, bf16[8,128,128]{2,1,0:T(8,128)(2,1)S(1)}, u32[]{:S(2)}, u32[]{:S(2)}) collective-permute-start(bf16[8,128,128]{2,1,0:T(8,128)(2,1)S(1)} %get-tuple-element.50), channel_id=1, source_target_pairs={{0,16},{8,24},{16,0},{24,8},{1,17},{9,25},{17,1},{25,9},{2,18},{10... | collective-permute-start | bytes 786440 | tf_op jit(solution)/shard_map/ppermute | solution.py:47
  45.4 0.2 collective-permute-done.refs_1_
  45.7 3.7 %collective-permute-start.14 = (bf16[8,128,128]{2,1,0:T(8,128)(2,1)S(1)}, bf16[8,128,128]{2,1,0:T(8,128)(2,1)S(1)}, u32[]{:S(2)}, u32[]{:S(2)}) collective-permute-start(bf16[8,128,128]{2,1,0:T(8,128)(2,1)S(1)} %get-tuple-element.51), channel_id=1, source_target_pairs={{0,24},{8,16},{16,8},{24,0},{1,25},{9,17},{17,9},{25,1},{2,26},{10... | collective-permute-start | bytes 786440 | tf_op jit(solution)/shard_map/ppermute | solution.py:47
  49.4 0.4 own_states.3
  49.8 0.1 collective-permute-start.8
  49.9 0.1 chip_states.9
  50.0 0.5 collective-permute-start.11
  50.6 0.6 collective-permute-done.8.partner
  51.2 1.6 %collective-permute-start.9 = (bf16[2,3,64,128]{3,2,1,0:T(8,128)(2,1)S(1)}, bf16[2,3,64,128]{3,2,1,0:T(8,128)(2,1)S(1)}, u32[]{:S(2)}, u32[]{:S(2)}) collective-permute-start(bf16[2,3,64,128]{3,2,1,0:T(8,128)(2,1)S(1)} %chip_states.7), channel_id=1, source_target_pairs={{0,2},{1,3},{2,0},{3,1},{4,6},{5,7},{6,4},{7,5},{8,10},{9,11},{10,... | collective-permute-start | bytes 294920 | tf_op jit(solution)/shard_map/ppermute | solution.py:47
  52.8 3.8 %gradients.3 = (bf16[1,512,1024]{2,1,0:T(8,128)(2,1)}, bf16[1,512,1024]{2,1,0:T(8,128)(2,1)}, bf16[1,512,1024]{2,1,0:T(8,128)(2,1)}, f32[8,128]{1,0:T(8,128)S(1)}) custom-call(bf16[16,128,128]{2,1,0:T(8,128)(2,1)S(1)} %get-tuple-element.38.refs_0_, bf16[16,128,128]{2,1,0:T(8,128)(2,1)S(1)} %collective-permute-done.3.refs_1_, ...), custom_call_target="tpu_custom_call" | custom-call | flops 1000 | bytes 2048 | tf_op jit(solution)/shard_map/gradients/pallas_call | solution.py:359
  56.7 3.2 %collective-permute-start.12 = (bf16[3,64,128]{2,1,0:T(8,128)(2,1)S(1)}, bf16[3,64,128]{2,1,0:T(8,128)(2,1)S(1)}, u32[]{:S(2)}, u32[]{:S(2)}) collective-permute-start(bf16[3,64,128]{2,1,0:T(8,128)(2,1)S(1)} %chip_states.10), channel_id=1, source_target_pairs={{0,4},{1,5},{2,6},{3,7},{4,0},{5,1},{6,2},{7,3},{8,12},{9,13},{10,... | collective-permute-start | bytes 147464 | tf_op jit(solution)/shard_map/ppermute | solution.py:47
  59.9 2.8 %gradients.4 = (bf16[1,512,1024]{2,1,0:T(8,128)(2,1)}, bf16[1,512,1024]{2,1,0:T(8,128)(2,1)}, bf16[1,512,1024]{2,1,0:T(8,128)(2,1)}, f32[8,128]{1,0:T(8,128)S(1)}) custom-call(bf16[8,128,128]{2,1,0:T(8,128)(2,1)S(1)} %get-tuple-element.49.refs_0_, ...), custom_call_target="tpu_custom_call", output_to_operand_aliasing={{0}: (6, {}), {1}: (7, {}), {2}: (8, {})} | custom-call | flops 1000 | bytes 2048 | tf_op jit(solution)/shard_map/gradients/pallas_call | solution.py:359
  62.7 0.1 chip_states.11
  62.8 0.1 collective-permute-start.16
  62.9 1.3 %collective-permute-done.16.refs_5_ = bf16[2,3,64,128]{3,2,1,0:T(8,128)(2,1)S(1)} collective-permute-done((bf16[2,3,64,128]{3,2,1,0:T(8,128)(2,1)S(1)}, bf16[2,3,64,128]{3,2,1,0:T(8,128)(2,1)S(1)}, u32[]{:S(2)}, u32[]{:S(2)}) %collective-permute-start.16) | collective-permute-done | bytes 98336 | tf_op jit(solution)/shard_map/ppermute | solution.py:47
  64.2 4.4 %gradients.5 = (bf16[1,512,1024]{2,1,0:T(8,128)(2,1)}, bf16[1,512,1024]{2,1,0:T(8,128)(2,1)}, bf16[1,512,1024]{2,1,0:T(8,128)(2,1)}, f32[8,128]{1,0:T(8,128)}) custom-call(bf16[12,128,128]{2,1,0:T(8,128)(2,1)S(1)} %get-tuple-element.34.refs_0_, ...), custom_call_target="tpu_custom_call", output_to_operand_aliasing={{0}: (6, {}), {1}: (7, {}), {2}: (8, {})} | custom-call | flops 1000 | bytes 2048 | tf_op jit(solution)/shard_map/gradients/pallas_call | solution.py:359
  (15 shorter events, 0.2 us)
Async XLA Ops:
  2.5 27.2 %collective-permute-start.3 = (bf16[16,128,128]{2,1,0:T(8,128)(2,1)S(1)}, bf16[16,128,128]{2,1,0:T(8,128)(2,1)S(1)}, u32[]{:S(2)}, u32[]{:S(2)}) collective-permute-start(bf16[16,128,128]{2,1,0:T(8,128)(2,1)S(1)} %get-tuple-element.39), channel_id=1, source_target_pairs={{0,16},{8,24},{16,0},{24,8},{1,17},{9,25},{17,1},{25,9},{2,18},{10... | collective-permute-start | bytes 1572872 | tf_op jit(solution)/shard_map/ppermute | solution.py:47
  5.5 26.4 %collective-permute-start.4 = (bf16[16,128,128]{2,1,0:T(8,128)(2,1)S(1)}, bf16[16,128,128]{2,1,0:T(8,128)(2,1)S(1)}, u32[]{:S(2)}, u32[]{:S(2)}) collective-permute-start(bf16[16,128,128]{2,1,0:T(8,128)(2,1)S(1)} %get-tuple-element.40), channel_id=1, source_target_pairs={{0,24},{8,16},{16,8},{24,0},{1,25},{9,17},{17,9},{25,1},{2,26},{10... | collective-permute-start | bytes 1572872 | tf_op jit(solution)/shard_map/ppermute | solution.py:47
  7.0 25.0 %collective-permute-start.5 = (bf16[16,128,128]{2,1,0:T(8,128)(2,1)S(1)}, bf16[16,128,128]{2,1,0:T(8,128)(2,1)S(1)}, u32[]{:S(2)}, u32[]{:S(2)}) collective-permute-start(bf16[16,128,128]{2,1,0:T(8,128)(2,1)S(1)} %get-tuple-element.41), channel_id=1, source_target_pairs={{0,8},{8,0},{16,24},{24,16},{1,9},{9,1},{17,25},{25,17},{2,10},{10... | collective-permute-start | bytes 1572872 | tf_op jit(solution)/shard_map/ppermute | solution.py:47
  9.2 36.5 %collective-permute-start = (bf16[12,128,128]{2,1,0:T(8,128)(2,1)S(1)}, bf16[12,128,128]{2,1,0:T(8,128)(2,1)S(1)}, u32[]{:S(2)}, u32[]{:S(2)}) collective-permute-start(bf16[12,128,128]{2,1,0:T(8,128)(2,1)S(1)} %get-tuple-element.35), channel_id=1, source_target_pairs={{0,16},{8,24},{16,0},{24,8},{1,17},{9,25},{17,1},{25,9},{2,18},{10... | collective-permute-start | bytes 1179656 | tf_op jit(solution)/shard_map/ppermute | solution.py:47
  11.2 38.1 %collective-permute-start.1 = (bf16[12,128,128]{2,1,0:T(8,128)(2,1)S(1)}, bf16[12,128,128]{2,1,0:T(8,128)(2,1)S(1)}, u32[]{:S(2)}, u32[]{:S(2)}) collective-permute-start(bf16[12,128,128]{2,1,0:T(8,128)(2,1)S(1)} %get-tuple-element.36), channel_id=1, source_target_pairs={{0,24},{8,16},{16,8},{24,0},{1,25},{9,17},{17,9},{25,1},{2,26},{10... | collective-permute-start | bytes 1179656 | tf_op jit(solution)/shard_map/ppermute | solution.py:47
  29.7 19.6 %collective-permute-start.2 = (bf16[12,128,128]{2,1,0:T(8,128)(2,1)S(1)}, bf16[12,128,128]{2,1,0:T(8,128)(2,1)S(1)}, u32[]{:S(2)}, u32[]{:S(2)}) collective-permute-start(bf16[12,128,128]{2,1,0:T(8,128)(2,1)S(1)} %get-tuple-element.37), channel_id=1, source_target_pairs={{0,8},{8,0},{16,24},{24,16},{1,9},{9,1},{17,25},{25,17},{2,10},{10... | collective-permute-start | bytes 1179656 | tf_op jit(solution)/shard_map/ppermute | solution.py:47
  32.4 1.5 %collective-permute-start.6 = (bf16[2,5,64,128]{3,2,1,0:T(8,128)(2,1)S(1)}, bf16[2,5,64,128]{3,2,1,0:T(8,128)(2,1)S(1)}, u32[]{:S(2)}, u32[]{:S(2)}) collective-permute-start(bf16[2,5,64,128]{3,2,1,0:T(8,128)(2,1)S(1)} %get-tuple-element.43), channel_id=1, source_target_pairs={{0,1},{1,0},{2,3},{3,2},{4,5},{5,4},{6,7},{7,6},{8,9},{9,8},{10,11... | collective-permute-start | bytes 491528 | tf_op jit(solution)/shard_map/ppermute | solution.py:47
  33.9 6.3 %collective-permute-start.7 = (bf16[2,5,64,128]{3,2,1,0:T(8,128)(2,1)S(1)}, bf16[2,5,64,128]{3,2,1,0:T(8,128)(2,1)S(1)}, u32[]{:S(2)}, u32[]{:S(2)}) collective-permute-start(bf16[2,5,64,128]{3,2,1,0:T(8,128)(2,1)S(1)} %chip_states.6), channel_id=1, source_target_pairs={{0,2},{1,3},{2,0},{3,1},{4,6},{5,7},{6,4},{7,5},{8,10},{9,11},{10,... | collective-permute-start | bytes 491528 | tf_op jit(solution)/shard_map/ppermute | solution.py:47
  40.3 9.6 %collective-permute-start.10 = (bf16[5,64,128]{2,1,0:T(8,128)(2,1)S(1)}, bf16[5,64,128]{2,1,0:T(8,128)(2,1)S(1)}, u32[]{:S(2)}, u32[]{:S(2)}) collective-permute-start(bf16[5,64,128]{2,1,0:T(8,128)(2,1)S(1)} %chip_states.8), channel_id=1, source_target_pairs={{0,4},{1,5},{2,6},{3,7},{4,0},{5,1},{6,2},{7,3},{8,12},{9,13},{10,... | collective-permute-start | bytes 245768 | tf_op jit(solution)/shard_map/ppermute | solution.py:47
  42.9 16.9 %collective-permute-start.13 = (bf16[8,128,128]{2,1,0:T(8,128)(2,1)S(1)}, bf16[8,128,128]{2,1,0:T(8,128)(2,1)S(1)}, u32[]{:S(2)}, u32[]{:S(2)}) collective-permute-start(bf16[8,128,128]{2,1,0:T(8,128)(2,1)S(1)} %get-tuple-element.50), channel_id=1, source_target_pairs={{0,16},{8,24},{16,0},{24,8},{1,17},{9,25},{17,1},{25,9},{2,18},{10... | collective-permute-start | bytes 786440 | tf_op jit(solution)/shard_map/ppermute | solution.py:47
  45.7 14.2 %collective-permute-start.14 = (bf16[8,128,128]{2,1,0:T(8,128)(2,1)S(1)}, bf16[8,128,128]{2,1,0:T(8,128)(2,1)S(1)}, u32[]{:S(2)}, u32[]{:S(2)}) collective-permute-start(bf16[8,128,128]{2,1,0:T(8,128)(2,1)S(1)} %get-tuple-element.51), channel_id=1, source_target_pairs={{0,24},{8,16},{16,8},{24,0},{1,25},{9,17},{17,9},{25,1},{2,26},{10... | collective-permute-start | bytes 786440 | tf_op jit(solution)/shard_map/ppermute | solution.py:47
  49.3 10.5 %collective-permute-start.15 = (bf16[8,128,128]{2,1,0:T(8,128)(2,1)S(1)}, bf16[8,128,128]{2,1,0:T(8,128)(2,1)S(1)}, u32[]{:S(2)}, u32[]{:S(2)}) collective-permute-start(bf16[8,128,128]{2,1,0:T(8,128)(2,1)S(1)} %get-tuple-element.52), channel_id=1, source_target_pairs={{0,8},{8,0},{16,24},{24,16},{1,9},{9,1},{17,25},{25,17},{2,10},{10... | collective-permute-start | bytes 786440 | tf_op jit(solution)/shard_map/ppermute | solution.py:47
  49.8 1.4 %collective-permute-start.8 = (bf16[2,3,64,128]{3,2,1,0:T(8,128)(2,1)S(1)}, bf16[2,3,64,128]{3,2,1,0:T(8,128)(2,1)S(1)}, u32[]{:S(2)}, u32[]{:S(2)}) collective-permute-start(bf16[2,3,64,128]{3,2,1,0:T(8,128)(2,1)S(1)} %get-tuple-element.45), channel_id=1, source_target_pairs={{0,1},{1,0},{2,3},{3,2},{4,5},{5,4},{6,7},{7,6},{8,9},{9,8},{10,11... | collective-permute-start | bytes 294920 | tf_op jit(solution)/shard_map/ppermute | solution.py:47
  50.0 2.8 %collective-permute-start.11 = (bf16[2,5,64,128]{3,2,1,0:T(8,128)(2,1)S(1)}, bf16[2,5,64,128]{3,2,1,0:T(8,128)(2,1)S(1)}, u32[]{:S(2)}, u32[]{:S(2)}) collective-permute-start(bf16[2,5,64,128]{3,2,1,0:T(8,128)(2,1)S(1)} %get-tuple-element.47), channel_id=1, source_target_pairs={{0,1},{1,0},{2,3},{3,2},{4,5},{5,4},{6,7},{7,6},{8,9},{9,8},{10,11... | collective-permute-start | bytes 491528 | tf_op jit(solution)/shard_map/ppermute | solution.py:47
  51.2 5.4 %collective-permute-start.9 = (bf16[2,3,64,128]{3,2,1,0:T(8,128)(2,1)S(1)}, bf16[2,3,64,128]{3,2,1,0:T(8,128)(2,1)S(1)}, u32[]{:S(2)}, u32[]{:S(2)}) collective-permute-start(bf16[2,3,64,128]{3,2,1,0:T(8,128)(2,1)S(1)} %chip_states.7), channel_id=1, source_target_pairs={{0,2},{1,3},{2,0},{3,1},{4,6},{5,7},{6,4},{7,5},{8,10},{9,11},{10,... | collective-permute-start | bytes 294920 | tf_op jit(solution)/shard_map/ppermute | solution.py:47
  56.7 6.0 %collective-permute-start.12 = (bf16[3,64,128]{2,1,0:T(8,128)(2,1)S(1)}, bf16[3,64,128]{2,1,0:T(8,128)(2,1)S(1)}, u32[]{:S(2)}, u32[]{:S(2)}) collective-permute-start(bf16[3,64,128]{2,1,0:T(8,128)(2,1)S(1)} %chip_states.10), channel_id=1, source_target_pairs={{0,4},{1,5},{2,6},{3,7},{4,0},{5,1},{6,2},{7,3},{8,12},{9,13},{10,... | collective-permute-start | bytes 147464 | tf_op jit(solution)/shard_map/ppermute | solution.py:47
  62.8 1.4 %collective-permute-start.16 = (bf16[2,3,64,128]{3,2,1,0:T(8,128)(2,1)S(1)}, bf16[2,3,64,128]{3,2,1,0:T(8,128)(2,1)S(1)}, u32[]{:S(2)}, u32[]{:S(2)}) collective-permute-start(bf16[2,3,64,128]{3,2,1,0:T(8,128)(2,1)S(1)} %get-tuple-element.58), channel_id=1, source_target_pairs={{0,1},{1,0},{2,3},{3,2},{4,5},{5,4},{6,7},{7,6},{8,9},{9,8},{10,11... | collective-permute-start | bytes 294920 | tf_op jit(solution)/shard_map/ppermute | solution.py:47
